TPU v7x, 32 devices: a whole 2x2x4 slice. The times are simulated.
32 devices in a mesh: groups: 2 (over y), dp: 8 (over z, core), tensor: 2 (over x).
Axes of the slice: x: 2, y: 2, z: 4, core: 2. Of those that a mesh axis runs over, the one named last changes fastest.
Arguments:
- patches: bfloat16 [16, 128, 16, 1792], P(('groups', 'dp'), 'tensor'), parts along dimension 0, may hold values from -24 to 24
- kept_count: int32 [16], P('groups'), parts along dimension 0, may hold values from 1 to 16, as said below
- keep_list: int32 [16, 16], P(('groups', 'dp')), parts along dimension 0, may hold values from 0 to 15, as said below
- pre_gain: float32 [1792], replicated, may hold values from 0.1 to 1.9
- pre_shift: float32 [1792], replicated, may hold values from -2.5 to 2.5
- w_qkv: bfloat16 [3, 1792, 1792], P(None, None, 'tensor'), may hold values from -9 to 9
- b_qkv: float32 [3, 1792], P(None, 'tensor'), may hold values from -2.5 to 2.5
- w_out: bfloat16 [1792, 1792], P('tensor'), may hold values from -0.125 to 0.125
- b_out: float32 [1792], replicated, may hold values from -2.5 to 2.5
- mlp_gain: float32 [1792], replicated, may hold values from 0.1 to 1.9
- mlp_shift: float32 [1792], replicated, may hold values from -2.5 to 2.5
- w_up: bfloat16 [1792, 9216], P(None, 'tensor'), may hold values from -0.125 to 0.125
- b_up: float32 [9216], P('tensor'), may hold values from -2.5 to 2.5
- w_down: bfloat16 [9216, 1792], P('tensor'), may hold values from -0.0625 to 0.0625
- b_down: float32 [1792], replicated, may hold values from -2.5 to 2.5
Outputs:
- encoded: bfloat16 [16, 128, 16, 1792], P(('groups', 'dp'), 'tensor'), parts along dimension 0
There are 2 independent parts, one for each index of `groups`. A program takes and returns all parts, laid end to end along the dimension named above; an argument that names none is the same for every part. Nothing has to cross between parts.
Inputs may be any that keep to these rules, and one draw needn't show every extreme that they name: kept_count sums to 32, and one page keeps all 16 of its blocks. `keep_list`: each row is a permutation of the page's blocks: its first kept_count[p] entries are the kept blocks in ascending order, the rest the dropped blocks in ascending order.
All inputs are finite; a program needn't handle non-finite values.
Results may differ from a plain program's by a relative error of at most 0.007.
Values may be sent and summed in bfloat16 or wider, within the bound.
No kernel may reach another device: no remote copies, remote signals or barrier semaphores. Data moves between devices by JAX's collectives and lax.ppermute only.
A program may use at most 128 MiB of HBM per device.

v0:
```python
import functools

import jax
import jax.numpy as jnp
from jax import lax
from jax.experimental import pallas as pl
from jax.experimental.pallas import tpu as pltpu
from jax.sharding import PartitionSpec as P

HEAD_DIM = 112
CHUNKS = (2, 2, 1)
STARTS = (0, 2, 4)
ROOM = 5
PAGE_HALF = 8
GROUP_ROWS = 16
F32 = jnp.float32
BF16 = jnp.bfloat16
MIB = 1 << 20
SMALL_COST = pl.CostEstimate(flops=1000, bytes_accessed=1000, transcendentals=0)


def norm_rows(inputs, gain, shift):
    average = jnp.mean(inputs, axis=-1, keepdims=True)
    centred = inputs - average
    variance = jnp.mean(centred * centred, axis=-1, keepdims=True)
    return centred * lax.rsqrt(variance + 1e-06) * gain + shift


def pick_at(values, index):
    total = jnp.int32(0)
    for place, value in enumerate(values):
        total = total + jnp.where(index == place, value, 0)
    return total


def page_ends_of(count_ref, pages):
    ends = [jnp.int32(0)]
    for page in range(pages):
        ends.append(ends[-1] + count_ref[page])
    return ends


def chunk_of(slot):
    number, start = jnp.int32(0), jnp.int32(0)
    for chunk in range(1, len(CHUNKS)):
        number = jnp.where(slot >= STARTS[chunk], chunk, number)
        start = jnp.where(slot >= STARTS[chunk], STARTS[chunk], start)
    return number, slot - start


def line_plan(ends, chips, core):
    held = [(ends[2 * chip] + 1 - core) >> 1 for chip in range(chips + 1)]
    total = held[chips]
    wanted = [
        jnp.clip(held[i], jnp.maximum(total - ROOM * (chips - i), 0), jnp.minimum(total, ROOM * i))
        for i in range(chips + 1)
    ]
    below, above = list(wanted), list(wanted)
    for i in range(1, chips + 1):
        below[i] = jnp.minimum(below[i], below[i - 1] + ROOM)
    for i in range(chips - 1, -1, -1):
        above[i] = jnp.maximum(above[i], above[i + 1] - ROOM)
    dealt = [(low + high) >> 1 for low, high in zip(below, above)]
    short = jnp.int32(0)
    for cut in range(1, chips):
        right = held[cut] - dealt[cut]
        most_right = jnp.minimum(held[cut] - held[cut - 1], ROOM)
        most_left = jnp.minimum(held[cut + 1] - held[cut], ROOM)
        short = short + jnp.where((right > most_right) | (-right > most_left), 1, 0)
    return held, dealt, short


AT_RIGHT = 0
AT_LEFT = AT_RIGHT + ROOM
AT_DEALT = AT_LEFT + ROOM
AT_HOME = AT_DEALT + ROOM
AT_SHORT = AT_HOME + 2 * PAGE_HALF
AT_SLOW_SOURCE = AT_SHORT + 1
AT_SLOW_PLACE = AT_SLOW_SOURCE + ROOM
AT_SLOW_HOME = AT_SLOW_PLACE + ROOM
AT_SLOW_SEND = AT_SLOW_HOME + 2 * PAGE_HALF


def plan_kernel(pages, device_ref, count_ref, table_ref):
    chips = pages // 2
    device = device_ref[0]
    core, chip = device & 1, device >> 1
    ends = page_ends_of(count_ref, pages)
    held, dealt, short = line_plan(ends, chips, core)
    short_other = line_plan(ends, chips, 1 - core)[2]
    table_ref[AT_SHORT] = jnp.where(short + short_other > 0, 1, 0)
    falls = [jnp.where(held[i] - dealt[i] > 2, 1, 0) for i in range(chips)]

    low, high = pick_at(held, chip), pick_at(held, chip + 1)
    first, end = pick_at(dealt, chip), pick_at(dealt, chip + 1)
    before = pick_at(dealt, chip - 1)
    falls_here, falls_right, falls_left = (pick_at(falls, chip + i) for i in (0, 1, -1))
    own_start, own_end = pick_at(ends, device), pick_at(ends, device + 1)
    mate_start = pick_at(ends, device ^ 1)

    def turned(offset, falling):
        return jnp.where(falling > 0, ROOM - 1 - offset, offset)

    def local_code(rank):
        position = 2 * rank + core
        own = (position >= own_start) & (position < own_end)
        return jnp.where(own, (position - own_start) >> 1, 16 + ((position - mate_start) >> 1))

    def part_code(count, source):
        number, place = chunk_of(count)
        return (source + number) * 16 + place

    for slot in range(ROOM):
        table_ref[AT_RIGHT + slot] = local_code(high - 1 - slot)
        table_ref[AT_LEFT + slot] = local_code(low + slot)
        offset = turned(jnp.int32(slot), falls_here)
        rank = first + offset
        code = jnp.where(rank < low, part_code(low - 1 - rank, 2), local_code(rank))
        code = jnp.where(rank >= high, part_code(rank - high, 2 + len(CHUNKS)), code)
        table_ref[AT_DEALT + slot] = code
        node = jnp.int32(0)
        for place in range(1, chips):
            node = node + jnp.where(held[place] <= rank, 1, 0)
        table_ref[AT_SLOW_SOURCE + slot] = 2 * node + core
        table_ref[AT_SLOW_PLACE + slot] = offset
    for half, start in enumerate((own_start, mate_start)):
        for slot in range(PAGE_HALF):
            rank = (start + ((start + core) & 1) + 2 * slot - core) >> 1
            at = half * PAGE_HALF + slot
            code = part_code(turned(rank - first, falls_here), 0)
            right = part_code(turned(rank - end, falls_right), len(CHUNKS))
            left = part_code(turned(rank - before, falls_left), 2 * len(CHUNKS))
            code = jnp.where(rank >= end, right, code)
            table_ref[AT_HOME + at] = jnp.where(rank < first, left, code)
            node, start_there, falls_there = jnp.int32(0), jnp.int32(0), falls[0]
            for place in range(1, chips):
                there = dealt[place] <= rank
                node = node + jnp.where(there, 1, 0)
                start_there = jnp.where(there, dealt[place], start_there)
                falls_there = jnp.where(there, falls[place], falls_there)
            slow = (2 * node + core) * ROOM + turned(rank - start_there, falls_there)
            table_ref[AT_SLOW_HOME + at] = jnp.clip(slow, 0, pages * ROOM - 1)
    for node in range(chips):
        for slot in range(ROOM):
            code = local_code(dealt[node] + slot)
            table_ref[AT_SLOW_SEND + node * ROOM + slot] = jnp.clip(code, 0, 31)


def make_plan(device, kept_count):
    pages = kept_count.shape[0]
    size = AT_SLOW_SEND + ROOM * (pages // 2)
    return pl.pallas_call(
        functools.partial(plan_kernel, pages),
        out_shape=jax.ShapeDtypeStruct((size,), jnp.int32),
        in_specs=[pl.BlockSpec(memory_space=pltpu.SMEM)] * 2,
        out_specs=pl.BlockSpec(memory_space=pltpu.SMEM),
        compiler_params=pltpu.CompilerParams(vmem_limit_bytes=MIB),
        cost_estimate=SMALL_COST,
        name="plan",
    )(device, kept_count)


def kept_blocks(device_ref, count_ref, keep_ref, pages):
    device = device_ref[0]
    start, count = jnp.int32(0), jnp.int32(0)
    for page in range(pages):
        start = start + jnp.where(page < device, count_ref[page], 0)
        count = count + jnp.where(page == device, count_ref[page], 0)
    blocks = []
    for half in range(2):
        offset = (start + device + half) & 1
        for slot in range(PAGE_HALF):
            index = 2 * slot + offset
            block = keep_ref[jnp.minimum(index, 2 * PAGE_HALF - 1)]
            blocks.append(jnp.where(index < count, block, -1))
    return blocks


def pack_kernel(pages, device_ref, count_ref, keep_ref, home_ref, mine_ref, mate_ref):
    page_blocks, width = home_ref.shape[1], home_ref.shape[2]
    blocks = kept_blocks(device_ref, count_ref, keep_ref, pages)
    span = GROUP_ROWS * page_blocks
    row = lax.broadcasted_iota(jnp.int32, (GROUP_ROWS, span), 0)
    column = lax.broadcasted_iota(jnp.int32, (GROUP_ROWS, span), 1)
    chosen = jnp.concatenate(
        [jnp.where(column == row * page_blocks + block, 1.0, 0.0).astype(BF16) for block in blocks],
        axis=0,
    )
    packed = jnp.dot(
        chosen, home_ref[...].reshape(span, width), preferred_element_type=F32
    ).astype(BF16)
    half = PAGE_HALF * GROUP_ROWS
    mine_ref[...] = packed[:half].reshape(PAGE_HALF, GROUP_ROWS, width)
    mate_ref[...] = packed[half:].reshape(PAGE_HALF, GROUP_ROWS, width)


def pack(device, kept_count, keep_row, home):
    rows, page_blocks, width = home.shape
    shape = jax.ShapeDtypeStruct((PAGE_HALF, rows, width), BF16)
    place = pl.BlockSpec((PAGE_HALF, GROUP_ROWS, width), lambda step, *_: (0, step, 0))
    return pl.pallas_call(
        functools.partial(pack_kernel, kept_count.shape[0]),
        out_shape=(shape, shape),
        grid_spec=pltpu.PrefetchScalarGridSpec(
            num_scalar_prefetch=3,
            grid=(rows // GROUP_ROWS,),
            in_specs=[
                pl.BlockSpec((GROUP_ROWS, page_blocks, width), lambda step, *_: (step, 0, 0))
            ],
            out_specs=(place, place),
        ),
        compiler_params=pltpu.CompilerParams(vmem_limit_bytes=16 * MIB),
        name="pack",
    )(device, kept_count, keep_row, home)


def merge_kernel(pages, device_ref, count_ref, keep_ref, home_ref, mine_ref, mate_ref, out_ref):
    page_blocks, width = home_ref.shape[1], home_ref.shape[2]
    blocks = kept_blocks(device_ref, count_ref, keep_ref, pages)
    span = GROUP_ROWS * page_blocks
    depth = 2 * PAGE_HALF * GROUP_ROWS
    row = lax.broadcasted_iota(jnp.int32, (span, depth), 0)
    column = lax.broadcasted_iota(jnp.int32, (span, depth), 1)
    slot = lax.broadcasted_iota(jnp.int32, (1, depth), 1) // GROUP_ROWS
    block_id = lax.broadcasted_iota(jnp.int32, (span, 1), 0) % page_blocks
    wanted = jnp.full((1, depth), -1, jnp.int32)
    kept = jnp.zeros((span, 1), jnp.int32)
    for place, block in enumerate(blocks):
        wanted = jnp.where(slot == place, block, wanted)
        kept = kept + jnp.where(block_id == block, 1, 0)
    chosen = jnp.where(
        (row // page_blocks == column % GROUP_ROWS) & (row % page_blocks == wanted), 1.0, 0.0
    ).astype(BF16)
    half = PAGE_HALF * GROUP_ROWS
    source = jnp.concatenate(
        [mine_ref[...].reshape(half, width), mate_ref[...].reshape(half, width)], axis=0
    )
    landed = jnp.dot(chosen, source, preferred_element_type=F32)
    home = home_ref[...].reshape(span, width).astype(F32)
    merged = jnp.where(kept > 0, landed, home).astype(BF16)
    out_ref[...] = merged.reshape(GROUP_ROWS, page_blocks, width)


def merge(device, kept_count, keep_row, home, mine, mate):
    rows, page_blocks, width = home.shape
    place = pl.BlockSpec((PAGE_HALF, GROUP_ROWS, width), lambda step, *_: (0, step, 0))
    page = pl.BlockSpec((GROUP_ROWS, page_blocks, width), lambda step, *_: (step, 0, 0))
    return pl.pallas_call(
        functools.partial(merge_kernel, kept_count.shape[0]),
        out_shape=jax.ShapeDtypeStruct(home.shape, BF16),
        grid_spec=pltpu.PrefetchScalarGridSpec(
            num_scalar_prefetch=3,
            grid=(rows // GROUP_ROWS,),
            in_specs=[page, place, place],
            out_specs=page,
        ),
        compiler_params=pltpu.CompilerParams(vmem_limit_bytes=16 * MIB),
        name="merge",
    )(device, kept_count, keep_row, home, mine, mate)


def choose_kernel(parts, n_sources, table_ref, *refs):
    sources, outs, sems = refs[:n_sources], refs[-1 - len(parts) : -1], refs[-1]
    number = 0
    for (at, total), out_ref in zip(parts, outs):
        for slot in range(total):
            code = table_ref[at + slot]
            which, place = code >> 4, code & 15
            for index, source in enumerate(sources):
                if len(sources) == 1:
                    here = which > -(1 << 20)
                elif index == 0:
                    here = which <= 0
                elif index == len(sources) - 1:
                    here = which >= index
                else:
                    here = which == index

                @pl.when(here)
                def _(source=source, out_ref=out_ref, slot=slot, place=place, number=number):
                    inside = jnp.minimum(place, source.shape[0] - 1)
                    pltpu.make_async_copy(
                        source.at[inside], out_ref.at[slot], sems.at[number]
                    ).start()

            number += 1
    number = 0
    for (_, total), out_ref in zip(parts, outs):
        for slot in range(total):
            pltpu.make_async_copy(sources[0].at[0], out_ref.at[slot], sems.at[number]).wait()
            number += 1


def choose(table, parts, sources, name, after=()):
    block = sources[0].shape[1:]
    total = sum(count for _, count in parts)
    return pl.pallas_call(
        functools.partial(choose_kernel, parts, len(sources)),
        out_shape=tuple(jax.ShapeDtypeStruct((count,) + block, BF16) for _, count in parts),
        in_specs=[pl.BlockSpec(memory_space=pltpu.SMEM)]
        + [pl.BlockSpec(memory_space=pl.ANY)] * (len(sources) + len(after)),
        out_specs=tuple(pl.BlockSpec(memory_space=pltpu.VMEM) for _ in parts),
        scratch_shapes=[pltpu.SemaphoreType.DMA((total,))],
        compiler_params=pltpu.CompilerParams(vmem_limit_bytes=8 * MIB),
        cost_estimate=SMALL_COST,
        name=name,
    )(table, *sources, *after)


def join_kernel(spots_ref, near, side, mate, out_ref, sems):
    piece = near.shape[0]
    sources = (near, side, mate.at[0], mate.at[1])
    copies = []
    for number, source in enumerate(sources):
        place = pl.ds(pl.multiple_of(spots_ref[number] * piece, piece), piece)
        copies.append(pltpu.make_async_copy(source, out_ref.at[place, :], sems.at[number]))
    for copy in copies:
        copy.start()
    for copy in copies:
        copy.wait()


def join(spots, near, side, mate):
    shape = (4 * near.shape[0], near.shape[1])
    any_space = pl.BlockSpec(memory_space=pl.ANY)
    return pl.pallas_call(
        join_kernel,
        out_shape=jax.ShapeDtypeStruct(shape, BF16),
        in_specs=[pl.BlockSpec(memory_space=pltpu.SMEM)] + [any_space] * 3,
        out_specs=pl.BlockSpec(memory_space=pltpu.VMEM),
        scratch_shapes=[pltpu.SemaphoreType.DMA((4,))],
        compiler_params=pltpu.CompilerParams(vmem_limit_bytes=8 * MIB),
        name="join",
    )(spots, near, side, mate)


def in_hbm(array):
    return pltpu.with_memory_space_constraint(array, pltpu.HBM)


def split_store(value, high_ref, low_ref):
    high = value.astype(BF16)
    high_ref[...] = high
    low_ref[...] = (value - high.astype(F32)).astype(BF16)


def attend_kernel(n_after, own_ref, other_ref, rows_ref, b_ref, w_ref, *refs):
    (out_ref, held, normed, q_high, q_low, k_high, k_low, values, scores, sems) = refs[n_after:]
    blocks, rows, width = own_ref.shape
    span = held.shape[2]
    loads = [pltpu.make_async_copy(w_ref.at[j], held.at[j], sems.at[j]) for j in range(3)]
    for load in loads:
        load.start()
    gain, shift = rows_ref[0:1, :], rows_ref[1:2, :]
    for half, ref in enumerate((own_ref, other_ref)):
        for block in range(blocks):
            at = (half * blocks + block) * rows
            normed[at : at + rows] = norm_rows(ref[block].astype(F32), gain, shift).astype(BF16)

    def project(j):
        loads[j].wait()
        product = jnp.dot(normed[...], held[j], preferred_element_type=F32)
        return product + b_ref[j : j + 1, :]

    split_store(project(0) * HEAD_DIM ** (-0.5), q_high, q_low)
    split_store(project(1), k_high, k_low)
    values[...] = project(2).astype(BF16)
    tiles = span // 128
    heads = span // HEAD_DIM
    size = 2 * rows
    lane = lax.broadcasted_iota(jnp.int32, (1, 256), 1)

    def window(head):
        tile = min(head * HEAD_DIM // 128, tiles - 2)
        first = head * HEAD_DIM - tile * 128
        inside = (lane >= first) & (lane < first + HEAD_DIM)
        return tile, slice(tile * 128, tile * 128 + 256), inside

    def one_block(block, carry):
        near = pl.ds(pl.multiple_of(block * rows, rows), rows)
        far = pl.ds(pl.multiple_of((blocks + block) * rows, rows), rows)

        def both(ref, columns):
            return jnp.concatenate([ref[near, columns], ref[far, columns]], axis=0)

        def times(left, right):
            return lax.dot_general(
                left, right, (((1,), (1,)), ((), ())), preferred_element_type=F32
            )

        for head in range(heads):
            _, columns, inside = window(head)
            none = jnp.zeros((), BF16)
            qh = jnp.where(inside, both(q_high, columns), none)
            ql = jnp.where(inside, both(q_low, columns), none)
            kh, kl = both(k_high, columns), both(k_low, columns)
            scores[head * size : (head + 1) * size, :] = (
                times(qh, kh) + times(qh, kl) + times(ql, kh)
            )
        value = scores[...]
        value = jnp.exp(value - jnp.max(value, axis=-1, keepdims=True))
        weights = (value * (1.0 / jnp.sum(value, axis=-1, keepdims=True))).astype(BF16)
        sums = [None] * tiles
        for head in range(heads):
            tile, columns, inside = window(head)
            mixed = jnp.dot(
                weights[head * size : (head + 1) * size, :], both(values, columns),
                preferred_element_type=F32,
            )
            mixed = jnp.where(inside, mixed, 0.0)
            for part in range(2):
                piece = mixed[:, part * 128 : part * 128 + 128]
                old = sums[tile + part]
                sums[tile + part] = piece if old is None else old + piece
        result = jnp.concatenate(sums, axis=1).astype(BF16)
        out_ref[0, block] = result[:rows]
        out_ref[1, block] = result[rows:]
        return carry

    lax.fori_loop(0, blocks, one_block, 0)


def attend(own, other, rows_params, w_qkv, b_qkv, after=()):
    blocks, rows, width = own.shape
    span = w_qkv.shape[2]
    total = 2 * blocks * rows
    vmem = pl.BlockSpec(memory_space=pltpu.VMEM)
    return pl.pallas_call(
        functools.partial(attend_kernel, len(after)),
        out_shape=jax.ShapeDtypeStruct((2, blocks, rows, span), BF16),
        in_specs=[vmem] * 4 + [pl.BlockSpec(memory_space=pl.ANY)] * (1 + len(after)),
        out_specs=vmem,
        scratch_shapes=[pltpu.VMEM((3, width, span), BF16), pltpu.VMEM((total, width), BF16)]
        + [pltpu.VMEM((total, span), BF16)] * 5
        + [
            pltpu.VMEM((2 * rows * (span // HEAD_DIM), 2 * rows), F32),
            pltpu.SemaphoreType.DMA((3,)),
        ],
        compiler_params=pltpu.CompilerParams(vmem_limit_bytes=28 * MIB),
        cost_estimate=SMALL_COST,
        name="attend",
    )(own, other, rows_params, b_qkv, in_hbm(w_qkv), *after)


UP_TILE = 512
DOWN_TILE = 256
SLOTS = 5


def mlp_kernel(n_after, own_ref, other_ref, mine_ref, theirs_ref, rows_ref, b_up_ref, w_mine, w_theirs,
               w_up, w_down, *refs):
    (keep_ref, send_ref, residual, renormed, hidden, outs, ups, downs, out_sems, up_sems,
     down_sems) = refs[n_after:]
    blocks, rows, width = own_ref.shape
    half = blocks * rows
    span = outs.shape[1]
    up_steps, down_steps = w_up.shape[1] // UP_TILE, width // DOWN_TILE

    def load_up(step):
        columns = pl.ds(pl.multiple_of(step * UP_TILE, UP_TILE), UP_TILE)
        slot = lax.rem(step, SLOTS)
        return pltpu.make_async_copy(w_up.at[:, columns], ups.at[slot], up_sems.at[slot])

    def load_down(step):
        columns = pl.ds(pl.multiple_of(step * DOWN_TILE, DOWN_TILE), DOWN_TILE)
        slot = lax.rem(step, SLOTS)
        return pltpu.make_async_copy(w_down.at[:, columns], downs.at[slot], down_sems.at[slot])

    out_loads = [
        pltpu.make_async_copy(source, outs.at[number], out_sems.at[number])
        for number, source in enumerate((w_mine, w_theirs))
    ]
    for load in out_loads:
        load.start()
    for slot in range(SLOTS):
        load_up(jnp.int32(slot)).start()
    gain, shift = rows_ref[2:3, :], rows_ref[3:4, :]
    mine = mine_ref[...].reshape(2 * half, span)
    theirs = jnp.concatenate(
        [theirs_ref[1].reshape(half, span), theirs_ref[0].reshape(half, span)], axis=0
    )
    for number, attended in enumerate((mine, theirs)):
        out_loads[number].wait()
        for column in range(0, width, DOWN_TILE):
            columns = slice(column, column + DOWN_TILE)
            part = jnp.dot(attended, outs[number, :, columns], preferred_element_type=F32)
            part = part.astype(BF16).astype(F32)
            if number == 0:
                residual[:, columns] = part + rows_ref[4:5, columns]
            else:
                residual[:, columns] += part
    for side, ref in enumerate((own_ref, other_ref)):
        for block in range(blocks):
            at = slice((side * blocks + block) * rows, (side * blocks + block + 1) * rows)
            value = ref[block].astype(F32) + residual[at]
            if side == 0:
                residual[at] = value
            renormed[at] = norm_rows(value, gain, shift).astype(BF16)

    def one_up(step, carry):
        load_up(step).wait()
        slot = lax.rem(step, SLOTS)
        for part in range(0, UP_TILE, 256):
            columns = pl.ds(pl.multiple_of(step * UP_TILE + part, 256), 256)
            raised = jnp.dot(
                renormed[...], ups[slot, :, part : part + 256], preferred_element_type=F32
            )
            raised = raised + b_up_ref[0:1, columns]
            hidden[:, columns] = jax.nn.gelu(raised, approximate=True).astype(BF16)
        ahead = step + SLOTS

        @pl.when(ahead < up_steps)
        def _():
            load_up(ahead).start()

        @pl.when((ahead >= up_steps) & (ahead < up_steps + down_steps))
        def _():
            load_down(ahead - up_steps).start()

        return carry

    lax.fori_loop(0, up_steps, one_up, 0)

    def one_down(step, carry):
        load_down(step).wait()
        columns = pl.ds(pl.multiple_of(step * DOWN_TILE, DOWN_TILE), DOWN_TILE)
        lowered = jnp.dot(
            hidden[...], downs[lax.rem(step, SLOTS)], preferred_element_type=F32
        )
        kept = residual[:half, columns] + lowered[:half] + rows_ref[5:6, columns]
        keep_ref[:, :, columns] = kept.reshape(blocks, rows, DOWN_TILE)
        send_ref[:, :, columns] = lowered[half:].astype(BF16).reshape(blocks, rows, DOWN_TILE)

        @pl.when(step + SLOTS < down_steps)
        def _():
            load_down(step + SLOTS).start()

        return carry

    lax.fori_loop(0, down_steps, one_down, 0)


def mlp(own, other, mine, theirs, rows_params, b_up, weights, after):
    blocks, rows, width = own.shape
    span = mine.shape[3]
    total = 2 * blocks * rows
    vmem = pl.BlockSpec(memory_space=pltpu.VMEM)
    hbm = pl.BlockSpec(memory_space=pl.ANY)
    w_mine, w_theirs, w_up, w_down = weights
    hidden = w_up.shape[1]
    return pl.pallas_call(
        functools.partial(mlp_kernel, len(after)),
        out_shape=(
            jax.ShapeDtypeStruct((blocks, rows, width), F32),
            jax.ShapeDtypeStruct((blocks, rows, width), BF16),
        ),
        in_specs=[vmem] * 6 + [hbm] * (4 + len(after)),
        out_specs=(vmem, vmem),
        scratch_shapes=[
            pltpu.VMEM((total, width), F32),
            pltpu.VMEM((total, width), BF16),
            pltpu.VMEM((total, hidden), BF16),
            pltpu.VMEM((2, span, width), BF16),
            pltpu.VMEM((SLOTS, width, UP_TILE), BF16),
            pltpu.VMEM((SLOTS, hidden, DOWN_TILE), BF16),
            pltpu.SemaphoreType.DMA((2,)),
            pltpu.SemaphoreType.DMA((SLOTS,)),
            pltpu.SemaphoreType.DMA((SLOTS,)),
        ],
        compiler_params=pltpu.CompilerParams(vmem_limit_bytes=46 * MIB),
        cost_estimate=SMALL_COST,
        name="mlp",
    )(
        own, other, mine, theirs, rows_params, b_up, in_hbm(w_mine), w_theirs, in_hbm(w_up),
        in_hbm(w_down), *after,
    )


def add_kernel(n_after, keep_ref, came_ref, *refs):
    out_ref = refs[n_after]
    out_ref[...] = (keep_ref[...] + came_ref[...].astype(F32)).astype(BF16)


def add(keep, came, after):
    vmem = pl.BlockSpec(memory_space=pltpu.VMEM)
    return pl.pallas_call(
        functools.partial(add_kernel, len(after)),
        out_shape=jax.ShapeDtypeStruct(came.shape, BF16),
        in_specs=[vmem] * 2 + [pl.BlockSpec(memory_space=pl.ANY)] * len(after),
        out_specs=vmem,
        compiler_params=pltpu.CompilerParams(vmem_limit_bytes=8 * MIB),
        cost_estimate=SMALL_COST,
        name="add",
    )(keep, came, *after)


def swap(value):
    return lax.ppermute(value, "tensor", [(0, 1), (1, 0)])


def line_up_kernel(total, n_after, *refs):
    sources, out_ref, sems = refs[:total], refs[total + n_after], refs[-1]
    copies = [
        pltpu.make_async_copy(source, out_ref.at[number], sems.at[number])
        for number, source in enumerate(sources)
    ]
    for copy in copies:
        copy.start()
    for copy in copies:
        copy.wait()


def line_up(arrays, after, name):
    any_space = pl.BlockSpec(memory_space=pl.ANY)
    total = len(arrays)
    return pl.pallas_call(
        functools.partial(line_up_kernel, total, len(after)),
        out_shape=jax.ShapeDtypeStruct((total,) + arrays[0].shape, arrays[0].dtype),
        in_specs=[any_space] * (total + len(after)),
        out_specs=pl.BlockSpec(memory_space=pltpu.VMEM),
        scratch_shapes=[pltpu.SemaphoreType.DMA((total,))],
        compiler_params=pltpu.CompilerParams(vmem_limit_bytes=8 * MIB),
        cost_estimate=SMALL_COST,
        name=name,
    )(*arrays, *after)


def w_out_place(w_out):
    core = lax.axis_index("dp") & 1
    group = lax.axis_index("groups")
    return 2 * group + core, 2 * (1 - group) + core, w_out.shape[0] // 4


def other_w_out(w_out, near, early, late):
    number, other, _ = w_out_place(w_out)
    dp_size = lax.axis_size("dp")
    sent = line_up([near], early, "w_near")
    side = lax.ppermute(sent, "groups", [(0, 1), (1, 0)])[0]
    both = line_up([near, side], late, "w_both")
    mate = lax.ppermute(both, "dp", [(d, d ^ 1) for d in range(dp_size)])
    spots = jnp.stack([number, other, number ^ 1, other ^ 1]).astype(jnp.int32)
    return join(spots, near, side, mate)


def attend_rows(projected):
    row_total, count_blocks, width = (projected.shape[0], projected.shape[1], projected.shape[3])
    head_count = width // HEAD_DIM
    queries = projected[:, :, 0].reshape(row_total, count_blocks, head_count, HEAD_DIM)
    key_rows = projected[:, :, 1].reshape(row_total, count_blocks, head_count, HEAD_DIM)
    values = projected[:, :, 2].astype(BF16).reshape(row_total, count_blocks, head_count, HEAD_DIM)
    scores = jnp.einsum(
        "qnhd,snhd->nhqs", queries, key_rows, precision=lax.Precision.HIGHEST
    ) * HEAD_DIM ** (-0.5)
    weights = jax.nn.softmax(scores, axis=-1).astype(BF16)
    attended = jnp.einsum("nhqs,snhd->qnhd", weights, values, preferred_element_type=F32)
    return attended.astype(BF16).reshape(row_total, count_blocks, width)


def encode_split(own, params):
    (pre_gain, pre_shift, w_qkv, b_qkv, w_out, b_out, mlp_gain, mlp_shift, w_up, b_up, w_down,
     b_down) = params
    block_rows = jnp.swapaxes(own, 0, 1)
    rows_dev = block_rows.shape[0]
    gathered = lax.all_gather(block_rows, "tensor", axis=0, tiled=True)
    normed = norm_rows(gathered.astype(F32), pre_gain, pre_shift).astype(BF16)
    attended = attend_rows(
        jnp.einsum("qnd,jde->qnje", normed, w_qkv, preferred_element_type=F32) + b_qkv[None, None]
    )
    partial_value = jnp.einsum("qne,ed->qnd", attended, w_out, preferred_element_type=F32)
    summed = lax.psum(partial_value.astype(BF16), "tensor").astype(F32)
    residual_all = gathered.astype(F32) + summed + b_out
    renormed = norm_rows(residual_all, mlp_gain, mlp_shift).astype(BF16)
    raised = jnp.einsum("qnd,df->qnf", renormed, w_up, preferred_element_type=F32) + b_up
    hidden = jax.nn.gelu(raised, approximate=True).astype(BF16)
    residual = lax.dynamic_slice_in_dim(
        residual_all, lax.axis_index("tensor") * rows_dev, rows_dev, 0
    )
    mlp_out = lax.psum_scatter(
        jnp.einsum("qnf,fd->qnd", hidden, w_down, preferred_element_type=F32).astype(BF16),
        "tensor", scatter_dimension=0, tiled=True,
    ).astype(F32)
    return jnp.swapaxes((residual + mlp_out + b_down).astype(BF16), 0, 1)


def per_device(paired, patches, kept_count, keep_list, *params):
    home = in_hbm(patches[0])
    keep_row = in_hbm(keep_list[0])
    kept_count = in_hbm(kept_count)
    dp_size = lax.axis_size("dp")
    device = lax.axis_index("dp").astype(jnp.int32).reshape(1)
    mates = [(d, d ^ 1) for d in range(dp_size)]
    rightwards = [(d, d + 2) for d in range(dp_size - 2)]
    leftwards = [(d + 2, d) for d in range(dp_size - 2)]

    def to_mate(value):
        return lax.ppermute(value, "dp", mates)

    def to_right(value):
        return lax.ppermute(value, "dp", rightwards)

    def to_left(value):
        return lax.ppermute(value, "dp", leftwards)

    mine, for_mate = pack(device, kept_count, keep_row, home)
    from_mate = to_mate(for_mate)
    table = make_plan(device, kept_count)
    short = table[AT_SHORT : AT_SHORT + 1].astype(F32)
    if paired:
        short = short + lax.ppermute(short, "groups", [(0, 1), (1, 0)])
    else:
        short = lax.pmax(short, "groups")
    short = short[0] > 0

    parts = tuple(zip(STARTS, CHUNKS))
    sends = [(AT_RIGHT + at, size) for at, size in parts] + [(AT_LEFT + at, size) for at, size in parts]
    going = choose(table, sends, [mine, from_mate], "send")
    came_right = [to_right(value) for value in going[: len(parts)]]
    came_left = [to_left(value) for value in going[len(parts) :]]

    def deal_fast(chunk, spare, after):
        right = [came_right[min(part, chunk)] for part in range(len(parts))]
        left = [came_left[min(part, chunk)] for part in range(len(parts))]
        wanted = [(AT_DEALT + at, size) for at, size in parts[chunk : len(parts) if spare else chunk + 1]]
        return choose(table, wanted, [mine, from_mate] + right + left, "deal_%d" % chunk, after)

    def deal_slow():
        chips = dp_size // 2
        (picked,) = choose(table, [(AT_SLOW_SEND, ROOM * chips)], [mine, from_mate], "deal_slow")
        picked = picked.reshape((chips, ROOM) + picked.shape[1:])
        spread = jnp.repeat(picked, 2, axis=0)
        arrived = lax.all_to_all(spread, "dp", split_axis=0, concat_axis=0, tiled=True)
        dealt = [arrived[table[AT_SLOW_SOURCE + j], table[AT_SLOW_PLACE + j]] for j in range(ROOM)]
        return tuple(jnp.stack(dealt[at : at + size]) for at, size in parts)

    spares = lax.cond(short, deal_slow, functools.partial(deal_fast, 0, True, ()))

    def deal(chunk, after):
        return lax.cond(
            short, lambda: spares[chunk], lambda: deal_fast(chunk, False, after)[0]
        )

    if paired:
        (pre_gain, pre_shift, w_qkv, b_qkv, w_out, b_out, mlp_gain, mlp_shift, w_up, b_up, w_down,
         b_down) = params
        rows_params = jnp.stack([pre_gain, pre_shift, mlp_gain, mlp_shift, b_out, b_down])
        b_up = b_up.reshape(1, -1)
        number, _, piece = w_out_place(w_out)
        w_near = swap(lax.dynamic_slice_in_dim(w_out, number * piece, piece, 0))

        def start(own, after):
            other = swap(own)
            mine = attend(own, other, rows_params, w_qkv, b_qkv, after)
            return own, other, mine, swap(mine)

        def finish(state, after):
            keep, send = mlp(*state, rows_params, b_up, weights, after)
            return keep, swap(send)

        blocks_0 = spares[0]
        state_0 = start(blocks_0, [])
        blocks_1 = deal(1, [])
        state_1 = start(blocks_1, [])
        blocks_2 = deal(2, [])
        state_2 = start(blocks_2, [state_1[2]])
        w_theirs = other_w_out(w_out, w_near, [blocks_0], [blocks_1, state_0[2]])
        weights = (w_out, w_theirs, w_up, w_down)
        done_0 = finish(state_0, [state_2[2]])
        done_1 = finish(state_1, [done_0[0], state_2[3]])
        done_2 = finish(state_2, [done_1[0]])
        results, from_right, from_left = [], [], []
        for done, beside in ((done_0, done_1[:1]), (done_1, done_2[:1]), (done_2, ())):
            results.append(add(*done, list(beside) + from_right[-1:] + from_left[-1:]))
            from_right.append(to_left(results[-1]))
            from_left.append(to_right(results[-1]))
    else:
        results = [
            encode_split(part, params) for part in (spares[0], deal(1, ()), deal(2, ()))
        ]
        from_right = [to_left(value) for value in results]
        from_left = [to_right(value) for value in results]

    def home_fast():
        return choose(
            table,
            [(AT_HOME, PAGE_HALF), (AT_HOME + PAGE_HALF, PAGE_HALF)],
            results + from_right + from_left,
            "home_fast",
        )

    def home_slow():
        spread = lax.all_gather(jnp.concatenate(results), "dp", axis=0, tiled=True)
        places = table[AT_SLOW_HOME : AT_SLOW_HOME + 2 * PAGE_HALF]
        return (
            jnp.take(spread, places[:PAGE_HALF], axis=0),
            jnp.take(spread, places[PAGE_HALF:], axis=0),
        )

    back_mine, back_mate = lax.cond(short, home_slow, home_fast)
    return merge(device, kept_count, keep_row, home, back_mine, to_mate(back_mate))[None]


def solution(mesh):
    in_specs = (
        P(("groups", "dp"), "tensor", None, None),
        P("groups"),
        P(("groups", "dp"), None),
        P(),
        P(),
        P(None, None, "tensor"),
        P(None, "tensor"),
        P("tensor", None),
        P(),
        P(),
        P(),
        P(None, "tensor"),
        P("tensor"),
        P("tensor", None),
        P(),
    )
    out_specs = P(("groups", "dp"), "tensor", None, None)
    paired = mesh.shape["tensor"] == 2 and mesh.shape["groups"] == 2
    return jax.shard_map(
        functools.partial(per_device, paired), mesh=mesh, in_specs=in_specs, out_specs=out_specs,
        check_vma=False,
    )
```

profile of v0, /device:TPU:0, one launch (start us, length us, event | category | flops | bytes accessed | tf_op | source)
XLA Modules:
  0.0 237.1 jit_solution(5635944670340531059)
XLA Ops:
  6.5 5.5 %pack.1 = (bf16[8,64,1792]{2,1,0:T(8,128)(2,1)}, bf16[8,64,1792]{2,1,0:T(8,128)(2,1)S(1)}) custom-call(s32[1]{0:T(128)} %bitcast.17.device_ref, s32[8]{0:T(128)} %count_ref.5, s32[16]{0:T(128)} %bitcast.38, bf16[64,16,1792]{2,1,0:T(8,128)(2,1)} %bitcast.36), custom_call_target="tpu_custom_call" | custom-call | tf_op jit(solution)/shard_map/pack/pallas_call | solution.py:201
  14.5 2.5 %collective-permute-start.6 = (bf16[224,1792]{1,0:T(8,128)(2,1)}, bf16[224,1792]{1,0:T(8,128)(2,1)S(1)}, u32[]{:S(2)}, u32[]{:S(2)}) collective-permute-start(bf16[224,1792]{1,0:T(8,128)(2,1)} %constant_dynamic-slice_fusion), channel_id=1, source_target_pairs={{0,1},{1,0},{2,3},{3,2},{4,5},{5,4},{6,7},{7,6},{8,9},{9,8},{10,11... | collective-permute-start | bytes 2408456 | tf_op jit(solution)/shard_map/ppermute | solution.py:598
  19.0 3.1 %send.1 = (bf16[2,64,1792]{2,1,0:T(8,128)(2,1)S(1)}, bf16[2,64,1792]{2,1,0:T(8,128)(2,1)}, bf16[1,64,1792]{2,1,0:T(8,128)(2,1)S(1)}, bf16[2,64,1792]{2,1,0:T(8,1...) custom-call(s32[78]{0:T(128)S(1)} %plan.1.table_ref, ...), custom_call_target="tpu_custom_call" | custom-call | flops 1000 | bytes 1000 | tf_op jit(solution)/shard_map/send/pallas_call | solution.py:297
  23.6 4.3 %collective-permute-start.2 = (bf16[2,64,1792]{2,1,0:T(8,128)(2,1)S(1)}, bf16[2,64,1792]{2,1,0:T(8,128)(2,1)}, u32[]{:S(2)}, u32[]{:S(2)}) collective-permute-start(bf16[2,64,1792]{2,1,0:T(8,128)(2,1)S(1)} %get-tuple-element.154), channel_id=1, source_target_pairs={{0,4},{2,6},{4,8},{6,10},{8,12},{10,14},{1,5},{3,7},{5,9},{7,11},{... | collective-permute-start | bytes 1376264 | tf_op jit(solution)/shard_map/ppermute | solution.py:699
  30.3 2.9 %collective-permute-start = (f32[1]{0:T(128)}, f32[1]{0:T(128)}, u32[]{:S(2)}, u32[]{:S(2)}) collective-permute-start(f32[1]{0:T(128)} %convert_element_type.12), channel_id=1, source_target_pairs={{0,16},{16,0},{1,17},{17,1},{2,18},{18,2},{3,19},{19,3},{4,20},{20... | collective-permute-start | bytes 20 | tf_op jit(solution)/shard_map/ppermute | solution.py:709
  34.6 2.6 %collective-permute-done.2 = bf16[2,64,1792]{2,1,0:T(8,128)(2,1)} collective-permute-done((bf16[2,64,1792]{2,1,0:T(8,128)(2,1)S(1)}, bf16[2,64,1792]{2,1,0:T(8,128)(2,1)}, u32[]{:S(2)}, u32[]{:S(2)}) %collective-permute-start.2) | collective-permute-done | bytes 458784 | tf_op jit(solution)/shard_map/ppermute | solution.py:699
  37.2 5.0 %collective-permute-done.3 = bf16[2,64,1792]{2,1,0:T(8,128)(2,1)} collective-permute-done((bf16[2,64,1792]{2,1,0:T(8,128)(2,1)S(1)}, bf16[2,64,1792]{2,1,0:T(8,128)(2,1)}, u32[]{:S(2)}, u32[]{:S(2)}) %collective-permute-start.3) | collective-permute-done | bytes 458784 | tf_op jit(solution)/shard_map/ppermute | solution.py:702
  42.2 3.0 %conditional.4 = ((bf16[2,64,1792]{2,1,0:T(8,128)(2,1)}, bf16[2,64,1792]{2,1,0:T(8,128)(2,1)S(1)}, bf16[1,64,1792]{2,1,0:T(8,128)(2,1)})) conditional(s32[]{:T(128)} %bitcast.20, (s32[78]{0:T(128)S(1)}, bf16[8,64,1792]{2,1,0:T(8,128)(2,1)S(1)}, bf16[8,64,1792]{2,1,0:T(8,128)(2,1)}, bf16[2,64,1792]{2,1,0:T(8,128)(2,1)}, ...), branch_computations={%region_0.0_spmd, %region_1.0_spmd} | conditional | flops 459782 | bytes 63770612 | solution.py:735
  42.2 3.0 %deal_0.1 = (bf16[2,64,1792]{2,1,0:T(8,128)(2,1)}, bf16[2,64,1792]{2,1,0:T(8,128)(2,1)S(1)}, bf16[1,64,1792]{2,1,0:T(8,128)(2,1)}) custom-call(s32[78]{0:T(128)S(1)} %get-tuple-element.95.table_ref, bf16[8,64,1792]{2,1,0:T(8,128)(2,1)S(1)} %get-tuple-element.96.refs_0_, bf16[8,64,1792]{2,1,0:T(8,128)(2,1)} %get-tuple-element.97.refs_1_, ...), custom_call_target="tpu_custom_call" | custom-call | flops 1000 | bytes 1000 | tf_op jit(solution)/shard_map/cond/branch_0_fun/deal_0/pallas_call | solution.py:297
  47.8 3.5 %collective-permute-start.8 = (bf16[2,64,1792]{2,1,0:T(8,128)(2,1)}, bf16[2,64,1792]{2,1,0:T(8,128)(2,1)}, u32[]{:S(2)}, u32[]{:S(2)}) collective-permute-start(bf16[2,64,1792]{2,1,0:T(8,128)(2,1)} %get-tuple-element.157), channel_id=1, source_target_pairs={{0,4},{2,6},{4,8},{6,10},{8,12},{10,14},{1,5},{3,7},{5,9},{7,11},{... | collective-permute-start | bytes 1376264 | tf_op jit(solution)/shard_map/ppermute | solution.py:699
  53.3 5.9 %collective-permute-done.8 = bf16[2,64,1792]{2,1,0:T(8,128)(2,1)} collective-permute-done((bf16[2,64,1792]{2,1,0:T(8,128)(2,1)}, bf16[2,64,1792]{2,1,0:T(8,128)(2,1)}, u32[]{:S(2)}, u32[]{:S(2)}) %collective-permute-start.8) | collective-permute-done | bytes 458784 | tf_op jit(solution)/shard_map/ppermute | solution.py:699
  59.3 4.7 %collective-permute-done.9 = bf16[2,64,1792]{2,1,0:T(8,128)(2,1)} collective-permute-done((bf16[2,64,1792]{2,1,0:T(8,128)(2,1)S(1)}, bf16[2,64,1792]{2,1,0:T(8,128)(2,1)}, u32[]{:S(2)}, u32[]{:S(2)}) %collective-permute-start.9) | collective-permute-done | bytes 458784 | tf_op jit(solution)/shard_map/ppermute | solution.py:702
  63.9 2.4 %conditional.5 = (bf16[2,64,1792]{2,1,0:T(8,128)(2,1)}) conditional(s32[]{:T(128)} %bitcast.20, (s32[78]{0:T(128)S(1)}, bf16[8,64,1792]{2,1,0:T(8,128)(2,1)}, bf16[8,64,1792]{2,1,0:T(8,128)(2,1)}, bf16[2,64,1792]{2,1,0:T(8,128)(2,1)}, bf16[2,64,1792]{2,1,0:T(8,128)(2,1)}, /*index=5*/bf16[2,64,1792]{2,1,0:T(8,128)(2,1)}, ...), branch_computations={%region_2.0_spmd, %region_3.0_spmd} | conditional | flops 1000 | bytes 917512 | solution.py:738
  66.4 8.6 %attend.3.refs_3_.mine_ref = bf16[2,2,64,896]{3,2,1,0:T(8,128)(2,1)S(1)} custom-call(bf16[2,64,1792]{2,1,0:T(8,128)(2,1)} %get-tuple-element.156.own_ref.refs_1_, bf16[2,64,1792]{2,1,0:T(8,128)(2,1)S(1)} %collective-permute-done.4.other_ref, f32[6,1792]{1,0:T(8,128)S(1)} %stack.48.rows_ref, f32[3,896]{1,0:T(4,128)S(1)} %copy-done.1, bf16[3,1792,896]{2,1,0:T(8,128)(2,1)} %w_ref.5), custom_call_target="tpu_custom_call" | custom-call | flops 1000 | bytes 1000 | tf_op jit(solution)/shard_map/attend/pallas_call | solution.py:428
  76.5 2.8 %collective-permute-start.11 = (bf16[1,64,1792]{2,1,0:T(8,128)(2,1)S(1)}, bf16[1,64,1792]{2,1,0:T(8,128)(2,1)S(1)}, u32[]{:S(2)}, u32[]{:S(2)}) collective-permute-start(bf16[1,64,1792]{2,1,0:T(8,128)(2,1)S(1)} %copy-done.5), channel_id=1, source_target_pairs={{0,4},{2,6},{4,8},{6,10},{8,12},{10,14},{1,5},{3,7},{5,9},{7,11},{... | collective-permute-start | bytes 688136 | tf_op jit(solution)/shard_map/ppermute | solution.py:699
  84.8 4.1 %collective-permute-done.12 = bf16[1,64,1792]{2,1,0:T(8,128)(2,1)S(1)} collective-permute-done((bf16[1,64,1792]{2,1,0:T(8,128)(2,1)S(1)}, bf16[1,64,1792]{2,1,0:T(8,128)(2,1)S(1)}, u32[]{:S(2)}, u32[]{:S(2)}) %collective-permute-start.12) | collective-permute-done | bytes 229408 | tf_op jit(solution)/shard_map/ppermute | solution.py:702
  91.3 2.9 %collective-permute-done.14.other_ref = bf16[2,64,1792]{2,1,0:T(8,128)(2,1)S(1)} collective-permute-done((bf16[2,64,1792]{2,1,0:T(8,128)(2,1)}, bf16[2,64,1792]{2,1,0:T(8,128)(2,1)S(1)}, u32[]{:S(2)}, u32[]{:S(2)}) %collective-permute-start.14) | collective-permute-done | bytes 458784 | tf_op jit(solution)/shard_map/ppermute | solution.py:598
  94.3 8.6 %attend.4.refs_0_.mine_ref = bf16[2,2,64,896]{3,2,1,0:T(8,128)(2,1)S(1)} custom-call(bf16[2,64,1792]{2,1,0:T(8,128)(2,1)} %get-tuple-element.207.refs_2_.own_ref, bf16[2,64,1792]{2,1,0:T(8,128)(2,1)S(1)} %collective-permute-done.14.other_ref, f32[6,1792]{1,0:T(8,128)S(1)} %stack.48.rows_ref, f32[3,896]{1,0:T(4,128)S(1)} %copy-done.1, bf16[3,1792,896]{2,1,0:T(8,128)(2,1)} %w_ref.5), custom_call_target="tpu_custom_call" | custom-call | flops 1000 | bytes 1000 | tf_op jit(solution)/shard_map/attend/pallas_call | solution.py:428
  103.5 5.5 %collective-permute-done.13.other_ref = bf16[1,64,1792]{2,1,0:T(8,128)(2,1)S(1)} collective-permute-done((bf16[1,64,1792]{2,1,0:T(8,128)(2,1)}, bf16[1,64,1792]{2,1,0:T(8,128)(2,1)S(1)}, u32[]{:S(2)}, u32[]{:S(2)}) %collective-permute-start.13) | collective-permute-done | bytes 229408 | tf_op jit(solution)/shard_map/ppermute | solution.py:598
  109.0 5.5 %attend.5.refs_0_.mine_ref = bf16[2,1,64,896]{3,2,1,0:T(8,128)(2,1)S(1)} custom-call(bf16[1,64,1792]{2,1,0:T(8,128)(2,1)S(1)} %copy-done.9, bf16[1,64,1792]{2,1,0:T(8,128)(2,1)S(1)} %collective-permute-done.13.other_ref, f32[6,1792]{1,0:T(8,128)S(1)} %stack.48.rows_ref, f32[3,896]{1,0:T(4,128)S(1)} %copy-done.1, bf16[3,1792,896]{2,1,0:T(8,128)(2,1)} %w_ref.5, ...), custom_call_target="tpu_custom_call" | custom-call | flops 1000 | bytes 1000 | tf_op jit(solution)/shard_map/attend/pallas_call | solution.py:428
  116.6 18.6 %mlp.3 = (f32[2,64,1792]{2,1,0:T(8,128)S(1)}, bf16[2,64,1792]{2,1,0:T(8,128)(2,1)S(1)}) custom-call(bf16[2,64,1792]{2,1,0:T(8,128)(2,1)} %get-tuple-element.156.own_ref.refs_1_, bf16[2,64,1792]{2,1,0:T(8,128)(2,1)S(1)} %collective-permute-done.4.other_ref, bf16[2,2,64,896]{3,2,1,0:T(8,128)(2,1)S(1)} %attend.3.refs_3_.mine_ref, ...), custom_call_target="tpu_custom_call" | custom-call | flops 1000 | bytes 1000 | tf_op jit(solution)/shard_map/mlp/pallas_call | solution.py:551
  137.4 14.0 %collective-permute-done.17.refs_1_.theirs_ref = bf16[2,1,64,896]{3,2,1,0:T(8,128)(2,1)S(1)} collective-permute-done((bf16[2,1,64,896]{3,2,1,0:T(8,128)(2,1)S(1)}, bf16[2,1,64,896]{3,2,1,0:T(8,128)(2,1)S(1)}, u32[]{:S(2)}, u32[]{:S(2)}) %collective-permute-start.17) | collective-permute-done | bytes 229408 | tf_op jit(solution)/shard_map/ppermute | solution.py:598
  151.3 18.5 %mlp.4 = (f32[2,64,1792]{2,1,0:T(8,128)S(1)}, bf16[2,64,1792]{2,1,0:T(8,128)(2,1)S(1)}) custom-call(bf16[2,64,1792]{2,1,0:T(8,128)(2,1)} %get-tuple-element.207.refs_2_.own_ref, bf16[2,64,1792]{2,1,0:T(8,128)(2,1)S(1)} %collective-permute-done.14.other_ref, bf16[2,2,64,896]{3,2,1,0:T(8,128)(2,1)S(1)} %attend.4.refs_0_.mine_ref, ...), custom_call_target="tpu_custom_call" | custom-call | flops 1000 | bytes 1000 | tf_op jit(solution)/shard_map/mlp/pallas_call | solution.py:551
  171.8 4.6 %collective-permute-start.20 = (bf16[2,64,1792]{2,1,0:T(8,128)(2,1)S(1)}, bf16[2,64,1792]{2,1,0:T(8,128)(2,1)S(1)}, u32[]{:S(2)}, u32[]{:S(2)}) collective-permute-start(bf16[2,64,1792]{2,1,0:T(8,128)(2,1)S(1)} %add.66), channel_id=1, source_target_pairs={{0,4},{2,6},{4,8},{6,10},{8,12},{10,14},{1,5},{3,7},{5,9},{7,11},{... | collective-permute-start | bytes 1376264 | tf_op jit(solution)/shard_map/ppermute | solution.py:699
  176.4 12.7 %mlp.5 = (f32[1,64,1792]{2,1,0:T(8,128)S(1)}, bf16[1,64,1792]{2,1,0:T(8,128)(2,1)S(1)}) custom-call(bf16[1,64,1792]{2,1,0:T(8,128)(2,1)S(1)} %copy-done.9, bf16[1,64,1792]{2,1,0:T(8,128)(2,1)S(1)} %collective-permute-done.13.other_ref, bf16[2,1,64,896]{3,2,1,0:T(8,128)(2,1)S(1)} %attend.5.refs_0_.mine_ref, ...), custom_call_target="tpu_custom_call" | custom-call | flops 1000 | bytes 1000 | tf_op jit(solution)/shard_map/mlp/pallas_call | solution.py:551
  190.6 4.6 %collective-permute-start.23 = (bf16[2,64,1792]{2,1,0:T(8,128)(2,1)S(1)}, bf16[2,64,1792]{2,1,0:T(8,128)(2,1)S(1)}, u32[]{:S(2)}, u32[]{:S(2)}) collective-permute-start(bf16[2,64,1792]{2,1,0:T(8,128)(2,1)S(1)} %add.67), channel_id=1, source_target_pairs={{0,4},{2,6},{4,8},{6,10},{8,12},{10,14},{1,5},{3,7},{5,9},{7,11},{... | collective-permute-start | bytes 1376264 | tf_op jit(solution)/shard_map/ppermute | solution.py:699
  196.7 4.5 %collective-permute-done.21.came_ref = bf16[1,64,1792]{2,1,0:T(8,128)(2,1)S(1)} collective-permute-done((bf16[1,64,1792]{2,1,0:T(8,128)(2,1)S(1)}, bf16[1,64,1792]{2,1,0:T(8,128)(2,1)S(1)}, u32[]{:S(2)}, u32[]{:S(2)}) %collective-permute-start.21) | collective-permute-done | bytes 229408 | tf_op jit(solution)/shard_map/ppermute | solution.py:598
  203.0 5.0 %collective-permute-start.25 = (bf16[1,64,1792]{2,1,0:T(8,128)(2,1)S(1)}, bf16[1,64,1792]{2,1,0:T(8,128)(2,1)S(1)}, u32[]{:S(2)}, u32[]{:S(2)}) collective-permute-start(bf16[1,64,1792]{2,1,0:T(8,128)(2,1)S(1)} %add.68), channel_id=1, source_target_pairs={{0,4},{2,6},{4,8},{6,10},{8,12},{10,14},{1,5},{3,7},{5,9},{7,11},{... | collective-permute-start | bytes 688136 | tf_op jit(solution)/shard_map/ppermute | solution.py:699
  211.5 8.1 %conditional.7 = ((bf16[8,64,1792]{2,1,0:T(8,128)(2,1)}, bf16[8,64,1792]{2,1,0:T(8,128)(2,1)})) conditional(s32[]{:T(128)} %bitcast.20, (s32[78]{0:T(128)S(1)}, bf16[2,64,1792]{2,1,0:T(8,128)(2,1)S(1)}, bf16[2,64,1792]{2,1,0:T(8,128)(2,1)S(1)}, bf16[1,64,1792]{2,1,0:T(8,128)(2,1)S(1)}, bf16[2,64,1792]{2,1,0:T(8,128)(2,1)S(1)}, ...), branch_computations={%region_6.0_spmd, %region_7.9_spmd} | conditional | flops 2984032 | bytes 47948128 | solution.py:798
  211.5 8.1 %home_fast.1 = (bf16[8,64,1792]{2,1,0:T(8,128)(2,1)}, bf16[8,64,1792]{2,1,0:T(8,128)(2,1)}) custom-call(s32[78]{0:T(128)S(1)} %get-tuple-element.119.table_ref, bf16[2,64,1792]{2,1,0:T(8,128)(2,1)S(1)} %get-tuple-element.120.refs_0_, bf16[2,64,1792]{2,1,0:T(8,128)(2,1)S(1)} %get-tuple-element.121.refs_1_, ...), custom_call_target="tpu_custom_call" | custom-call | flops 1000 | bytes 1000 | tf_op jit(solution)/shard_map/cond/branch_0_fun/home_fast/pallas_call | solution.py:297
  219.7 4.0 %collective-permute-done.26.mate_ref = bf16[8,64,1792]{2,1,0:T(8,128)(2,1)S(1)} collective-permute-done((bf16[8,64,1792]{2,1,0:T(8,128)(2,1)}, bf16[8,64,1792]{2,1,0:T(8,128)(2,1)S(1)}, u32[]{:S(2)}, u32[]{:S(2)}) %collective-permute-start.26) | collective-permute-done | bytes 1835040 | tf_op jit(solution)/shard_map/ppermute | solution.py:696
  223.7 6.5 %merge.1 = bf16[64,16,1792]{2,1,0:T(8,128)(2,1)} custom-call(s32[1]{0:T(128)} %bitcast.17.device_ref, s32[8]{0:T(128)} %count_ref.5, s32[16]{0:T(128)} %bitcast.39, bf16[64,16,1792]{2,1,0:T(8,128)(2,1)} %bitcast.37, bf16[8,64,1792]{2,1,0:T(8,128)(2,1)} %get-tuple-element.169.mine_ref, bf16[8,64,1792]{2,1,0:T(8,128)(2,1)S(1)} %collective-permute-done.26.mate_ref), custom_call_target="tpu_custom_call" | custom-call | tf_op jit(solution)/shard_map/merge/pallas_call | solution.py:248
  (95 shorter events, 40.6 us)
Async XLA Ops:
  12.0 7.0 %collective-permute-start.1 = (bf16[8,64,1792]{2,1,0:T(8,128)(2,1)S(1)}, bf16[8,64,1792]{2,1,0:T(8,128)(2,1)}, u32[]{:S(2)}, u32[]{:S(2)}) collective-permute-start(bf16[8,64,1792]{2,1,0:T(8,128)(2,1)S(1)} %get-tuple-element.153), channel_id=1, source_target_pairs={{0,2},{2,0},{4,6},{6,4},{8,10},{10,8},{12,14},{14,12},{1,3},{3,1},... | collective-permute-start | bytes 5505032 | tf_op jit(solution)/shard_map/ppermute | solution.py:696
  14.5 30.8 %collective-permute-start.6 = (bf16[224,1792]{1,0:T(8,128)(2,1)}, bf16[224,1792]{1,0:T(8,128)(2,1)S(1)}, u32[]{:S(2)}, u32[]{:S(2)}) collective-permute-start(bf16[224,1792]{1,0:T(8,128)(2,1)} %constant_dynamic-slice_fusion), channel_id=1, source_target_pairs={{0,1},{1,0},{2,3},{3,2},{4,5},{5,4},{6,7},{7,6},{8,9},{9,8},{10,11... | collective-permute-start | bytes 2408456 | tf_op jit(solution)/shard_map/ppermute | solution.py:598
  19.0 23.2 %copy-start.11 = (s32[78]{0:T(128)}, s32[78]{0:T(128)S(1)}, u32[]{:S(2)}) copy-start(s32[78]{0:T(128)S(1)} %plan.1.table_ref) | copy-start | bytes 940
  19.0 23.2 %copy-start.6 = (bf16[8,64,1792]{2,1,0:T(8,128)(2,1)S(1)}, bf16[8,64,1792]{2,1,0:T(8,128)(2,1)}, u32[]{:S(2)}) copy-start(bf16[8,64,1792]{2,1,0:T(8,128)(2,1)} %get-tuple-element.152.refs_0_) | copy-start | bytes 5505028
  23.6 13.6 %collective-permute-start.2 = (bf16[2,64,1792]{2,1,0:T(8,128)(2,1)S(1)}, bf16[2,64,1792]{2,1,0:T(8,128)(2,1)}, u32[]{:S(2)}, u32[]{:S(2)}) collective-permute-start(bf16[2,64,1792]{2,1,0:T(8,128)(2,1)S(1)} %get-tuple-element.154), channel_id=1, source_target_pairs={{0,4},{2,6},{4,8},{6,10},{8,12},{10,14},{1,5},{3,7},{5,9},{7,11},{... | collective-permute-start | bytes 1376264 | tf_op jit(solution)/shard_map/ppermute | solution.py:699
  27.8 14.4 %collective-permute-start.3 = (bf16[2,64,1792]{2,1,0:T(8,128)(2,1)S(1)}, bf16[2,64,1792]{2,1,0:T(8,128)(2,1)}, u32[]{:S(2)}, u32[]{:S(2)}) collective-permute-start(bf16[2,64,1792]{2,1,0:T(8,128)(2,1)S(1)} %get-tuple-element.155), channel_id=1, source_target_pairs={{4,0},{6,2},{8,4},{10,6},{12,8},{14,10},{5,1},{7,3},{9,5},{11,7},{... | collective-permute-start | bytes 1376264 | tf_op jit(solution)/shard_map/ppermute | solution.py:702
  30.3 3.7 %collective-permute-start = (f32[1]{0:T(128)}, f32[1]{0:T(128)}, u32[]{:S(2)}, u32[]{:S(2)}) collective-permute-start(f32[1]{0:T(128)} %convert_element_type.12), channel_id=1, source_target_pairs={{0,16},{16,0},{1,17},{17,1},{2,18},{18,2},{3,19},{19,3},{4,20},{20... | collective-permute-start | bytes 20 | tf_op jit(solution)/shard_map/ppermute | solution.py:709
  46.0 17.9 %copy-start.12 = (s32[78]{0:T(128)S(1)}, s32[78]{0:T(128)}, u32[]{:S(2)}) copy-start(s32[78]{0:T(128)} %copy-done.11) | copy-start | bytes 940
  46.1 28.9 %collective-permute-start.7 = (bf16[1,224,1792]{2,1,0:T(8,128)(2,1)S(1)}, bf16[1,224,1792]{2,1,0:T(8,128)(2,1)S(1)}, u32[]{:S(2)}, u32[]{:S(2)}) collective-permute-start(bf16[1,224,1792]{2,1,0:T(8,128)(2,1)S(1)} %w_near.1), channel_id=1, source_target_pairs={{0,16},{16,0},{1,17},{17,1},{2,18},{18,2},{3,19},{19,3},{4,20},{20... | collective-permute-start | bytes 2408456 | tf_op jit(solution)/shard_map/ppermute | solution.py:638
  47.8 11.5 %collective-permute-start.8 = (bf16[2,64,1792]{2,1,0:T(8,128)(2,1)}, bf16[2,64,1792]{2,1,0:T(8,128)(2,1)}, u32[]{:S(2)}, u32[]{:S(2)}) collective-permute-start(bf16[2,64,1792]{2,1,0:T(8,128)(2,1)} %get-tuple-element.157), channel_id=1, source_target_pairs={{0,4},{2,6},{4,8},{6,10},{8,12},{10,14},{1,5},{3,7},{5,9},{7,11},{... | collective-permute-start | bytes 1376264 | tf_op jit(solution)/shard_map/ppermute | solution.py:699
  51.2 12.7 %collective-permute-start.9 = (bf16[2,64,1792]{2,1,0:T(8,128)(2,1)S(1)}, bf16[2,64,1792]{2,1,0:T(8,128)(2,1)}, u32[]{:S(2)}, u32[]{:S(2)}) collective-permute-start(bf16[2,64,1792]{2,1,0:T(8,128)(2,1)S(1)} %get-tuple-element.158), channel_id=1, source_target_pairs={{4,0},{6,2},{8,4},{10,6},{12,8},{14,10},{5,1},{7,3},{9,5},{11,7},{... | collective-permute-start | bytes 1376264 | tf_op jit(solution)/shard_map/ppermute | solution.py:702
  52.5 13.8 %collective-permute-start.4 = (bf16[2,64,1792]{2,1,0:T(8,128)(2,1)}, bf16[2,64,1792]{2,1,0:T(8,128)(2,1)S(1)}, u32[]{:S(2)}, u32[]{:S(2)}) collective-permute-start(bf16[2,64,1792]{2,1,0:T(8,128)(2,1)} %get-tuple-element.156.own_ref.refs_1_), channel_id=1, source_target_pairs={{0,1},{1,0},{2,3},{3,2},{4,5},{5,4},{6,7},{7,6},{8,9},{9,8},{10,11... | collective-permute-start | bytes 1376264 | tf_op jit(solution)/shard_map/ppermute | solution.py:598
  75.0 13.9 %copy-start.7 = (bf16[8,64,1792]{2,1,0:T(8,128)(2,1)S(1)}, bf16[8,64,1792]{2,1,0:T(8,128)(2,1)}, u32[]{:S(2)}) copy-start(bf16[8,64,1792]{2,1,0:T(8,128)(2,1)} %get-tuple-element.152.refs_0_) | copy-start | bytes 5505028
  76.4 38.1 %collective-permute-start.10 = (bf16[2,224,1792]{2,1,0:T(8,128)(2,1)}, bf16[2,224,1792]{2,1,0:T(8,128)(2,1)}, u32[]{:S(2)}, u32[]{:S(2)}) collective-permute-start(bf16[2,224,1792]{2,1,0:T(8,128)(2,1)} %w_both.1), channel_id=1, source_target_pairs={{0,2},{2,0},{4,6},{6,4},{8,10},{10,8},{12,14},{14,12},{1,3},{3,1},... | collective-permute-start | bytes 4816904 | tf_op jit(solution)/shard_map/ppermute | solution.py:640
  76.5 8.3 %collective-permute-start.11 = (bf16[1,64,1792]{2,1,0:T(8,128)(2,1)S(1)}, bf16[1,64,1792]{2,1,0:T(8,128)(2,1)S(1)}, u32[]{:S(2)}, u32[]{:S(2)}) collective-permute-start(bf16[1,64,1792]{2,1,0:T(8,128)(2,1)S(1)} %copy-done.5), channel_id=1, source_target_pairs={{0,4},{2,6},{4,8},{6,10},{8,12},{10,14},{1,5},{3,7},{5,9},{7,11},{... | collective-permute-start | bytes 688136 | tf_op jit(solution)/shard_map/ppermute | solution.py:699
  79.3 9.6 %collective-permute-start.12 = (bf16[1,64,1792]{2,1,0:T(8,128)(2,1)S(1)}, bf16[1,64,1792]{2,1,0:T(8,128)(2,1)S(1)}, u32[]{:S(2)}, u32[]{:S(2)}) collective-permute-start(bf16[1,64,1792]{2,1,0:T(8,128)(2,1)S(1)} %copy-done.3), channel_id=1, source_target_pairs={{4,0},{6,2},{8,4},{10,6},{12,8},{14,10},{5,1},{7,3},{9,5},{11,7},{... | collective-permute-start | bytes 688136 | tf_op jit(solution)/shard_map/ppermute | solution.py:702
  80.6 13.6 %collective-permute-start.14 = (bf16[2,64,1792]{2,1,0:T(8,128)(2,1)}, bf16[2,64,1792]{2,1,0:T(8,128)(2,1)S(1)}, u32[]{:S(2)}, u32[]{:S(2)}) collective-permute-start(bf16[2,64,1792]{2,1,0:T(8,128)(2,1)} %get-tuple-element.207.refs_2_.own_ref), channel_id=1, source_target_pairs={{0,1},{1,0},{2,3},{3,2},{4,5},{5,4},{6,7},{7,6},{8,9},{9,8},{10,11... | collective-permute-start | bytes 1376264 | tf_op jit(solution)/shard_map/ppermute | solution.py:598
  81.2 35.4 %collective-permute-start.5 = (bf16[2,2,64,896]{3,2,1,0:T(8,128)(2,1)S(1)}, bf16[2,2,64,896]{3,2,1,0:T(8,128)(2,1)}, u32[]{:S(2)}, u32[]{:S(2)}) collective-permute-start(bf16[2,2,64,896]{3,2,1,0:T(8,128)(2,1)S(1)} %attend.3.refs_3_.mine_ref), channel_id=1, source_target_pairs={{0,1},{1,0},{2,3},{3,2},{4,5},{5,4},{6,7},{7,6},{8,9},{9,8},{10,11... | collective-permute-start | bytes 1376264 | tf_op jit(solution)/shard_map/ppermute | solution.py:598
  90.7 18.3 %collective-permute-start.13 = (bf16[1,64,1792]{2,1,0:T(8,128)(2,1)}, bf16[1,64,1792]{2,1,0:T(8,128)(2,1)S(1)}, u32[]{:S(2)}, u32[]{:S(2)}) collective-permute-start(bf16[1,64,1792]{2,1,0:T(8,128)(2,1)} %copy-done.8), channel_id=1, source_target_pairs={{0,1},{1,0},{2,3},{3,2},{4,5},{5,4},{6,7},{7,6},{8,9},{9,8},{10,11... | collective-permute-start | bytes 688136 | tf_op jit(solution)/shard_map/ppermute | solution.py:598
  91.3 17.7 %copy-start.9 = (bf16[1,64,1792]{2,1,0:T(8,128)(2,1)S(1)}, bf16[1,64,1792]{2,1,0:T(8,128)(2,1)}, u32[]{:S(2)}) copy-start(bf16[1,64,1792]{2,1,0:T(8,128)(2,1)} %copy-done.8) | copy-start | bytes 688132
  102.9 48.4 %collective-permute-start.16 = (bf16[2,2,64,896]{3,2,1,0:T(8,128)(2,1)S(1)}, bf16[2,2,64,896]{3,2,1,0:T(8,128)(2,1)S(1)}, u32[]{:S(2)}, u32[]{:S(2)}) collective-permute-start(bf16[2,2,64,896]{3,2,1,0:T(8,128)(2,1)S(1)} %attend.4.refs_0_.mine_ref), channel_id=1, source_target_pairs={{0,1},{1,0},{2,3},{3,2},{4,5},{5,4},{6,7},{7,6},{8,9},{9,8},{10,11... | collective-permute-start | bytes 1376264 | tf_op jit(solution)/shard_map/ppermute | solution.py:598
  135.3 35.2 %collective-permute-start.15 = (bf16[2,64,1792]{2,1,0:T(8,128)(2,1)S(1)}, bf16[2,64,1792]{2,1,0:T(8,128)(2,1)S(1)}, u32[]{:S(2)}, u32[]{:S(2)}) collective-permute-start(bf16[2,64,1792]{2,1,0:T(8,128)(2,1)S(1)} %get-tuple-element.164), channel_id=1, source_target_pairs={{0,1},{1,0},{2,3},{3,2},{4,5},{5,4},{6,7},{7,6},{8,9},{9,8},{10,11... | collective-permute-start | bytes 1376264 | tf_op jit(solution)/shard_map/ppermute | solution.py:598
  135.9 15.4 %collective-permute-start.17 = (bf16[2,1,64,896]{3,2,1,0:T(8,128)(2,1)S(1)}, bf16[2,1,64,896]{3,2,1,0:T(8,128)(2,1)S(1)}, u32[]{:S(2)}, u32[]{:S(2)}) collective-permute-start(bf16[2,1,64,896]{3,2,1,0:T(8,128)(2,1)S(1)} %attend.5.refs_0_.mine_ref), channel_id=1, source_target_pairs={{0,1},{1,0},{2,3},{3,2},{4,5},{5,4},{6,7},{7,6},{8,9},{9,8},{10,11... | collective-permute-start | bytes 688136 | tf_op jit(solution)/shard_map/ppermute | solution.py:598
  169.8 19.3 %collective-permute-start.18 = (bf16[2,64,1792]{2,1,0:T(8,128)(2,1)S(1)}, bf16[2,64,1792]{2,1,0:T(8,128)(2,1)S(1)}, u32[]{:S(2)}, u32[]{:S(2)}) collective-permute-start(bf16[2,64,1792]{2,1,0:T(8,128)(2,1)S(1)} %get-tuple-element.166), channel_id=1, source_target_pairs={{0,1},{1,0},{2,3},{3,2},{4,5},{5,4},{6,7},{7,6},{8,9},{9,8},{10,11... | collective-permute-start | bytes 1376264 | tf_op jit(solution)/shard_map/ppermute | solution.py:598
  170.5 18.7 %collective-permute-start.19 = (bf16[2,64,1792]{2,1,0:T(8,128)(2,1)S(1)}, bf16[2,64,1792]{2,1,0:T(8,128)(2,1)S(1)}, u32[]{:S(2)}, u32[]{:S(2)}) collective-permute-start(bf16[2,64,1792]{2,1,0:T(8,128)(2,1)S(1)} %add.66), channel_id=1, source_target_pairs={{4,0},{6,2},{8,4},{10,6},{12,8},{14,10},{5,1},{7,3},{9,5},{11,7},{... | collective-permute-start | bytes 1376264 | tf_op jit(solution)/shard_map/ppermute | solution.py:702
  171.8 17.4 %collective-permute-start.20 = (bf16[2,64,1792]{2,1,0:T(8,128)(2,1)S(1)}, bf16[2,64,1792]{2,1,0:T(8,128)(2,1)S(1)}, u32[]{:S(2)}, u32[]{:S(2)}) collective-permute-start(bf16[2,64,1792]{2,1,0:T(8,128)(2,1)S(1)} %add.66), channel_id=1, source_target_pairs={{0,4},{2,6},{4,8},{6,10},{8,12},{10,14},{1,5},{3,7},{5,9},{7,11},{... | collective-permute-start | bytes 1376264 | tf_op jit(solution)/shard_map/ppermute | solution.py:699
  189.3 12.0 %collective-permute-start.22 = (bf16[2,64,1792]{2,1,0:T(8,128)(2,1)S(1)}, bf16[2,64,1792]{2,1,0:T(8,128)(2,1)S(1)}, u32[]{:S(2)}, u32[]{:S(2)}) collective-permute-start(bf16[2,64,1792]{2,1,0:T(8,128)(2,1)S(1)} %add.67), channel_id=1, source_target_pairs={{4,0},{6,2},{8,4},{10,6},{12,8},{14,10},{5,1},{7,3},{9,5},{11,7},{... | collective-permute-start | bytes 1376264 | tf_op jit(solution)/shard_map/ppermute | solution.py:702
  190.6 11.1 %collective-permute-start.23 = (bf16[2,64,1792]{2,1,0:T(8,128)(2,1)S(1)}, bf16[2,64,1792]{2,1,0:T(8,128)(2,1)S(1)}, u32[]{:S(2)}, u32[]{:S(2)}) collective-permute-start(bf16[2,64,1792]{2,1,0:T(8,128)(2,1)S(1)} %add.67), channel_id=1, source_target_pairs={{0,4},{2,6},{4,8},{6,10},{8,12},{10,14},{1,5},{3,7},{5,9},{7,11},{... | collective-permute-start | bytes 1376264 | tf_op jit(solution)/shard_map/ppermute | solution.py:699
  195.2 6.1 %collective-permute-start.21 = (bf16[1,64,1792]{2,1,0:T(8,128)(2,1)S(1)}, bf16[1,64,1792]{2,1,0:T(8,128)(2,1)S(1)}, u32[]{:S(2)}, u32[]{:S(2)}) collective-permute-start(bf16[1,64,1792]{2,1,0:T(8,128)(2,1)S(1)} %get-tuple-element.168), channel_id=1, source_target_pairs={{0,1},{1,0},{2,3},{3,2},{4,5},{5,4},{6,7},{7,6},{8,9},{9,8},{10,11... | collective-permute-start | bytes 688136 | tf_op jit(solution)/shard_map/ppermute | solution.py:598
  201.7 8.4 %collective-permute-start.24 = (bf16[1,64,1792]{2,1,0:T(8,128)(2,1)S(1)}, bf16[1,64,1792]{2,1,0:T(8,128)(2,1)S(1)}, u32[]{:S(2)}, u32[]{:S(2)}) collective-permute-start(bf16[1,64,1792]{2,1,0:T(8,128)(2,1)S(1)} %add.68), channel_id=1, source_target_pairs={{4,0},{6,2},{8,4},{10,6},{12,8},{14,10},{5,1},{7,3},{9,5},{11,7},{... | collective-permute-start | bytes 688136 | tf_op jit(solution)/shard_map/ppermute | solution.py:702
  203.0 8.5 %collective-permute-start.25 = (bf16[1,64,1792]{2,1,0:T(8,128)(2,1)S(1)}, bf16[1,64,1792]{2,1,0:T(8,128)(2,1)S(1)}, u32[]{:S(2)}, u32[]{:S(2)}) collective-permute-start(bf16[1,64,1792]{2,1,0:T(8,128)(2,1)S(1)} %add.68), channel_id=1, source_target_pairs={{0,4},{2,6},{4,8},{6,10},{8,12},{10,14},{1,5},{3,7},{5,9},{7,11},{... | collective-permute-start | bytes 688136 | tf_op jit(solution)/shard_map/ppermute | solution.py:699
  219.6 4.1 %collective-permute-start.26 = (bf16[8,64,1792]{2,1,0:T(8,128)(2,1)}, bf16[8,64,1792]{2,1,0:T(8,128)(2,1)S(1)}, u32[]{:S(2)}, u32[]{:S(2)}) collective-permute-start(bf16[8,64,1792]{2,1,0:T(8,128)(2,1)} %get-tuple-element.170), channel_id=1, source_target_pairs={{0,2},{2,0},{4,6},{6,4},{8,10},{10,8},{12,14},{14,12},{1,3},{3,1},... | collective-permute-start | bytes 5505032 | tf_op jit(solution)/shard_map/ppermute | solution.py:696
  (14 other events, 60.6 us)
where the time goes:
time: 238 us; the launch traced here: 237 us
  Pallas kernels  108 us (45%)
  waiting for transfers between devices  60.1 us (25%)
  starting transfers between devices  48.2 us (20%)
  between operations  15.1 us (6%)
  local copies, waits for them, and re-layouts  5.63 us (2%)
    pallas_call x3, Pallas kernels, mlp(): pl.pallas_call(functools.partial(mlp_kernel, len(after)), out_shape=(jax....  49.9 us
    ppermute x10, waiting for transfers between devices, swap(): return lax.ppermute(value, 'tensor', [(0, 1), (1, 0)])  26.9 us
    ppermute x6, starting transfers between devices, to_right(): return lax.ppermute(value, 'dp', rightwards)  24.8 us
    pallas_call x3, Pallas kernels, attend(): pl.pallas_call(functools.partial(attend_kernel, len(after)), out_shape=ja...  22.7 us
    pallas_call x5, Pallas kernels, choose(): pl.pallas_call(functools.partial(choose_kernel, parts, len(sources)), out...  17.5 us
    ppermute x6, waiting for transfers between devices, to_left(): return lax.ppermute(value, 'dp', leftwards)  15.9 us
    ppermute x6, waiting for transfers between devices, to_right(): return lax.ppermute(value, 'dp', rightwards)  12.5 us
    ppermute x10, starting transfers between devices, swap(): return lax.ppermute(value, 'tensor', [(0, 1), (1, 0)])  10.6 us
  transfers between devices with their start and end apart: 27, of which 15 were waited for; matrix products, arithmetic and copies ran while one was open for 1% of the time, Pallas kernels for 35%

commit v1 on v0

--- a/solution.py
+++ b/solution.py
@@ -8,8 +8,8 @@
 from jax.sharding import PartitionSpec as P
 
 HEAD_DIM = 112
-CHUNKS = (2, 2, 1)
-STARTS = (0, 2, 4)
+CHUNKS = (3, 2)
+STARTS = (0, 3)
 ROOM = 5
 PAGE_HALF = 8
 GROUP_ROWS = 16
@@ -78,7 +78,8 @@
 AT_SLOW_SOURCE = AT_SHORT + 1
 AT_SLOW_PLACE = AT_SLOW_SOURCE + ROOM
 AT_SLOW_HOME = AT_SLOW_PLACE + ROOM
-AT_SLOW_SEND = AT_SLOW_HOME + 2 * PAGE_HALF
+AT_IN_ORDER = AT_SLOW_HOME + 2 * PAGE_HALF
+AT_SLOW_SEND = AT_IN_ORDER + 2 * PAGE_HALF
 
 
 def plan_kernel(pages, device_ref, count_ref, table_ref):
@@ -87,14 +88,16 @@
     core, chip = device & 1, device >> 1
     ends = page_ends_of(count_ref, pages)
     held, dealt, short = line_plan(ends, chips, core)
-    short_other = line_plan(ends, chips, 1 - core)[2]
-    table_ref[AT_SHORT] = jnp.where(short + short_other > 0, 1, 0)
-    falls = [jnp.where(held[i] - dealt[i] > 2, 1, 0) for i in range(chips)]
+    held_mate, dealt_mate, short_mate = line_plan(ends, chips, 1 - core)
+    table_ref[AT_SHORT] = jnp.where(short + short_mate > 0, 1, 0)
+    falls, falls_mate = (
+        [jnp.where(ranks[i] - ranks_dealt[i] > 2, 1, 0) for i in range(chips)]
+        for ranks, ranks_dealt in ((held, dealt), (held_mate, dealt_mate))
+    )
 
     low, high = pick_at(held, chip), pick_at(held, chip + 1)
     first, end = pick_at(dealt, chip), pick_at(dealt, chip + 1)
-    before = pick_at(dealt, chip - 1)
-    falls_here, falls_right, falls_left = (pick_at(falls, chip + i) for i in (0, 1, -1))
+    falls_here = pick_at(falls, chip)
     own_start, own_end = pick_at(ends, device), pick_at(ends, device + 1)
     mate_start = pick_at(ends, device ^ 1)
 
@@ -123,23 +126,30 @@
             node = node + jnp.where(held[place] <= rank, 1, 0)
         table_ref[AT_SLOW_SOURCE + slot] = 2 * node + core
         table_ref[AT_SLOW_PLACE + slot] = offset
-    for half, start in enumerate((own_start, mate_start)):
+    sides = len(CHUNKS)
+    for half, (ranks_dealt, turns) in enumerate(((dealt, falls), (dealt_mate, falls_mate))):
+        lane = core ^ half
+        here, there = pick_at(ranks_dealt, chip), pick_at(ranks_dealt, chip + 1)
+        before = pick_at(ranks_dealt, chip - 1)
+        turns_here, turns_right, turns_left = (pick_at(turns, chip + i) for i in (0, 1, -1))
         for slot in range(PAGE_HALF):
-            rank = (start + ((start + core) & 1) + 2 * slot - core) >> 1
+            rank = (own_start + ((own_start + lane) & 1) + 2 * slot - lane) >> 1
             at = half * PAGE_HALF + slot
-            code = part_code(turned(rank - first, falls_here), 0)
-            right = part_code(turned(rank - end, falls_right), len(CHUNKS))
-            left = part_code(turned(rank - before, falls_left), 2 * len(CHUNKS))
-            code = jnp.where(rank >= end, right, code)
-            table_ref[AT_HOME + at] = jnp.where(rank < first, left, code)
-            node, start_there, falls_there = jnp.int32(0), jnp.int32(0), falls[0]
+            base = 3 * sides * half
+            code = part_code(turned(rank - here, turns_here), base)
+            right = part_code(turned(rank - there, turns_right), base + sides)
+            left = part_code(turned(rank - before, turns_left), base + 2 * sides)
+            code = jnp.where(rank >= there, right, code)
+            table_ref[AT_HOME + at] = jnp.where(rank < here, left, code)
+            node, start_there, turns_there = jnp.int32(0), jnp.int32(0), turns[0]
             for place in range(1, chips):
-                there = dealt[place] <= rank
-                node = node + jnp.where(there, 1, 0)
-                start_there = jnp.where(there, dealt[place], start_there)
-                falls_there = jnp.where(there, falls[place], falls_there)
-            slow = (2 * node + core) * ROOM + turned(rank - start_there, falls_there)
+                beyond = ranks_dealt[place] <= rank
+                node = node + jnp.where(beyond, 1, 0)
+                start_there = jnp.where(beyond, ranks_dealt[place], start_there)
+                turns_there = jnp.where(beyond, turns[place], turns_there)
+            slow = (2 * node + lane) * ROOM + turned(rank - start_there, turns_there)
             table_ref[AT_SLOW_HOME + at] = jnp.clip(slow, 0, pages * ROOM - 1)
+            table_ref[AT_IN_ORDER + at] = jnp.int32((6 * sides + half) * 16 + slot)
     for node in range(chips):
         for slot in range(ROOM):
             code = local_code(dealt[node] + slot)
@@ -176,9 +186,18 @@
     return blocks
 
 
-def pack_kernel(pages, device_ref, count_ref, keep_ref, home_ref, mine_ref, mate_ref):
+def kept_blocks_once(device_ref, count_ref, keep_ref, pages, held):
+    @pl.when(pl.program_id(0) == 0)
+    def _():
+        for slot, block in enumerate(kept_blocks(device_ref, count_ref, keep_ref, pages)):
+            held[slot] = block
+
+    return [held[slot] for slot in range(2 * PAGE_HALF)]
+
+
+def pack_kernel(pages, device_ref, count_ref, keep_ref, home_ref, mine_ref, mate_ref, held):
     page_blocks, width = home_ref.shape[1], home_ref.shape[2]
-    blocks = kept_blocks(device_ref, count_ref, keep_ref, pages)
+    blocks = kept_blocks_once(device_ref, count_ref, keep_ref, pages, held)
     span = GROUP_ROWS * page_blocks
     row = lax.broadcasted_iota(jnp.int32, (GROUP_ROWS, span), 0)
     column = lax.broadcasted_iota(jnp.int32, (GROUP_ROWS, span), 1)
@@ -208,87 +227,113 @@
                 pl.BlockSpec((GROUP_ROWS, page_blocks, width), lambda step, *_: (step, 0, 0))
             ],
             out_specs=(place, place),
+            scratch_shapes=[pltpu.SMEM((2 * PAGE_HALF,), jnp.int32)],
         ),
         compiler_params=pltpu.CompilerParams(vmem_limit_bytes=16 * MIB),
         name="pack",
     )(device, kept_count, keep_row, home)
 
 
-def merge_kernel(pages, device_ref, count_ref, keep_ref, home_ref, mine_ref, mate_ref, out_ref):
+def merge_kernel(pages, total, device_ref, count_ref, keep_ref, table_ref, slow_ref, home_ref, *refs):
+    sources = refs[:total]
+    out_ref, held, landed, sems = refs[total:]
     page_blocks, width = home_ref.shape[1], home_ref.shape[2]
-    blocks = kept_blocks(device_ref, count_ref, keep_ref, pages)
+    step = pl.program_id(0)
+    slots = 2 * PAGE_HALF
+
+    @pl.when(step == 0)
+    def _():
+        at = jnp.where(slow_ref[0] > 0, AT_IN_ORDER, AT_HOME)
+        start_copies(
+            sources,
+            [(table_ref[at + slot], landed.at[slot], sems.at[slot]) for slot in range(slots)],
+        )
+
+    blocks = kept_blocks_once(device_ref, count_ref, keep_ref, pages, held)
     span = GROUP_ROWS * page_blocks
-    depth = 2 * PAGE_HALF * GROUP_ROWS
+    depth = slots * GROUP_ROWS
     row = lax.broadcasted_iota(jnp.int32, (span, depth), 0)
     column = lax.broadcasted_iota(jnp.int32, (span, depth), 1)
-    slot = lax.broadcasted_iota(jnp.int32, (1, depth), 1) // GROUP_ROWS
+    slot_id = lax.broadcasted_iota(jnp.int32, (1, depth), 1) // GROUP_ROWS
     block_id = lax.broadcasted_iota(jnp.int32, (span, 1), 0) % page_blocks
     wanted = jnp.full((1, depth), -1, jnp.int32)
     kept = jnp.zeros((span, 1), jnp.int32)
     for place, block in enumerate(blocks):
-        wanted = jnp.where(slot == place, block, wanted)
+        wanted = jnp.where(slot_id == place, block, wanted)
         kept = kept + jnp.where(block_id == block, 1, 0)
     chosen = jnp.where(
         (row // page_blocks == column % GROUP_ROWS) & (row % page_blocks == wanted), 1.0, 0.0
     ).astype(BF16)
-    half = PAGE_HALF * GROUP_ROWS
-    source = jnp.concatenate(
-        [mine_ref[...].reshape(half, width), mate_ref[...].reshape(half, width)], axis=0
-    )
-    landed = jnp.dot(chosen, source, preferred_element_type=F32)
+
+    @pl.when(step == 0)
+    def _():
+        for slot in range(slots):
+            pltpu.make_async_copy(sources[0].at[0], landed.at[slot], sems.at[slot]).wait()
+
+    rows = pl.ds(pl.multiple_of(step * GROUP_ROWS, GROUP_ROWS), GROUP_ROWS)
+    source = landed[:, rows, :].reshape(depth, width)
+    result = jnp.dot(chosen, source, preferred_element_type=F32)
     home = home_ref[...].reshape(span, width).astype(F32)
-    merged = jnp.where(kept > 0, landed, home).astype(BF16)
+    merged = jnp.where(kept > 0, result, home).astype(BF16)
     out_ref[...] = merged.reshape(GROUP_ROWS, page_blocks, width)
 
 
-def merge(device, kept_count, keep_row, home, mine, mate):
+def merge(device, kept_count, keep_row, table, slow, home, sources):
     rows, page_blocks, width = home.shape
-    place = pl.BlockSpec((PAGE_HALF, GROUP_ROWS, width), lambda step, *_: (0, step, 0))
     page = pl.BlockSpec((GROUP_ROWS, page_blocks, width), lambda step, *_: (step, 0, 0))
-    return pl.pallas_call(
-        functools.partial(merge_kernel, kept_count.shape[0]),
+    slots = 2 * PAGE_HALF
+    return pl.pallas_call(
+        functools.partial(merge_kernel, kept_count.shape[0], len(sources)),
         out_shape=jax.ShapeDtypeStruct(home.shape, BF16),
         grid_spec=pltpu.PrefetchScalarGridSpec(
-            num_scalar_prefetch=3,
+            num_scalar_prefetch=5,
             grid=(rows // GROUP_ROWS,),
-            in_specs=[page, place, place],
+            in_specs=[page] + [pl.BlockSpec(memory_space=pl.ANY)] * len(sources),
             out_specs=page,
+            scratch_shapes=[
+                pltpu.SMEM((slots,), jnp.int32),
+                pltpu.VMEM((slots, rows, width), BF16),
+                pltpu.SemaphoreType.DMA((slots,)),
+            ],
         ),
-        compiler_params=pltpu.CompilerParams(vmem_limit_bytes=16 * MIB),
+        compiler_params=pltpu.CompilerParams(vmem_limit_bytes=20 * MIB),
+        cost_estimate=SMALL_COST,
         name="merge",
-    )(device, kept_count, keep_row, home, mine, mate)
+    )(device, kept_count, keep_row, table, slow, home, *sources)
+
+
+def start_copies(sources, wanted):
+    for code, target, sem in wanted:
+        which, place = code >> 4, code & 15
+        for index, source in enumerate(sources):
+            if len(sources) == 1:
+                here = which > -(1 << 20)
+            elif index == 0:
+                here = which <= 0
+            elif index == len(sources) - 1:
+                here = which >= index
+            else:
+                here = which == index
+
+            @pl.when(here)
+            def _(source=source, place=place, target=target, sem=sem):
+                inside = jnp.minimum(place, source.shape[0] - 1)
+                pltpu.make_async_copy(source.at[inside], target, sem).start()
 
 
 def choose_kernel(parts, n_sources, table_ref, *refs):
     sources, outs, sems = refs[:n_sources], refs[-1 - len(parts) : -1], refs[-1]
-    number = 0
-    for (at, total), out_ref in zip(parts, outs):
-        for slot in range(total):
-            code = table_ref[at + slot]
-            which, place = code >> 4, code & 15
-            for index, source in enumerate(sources):
-                if len(sources) == 1:
-                    here = which > -(1 << 20)
-                elif index == 0:
-                    here = which <= 0
-                elif index == len(sources) - 1:
-                    here = which >= index
-                else:
-                    here = which == index
-
-                @pl.when(here)
-                def _(source=source, out_ref=out_ref, slot=slot, place=place, number=number):
-                    inside = jnp.minimum(place, source.shape[0] - 1)
-                    pltpu.make_async_copy(
-                        source.at[inside], out_ref.at[slot], sems.at[number]
-                    ).start()
-
-            number += 1
-    number = 0
-    for (_, total), out_ref in zip(parts, outs):
-        for slot in range(total):
-            pltpu.make_async_copy(sources[0].at[0], out_ref.at[slot], sems.at[number]).wait()
-            number += 1
+    targets = [
+        (at + slot, out_ref.at[slot])
+        for (at, total), out_ref in zip(parts, outs)
+        for slot in range(total)
+    ]
+    start_copies(
+        sources,
+        [(table_ref[at], target, sems.at[number]) for number, (at, target) in enumerate(targets)],
+    )
+    for number, (_, target) in enumerate(targets):
+        pltpu.make_async_copy(sources[0].at[0], target, sems.at[number]).wait()
 
 
 def choose(table, parts, sources, name, after=()):
@@ -568,7 +613,11 @@
             pltpu.SemaphoreType.DMA((SLOTS,)),
         ],
         compiler_params=pltpu.CompilerParams(vmem_limit_bytes=46 * MIB),
-        cost_estimate=SMALL_COST,
+        cost_estimate=pl.CostEstimate(
+            flops=4 * total * width * (span + hidden),
+            bytes_accessed=4 * width * (span + hidden),
+            transcendentals=0,
+        ),
         name="mlp",
     )(
         own, other, mine, theirs, rows_params, b_up, in_hbm(w_mine), w_theirs, in_hbm(w_up),
@@ -629,6 +678,30 @@
     core = lax.axis_index("dp") & 1
     group = lax.axis_index("groups")
     return 2 * group + core, 2 * (1 - group) + core, w_out.shape[0] // 4
+
+
+def piece_kernel(n_after, number_ref, w_ref, *refs):
+    out_ref, sem = refs[n_after:]
+    piece = out_ref.shape[0]
+    rows = pl.ds(pl.multiple_of(number_ref[0] * piece, piece), piece)
+    copy = pltpu.make_async_copy(w_ref.at[rows, :], out_ref, sem)
+    copy.start()
+    copy.wait()
+
+
+def w_out_piece(w_out, after):
+    number, _, piece = w_out_place(w_out)
+    any_space = pl.BlockSpec(memory_space=pl.ANY)
+    return pl.pallas_call(
+        functools.partial(piece_kernel, len(after)),
+        out_shape=jax.ShapeDtypeStruct((piece, w_out.shape[1]), BF16),
+        in_specs=[pl.BlockSpec(memory_space=pltpu.SMEM)] + [any_space] * (1 + len(after)),
+        out_specs=pl.BlockSpec(memory_space=pltpu.VMEM),
+        scratch_shapes=[pltpu.SemaphoreType.DMA],
+        compiler_params=pltpu.CompilerParams(vmem_limit_bytes=4 * MIB),
+        cost_estimate=SMALL_COST,
+        name="w_piece",
+    )(number.astype(jnp.int32).reshape(1), in_hbm(w_out), *after)
 
 
 def other_w_out(w_out, near, early, late):
@@ -717,35 +790,36 @@
     came_right = [to_right(value) for value in going[: len(parts)]]
     came_left = [to_left(value) for value in going[len(parts) :]]
 
-    def deal_fast(chunk, spare, after):
+    def deal_fast(chunk, after):
         right = [came_right[min(part, chunk)] for part in range(len(parts))]
         left = [came_left[min(part, chunk)] for part in range(len(parts))]
-        wanted = [(AT_DEALT + at, size) for at, size in parts[chunk : len(parts) if spare else chunk + 1]]
-        return choose(table, wanted, [mine, from_mate] + right + left, "deal_%d" % chunk, after)
-
-    def deal_slow():
+        at, size = parts[chunk]
+        sources = [mine, from_mate] + right + left
+        return choose(table, [(AT_DEALT + at, size)], sources, "deal_%d" % chunk, after)[0]
+
+    def deal_slow(chunk):
         chips = dp_size // 2
         (picked,) = choose(table, [(AT_SLOW_SEND, ROOM * chips)], [mine, from_mate], "deal_slow")
         picked = picked.reshape((chips, ROOM) + picked.shape[1:])
         spread = jnp.repeat(picked, 2, axis=0)
         arrived = lax.all_to_all(spread, "dp", split_axis=0, concat_axis=0, tiled=True)
-        dealt = [arrived[table[AT_SLOW_SOURCE + j], table[AT_SLOW_PLACE + j]] for j in range(ROOM)]
-        return tuple(jnp.stack(dealt[at : at + size]) for at, size in parts)
-
-    spares = lax.cond(short, deal_slow, functools.partial(deal_fast, 0, True, ()))
-
-    def deal(chunk, after):
-        return lax.cond(
-            short, lambda: spares[chunk], lambda: deal_fast(chunk, False, after)[0]
+        at, size = parts[chunk]
+        return jnp.stack(
+            [
+                arrived[table[AT_SLOW_SOURCE + j], table[AT_SLOW_PLACE + j]]
+                for j in range(at, at + size)
+            ]
         )
+
+    def deal(chunk, after=()):
+        return lax.cond(short, lambda: deal_slow(chunk), lambda: deal_fast(chunk, after))
 
     if paired:
         (pre_gain, pre_shift, w_qkv, b_qkv, w_out, b_out, mlp_gain, mlp_shift, w_up, b_up, w_down,
          b_down) = params
         rows_params = jnp.stack([pre_gain, pre_shift, mlp_gain, mlp_shift, b_out, b_down])
         b_up = b_up.reshape(1, -1)
-        number, _, piece = w_out_place(w_out)
-        w_near = swap(lax.dynamic_slice_in_dim(w_out, number * piece, piece, 0))
+        w_near = swap(w_out_piece(w_out, [going[0]]))
 
         def start(own, after):
             other = swap(own)
@@ -756,36 +830,26 @@
             keep, send = mlp(*state, rows_params, b_up, weights, after)
             return keep, swap(send)
 
-        blocks_0 = spares[0]
-        state_0 = start(blocks_0, [])
-        blocks_1 = deal(1, [])
-        state_1 = start(blocks_1, [])
-        blocks_2 = deal(2, [])
-        state_2 = start(blocks_2, [state_1[2]])
-        w_theirs = other_w_out(w_out, w_near, [blocks_0], [blocks_1, state_0[2]])
+        state_0 = start(deal(0), [])
+        state_1 = start(deal(1), [])
+        w_theirs = other_w_out(
+            w_out, w_near, [state_0[1], came_right[1], came_left[1]], [state_0[2], state_1[0]]
+        )
         weights = (w_out, w_theirs, w_up, w_down)
-        done_0 = finish(state_0, [state_2[2]])
-        done_1 = finish(state_1, [done_0[0], state_2[3]])
-        done_2 = finish(state_2, [done_1[0]])
+        done_0 = finish(state_0, [state_1[2]])
+        done_1 = finish(state_1, [done_0[0]])
         results, from_right, from_left = [], [], []
-        for done, beside in ((done_0, done_1[:1]), (done_1, done_2[:1]), (done_2, ())):
+        for done, beside in ((done_0, done_1[:1]), (done_1, ())):
             results.append(add(*done, list(beside) + from_right[-1:] + from_left[-1:]))
             from_right.append(to_left(results[-1]))
             from_left.append(to_right(results[-1]))
     else:
-        results = [
-            encode_split(part, params) for part in (spares[0], deal(1, ()), deal(2, ()))
-        ]
+        results = [encode_split(deal(chunk), params) for chunk in range(len(parts))]
         from_right = [to_left(value) for value in results]
         from_left = [to_right(value) for value in results]
 
-    def home_fast():
-        return choose(
-            table,
-            [(AT_HOME, PAGE_HALF), (AT_HOME + PAGE_HALF, PAGE_HALF)],
-            results + from_right + from_left,
-            "home_fast",
-        )
+    back = results + from_right + from_left
+    back = back + [to_mate(value) for value in back]
 
     def home_slow():
         spread = lax.all_gather(jnp.concatenate(results), "dp", axis=0, tiled=True)
@@ -795,8 +859,9 @@
             jnp.take(spread, places[PAGE_HALF:], axis=0),
         )
 
-    back_mine, back_mate = lax.cond(short, home_slow, home_fast)
-    return merge(device, kept_count, keep_row, home, back_mine, to_mate(back_mate))[None]
+    found = lax.cond(short, home_slow, lambda: (mine, from_mate))
+    slow = short.astype(jnp.int32).reshape(1)
+    return merge(device, kept_count, keep_row, table, slow, home, back + list(found))[None]
 
 
 def solution(mesh):

time: 238 us -> 227 us (0.954)
  waiting for transfers between devices: 60.1 us -> 76.7 us
  Pallas kernels: 108 us -> 92.3 us
  starting transfers between devices: 48.2 us -> 38.7 us
  local copies, waits for them, and re-layouts: 5.63 us -> 2.49 us
    pallas_call x5 -> x3, Pallas kernels: 17.5 us -> 6.83 us  [choose(): pl.pallas_call(functools.partial(choose_kernel, parts, len(sources)), out...]
    ppermute x10 -> x7, waiting for transfers between devices: 26.9 us -> 36.2 us  [swap(): return lax.ppermute(value, 'tensor', [(0, 1), (1, 0)])]
    pallas_call x3 -> x2, Pallas kernels: 49.9 us -> 42.2 us  [mlp(): pl.pallas_call(functools.partial(mlp_kernel, len(after)), out_shape=(jax....]
    ppermute x6 -> x4, starting transfers between devices: 24.8 us -> 19 us  [to_right(): return lax.ppermute(value, 'dp', rightwards)]
    pallas_call x1 -> x2, Pallas kernels: 6.54 us -> 10.2 us  [the longest x1 8.93 us: merge(): pl.pallas_call(functools.partial(merge_kernel, kept_count.shape[0], len(s...]
    ppermute x1, waiting for transfers between devices: 0.01 us -> 3.47 us  [other_w_out(): side = lax.ppermute(sent, 'groups', [(0, 1), (1, 0)])[0]]
    ppermute x6 -> x4, waiting for transfers between devices: 12.5 us -> 15.4 us  [to_right(): return lax.ppermute(value, 'dp', rightwards)]
    ppermute x6 -> x4, starting transfers between devices: 7.73 us -> 5.14 us  [to_left(): return lax.ppermute(value, 'dp', leftwards)]
  transfers between devices with their start and end apart: 27 -> 25, of which waited for: 15 -> 14; matrix products, arithmetic and copies ran while one was open for 1% -> 0% of each run, Pallas kernels for 35% -> 32%
where the time goes in v1:
time: 227 us; the launch traced here: 225 us
  Pallas kernels  92.3 us (41%)
  waiting for transfers between devices  76.7 us (34%)
  starting transfers between devices  38.7 us (17%)
  between operations  15.1 us (7%)
  local copies, waits for them, and re-layouts  2.49 us (1%)
    pallas_call x2, Pallas kernels, mlp(): pl.pallas_call(functools.partial(mlp_kernel, len(after)), out_shape=(jax....  42.2 us
    ppermute x7, waiting for transfers between devices, swap(): return lax.ppermute(value, 'tensor', [(0, 1), (1, 0)])  36.2 us
    pallas_call x2, Pallas kernels, attend(): pl.pallas_call(functools.partial(attend_kernel, len(after)), out_shape=ja...  20.2 us
    ppermute x4, starting transfers between devices, to_right(): return lax.ppermute(value, 'dp', rightwards)  19 us
    ppermute x4, waiting for transfers between devices, to_left(): return lax.ppermute(value, 'dp', leftwards)  17.2 us
    ppermute x4, waiting for transfers between devices, to_right(): return lax.ppermute(value, 'dp', rightwards)  15.4 us
    pallas_call x1, Pallas kernels, merge(): pl.pallas_call(functools.partial(merge_kernel, kept_count.shape[0], len(s...  8.93 us
    ppermute x7, starting transfers between devices, swap(): return lax.ppermute(value, 'tensor', [(0, 1), (1, 0)])  8.58 us
  transfers between devices with their start and end apart: 25, of which 14 were waited for; matrix products, arithmetic and copies ran while one was open for 0% of the time, Pallas kernels for 32%

profile of v1, /device:TPU:0, one launch (start us, length us, event | category | flops | bytes accessed | tf_op | source)
XLA Modules:
  0.0 225.4 jit_solution(331752373258921602)
XLA Ops:
  6.5 4.6 %pack.1 = (bf16[8,64,1792]{2,1,0:T(8,128)(2,1)S(1)}, bf16[8,64,1792]{2,1,0:T(8,128)(2,1)S(1)}) custom-call(s32[1]{0:T(128)} %bitcast.19.device_ref, s32[8]{0:T(128)} %count_ref.5, s32[16]{0:T(128)} %bitcast.42, bf16[64,16,1792]{2,1,0:T(8,128)(2,1)} %bitcast.40), custom_call_target="tpu_custom_call" | custom-call | tf_op jit(solution)/shard_map/pack/pallas_call | solution.py:220
  11.6 2.0 plan.1.table_ref
  15.0 3.7 %send.1 = (bf16[3,64,1792]{2,1,0:T(8,128)(2,1)S(1)}, bf16[2,64,1792]{2,1,0:T(8,128)(2,1)S(1)}, bf16[3,64,1792]{2,1,0:T(8,128)(2,1)S(1)}, bf16[2,64,1792]{2,1,0:T(8,128)(2,1)S(1)}) custom-call(s32[94]{0:T(128)S(1)} %plan.1.table_ref, bf16[8,64,1792]{2,1,0:T(8,128)(2,1)S(1)} %get-tuple-element.91.refs_0_, bf16[8,64,1792]{2,1,0:T(8,128)(2,1)S(1)} %collective-permute-done.1.refs_1_), custom_call_target="tpu_custom_call" | custom-call | flops 1000 | bytes 1000 | tf_op jit(solution)/shard_map/send/pallas_call | solution.py:342
  20.9 6.3 %collective-permute-start.2 = (bf16[3,64,1792]{2,1,0:T(8,128)(2,1)S(1)}, bf16[3,64,1792]{2,1,0:T(8,128)(2,1)}, u32[]{:S(2)}, u32[]{:S(2)}) collective-permute-start(bf16[3,64,1792]{2,1,0:T(8,128)(2,1)S(1)} %get-tuple-element.93.refs_0_), channel_id=1, source_target_pairs={{0,4},{2,6},{4,8},{6,10},{8,12},{10,14},{1,5},{3,7},{5,9},{7,11},{... | collective-permute-start | bytes 2064392 | tf_op jit(solution)/shard_map/ppermute | solution.py:772
  28.5 2.0 collective-permute-start.6
  31.8 2.9 %collective-permute-start = (f32[1]{0:T(128)}, f32[1]{0:T(128)}, u32[]{:S(2)}, u32[]{:S(2)}) collective-permute-start(f32[1]{0:T(128)} %convert_element_type.12), channel_id=1, source_target_pairs={{0,16},{16,0},{1,17},{17,1},{2,18},{18,2},{3,19},{19,3},{4,20},{20... | collective-permute-start | bytes 20 | tf_op jit(solution)/shard_map/ppermute | solution.py:782
  36.1 4.1 %collective-permute-done.3 = bf16[3,64,1792]{2,1,0:T(8,128)(2,1)} collective-permute-done((bf16[3,64,1792]{2,1,0:T(8,128)(2,1)S(1)}, bf16[3,64,1792]{2,1,0:T(8,128)(2,1)}, u32[]{:S(2)}, u32[]{:S(2)}) %collective-permute-start.3) | collective-permute-done | bytes 688160 | tf_op jit(solution)/shard_map/ppermute | solution.py:775
  41.4 1.5 conditional.3
  41.4 1.5 deal_0.1
  43.8 1.7 collective-permute-start.4
  45.5 5.0 %collective-permute-start.7 = (bf16[2,64,1792]{2,1,0:T(8,128)(2,1)S(1)}, bf16[2,64,1792]{2,1,0:T(8,128)(2,1)S(1)}, u32[]{:S(2)}, u32[]{:S(2)}) collective-permute-start(bf16[2,64,1792]{2,1,0:T(8,128)(2,1)S(1)} %copy-done.4), channel_id=1, source_target_pairs={{0,4},{2,6},{4,8},{6,10},{8,12},{10,14},{1,5},{3,7},{5,9},{7,11},{... | collective-permute-start | bytes 1376264 | tf_op jit(solution)/shard_map/ppermute | solution.py:772
  51.8 7.3 %collective-permute-done.7.refs_2_ = bf16[2,64,1792]{2,1,0:T(8,128)(2,1)S(1)} collective-permute-done((bf16[2,64,1792]{2,1,0:T(8,128)(2,1)S(1)}, bf16[2,64,1792]{2,1,0:T(8,128)(2,1)S(1)}, u32[]{:S(2)}, u32[]{:S(2)}) %collective-permute-start.7) | collective-permute-done | bytes 458784 | tf_op jit(solution)/shard_map/ppermute | solution.py:772
  59.1 4.1 %collective-permute-done.8.refs_3_ = bf16[2,64,1792]{2,1,0:T(8,128)(2,1)S(1)} collective-permute-done((bf16[2,64,1792]{2,1,0:T(8,128)(2,1)S(1)}, bf16[2,64,1792]{2,1,0:T(8,128)(2,1)S(1)}, u32[]{:S(2)}, u32[]{:S(2)}) %collective-permute-start.8) | collective-permute-done | bytes 458784 | tf_op jit(solution)/shard_map/ppermute | solution.py:775
  64.3 1.8 collective-permute-start.9
  66.3 1.6 conditional.4
  66.3 1.6 deal_1.1
  68.0 11.6 %attend.2.refs_2_.mine_ref = bf16[2,3,64,896]{3,2,1,0:T(8,128)(2,1)S(1)} custom-call(bf16[3,64,1792]{2,1,0:T(8,128)(2,1)} %copy-done.13, bf16[3,64,1792]{2,1,0:T(8,128)(2,1)S(1)} %collective-permute-done.4.other_ref.refs_1_, f32[6,1792]{1,0:T(8,128)S(1)} %stack.48.rows_ref, f32[3,896]{1,0:T(4,128)S(1)} %copy-done.2, bf16[3,1792,896]{2,1,0:T(8,128)(2,1)} %w_ref.5), custom_call_target="tpu_custom_call" | custom-call | flops 1000 | bytes 1000 | tf_op jit(solution)/shard_map/attend/pallas_call | solution.py:473
  79.6 3.5 %collective-permute-done.9 = bf16[1,224,1792]{2,1,0:T(8,128)(2,1)S(1)} collective-permute-done((bf16[1,224,1792]{2,1,0:T(8,128)(2,1)}, bf16[1,224,1792]{2,1,0:T(8,128)(2,1)S(1)}, u32[]{:S(2)}, u32[]{:S(2)}) %collective-permute-start.9) | collective-permute-done | bytes 802848 | tf_op jit(solution)/shard_map/ppermute | solution.py:711
  86.6 25.5 %collective-permute-done.11.other_ref = bf16[2,64,1792]{2,1,0:T(8,128)(2,1)S(1)} collective-permute-done((bf16[2,64,1792]{2,1,0:T(8,128)(2,1)}, bf16[2,64,1792]{2,1,0:T(8,128)(2,1)S(1)}, u32[]{:S(2)}, u32[]{:S(2)}) %collective-permute-start.11) | collective-permute-done | bytes 458784 | tf_op jit(solution)/shard_map/ppermute | solution.py:647
  112.1 8.6 %attend.3.refs_0_.mine_ref = bf16[2,2,64,896]{3,2,1,0:T(8,128)(2,1)S(1)} custom-call(bf16[2,64,1792]{2,1,0:T(8,128)(2,1)} %copy-done.11, bf16[2,64,1792]{2,1,0:T(8,128)(2,1)S(1)} %collective-permute-done.11.other_ref, f32[6,1792]{1,0:T(8,128)S(1)} %stack.48.rows_ref, f32[3,896]{1,0:T(4,128)S(1)} %copy-done.2, bf16[3,1792,896]{2,1,0:T(8,128)(2,1)} %w_ref.5), custom_call_target="tpu_custom_call" | custom-call | flops 1000 | bytes 1000 | tf_op jit(solution)/shard_map/attend/pallas_call | solution.py:473
  122.1 2.1 join.1.w_theirs
  124.3 24.7 %mlp.2 = (f32[3,64,1792]{2,1,0:T(8,128)S(1)}, bf16[3,64,1792]{2,1,0:T(8,128)(2,1)S(1)}) custom-call(bf16[3,64,1792]{2,1,0:T(8,128)(2,1)S(1)} %copy-done.14, bf16[3,64,1792]{2,1,0:T(8,128)(2,1)S(1)} %collective-permute-done.4.other_ref.refs_1_, bf16[2,3,64,896]{3,2,1,0:T(8,128)(2,1)S(1)} %attend.2.refs_2_.mine_ref, ...), custom_call_target="tpu_custom_call" | custom-call | flops 15149826048 | bytes 39452672 | tf_op jit(solution)/shard_map/mlp/pallas_call | solution.py:596
  149.8 17.5 %mlp.3 = (f32[2,64,1792]{2,1,0:T(8,128)S(1)}, bf16[2,64,1792]{2,1,0:T(8,128)(2,1)S(1)}) custom-call(bf16[2,64,1792]{2,1,0:T(8,128)(2,1)S(1)} %copy-done.12, bf16[2,64,1792]{2,1,0:T(8,128)(2,1)S(1)} %collective-permute-done.11.other_ref, bf16[2,2,64,896]{3,2,1,0:T(8,128)(2,1)S(1)} %attend.3.refs_0_.mine_ref, ...), custom_call_target="tpu_custom_call" | custom-call | flops 10099884032 | bytes 39452672 | tf_op jit(solution)/shard_map/mlp/pallas_call | solution.py:596
  168.2 3.6 %collective-permute-start.16 = (bf16[3,64,1792]{2,1,0:T(8,128)(2,1)}, bf16[3,64,1792]{2,1,0:T(8,128)(2,1)S(1)}, u32[]{:S(2)}, u32[]{:S(2)}) collective-permute-start(bf16[3,64,1792]{2,1,0:T(8,128)(2,1)} %add.61.refs_0_), channel_id=1, source_target_pairs={{0,4},{2,6},{4,8},{6,10},{8,12},{10,14},{1,5},{3,7},{5,9},{7,11},{... | collective-permute-start | bytes 2064392 | tf_op jit(solution)/shard_map/ppermute | solution.py:772
  173.8 10.7 %collective-permute-done.14.came_ref = bf16[2,64,1792]{2,1,0:T(8,128)(2,1)S(1)} collective-permute-done((bf16[2,64,1792]{2,1,0:T(8,128)(2,1)S(1)}, bf16[2,64,1792]{2,1,0:T(8,128)(2,1)S(1)}, u32[]{:S(2)}, u32[]{:S(2)}) %collective-permute-start.14) | collective-permute-done | bytes 458784 | tf_op jit(solution)/shard_map/ppermute | solution.py:647
  184.5 1.6 collective-permute-done.16.refs_1_.refs_4_
  186.1 4.0 %collective-permute-done.15.refs_0_.refs_2_ = bf16[3,64,1792]{2,1,0:T(8,128)(2,1)S(1)} collective-permute-done((bf16[3,64,1792]{2,1,0:T(8,128)(2,1)}, bf16[3,64,1792]{2,1,0:T(8,128)(2,1)S(1)}, u32[]{:S(2)}, u32[]{:S(2)}) %collective-permute-start.15) | collective-permute-done | bytes 688160 | tf_op jit(solution)/shard_map/ppermute | solution.py:775
  191.1 4.1 %collective-permute-start.18 = (bf16[2,64,1792]{2,1,0:T(8,128)(2,1)}, bf16[2,64,1792]{2,1,0:T(8,128)(2,1)}, u32[]{:S(2)}, u32[]{:S(2)}) collective-permute-start(bf16[2,64,1792]{2,1,0:T(8,128)(2,1)} %add.62.refs_1_), channel_id=1, source_target_pairs={{0,4},{2,6},{4,8},{6,10},{8,12},{10,14},{1,5},{3,7},{5,9},{7,11},{... | collective-permute-start | bytes 1376264 | tf_op jit(solution)/shard_map/ppermute | solution.py:772
  197.1 5.4 %collective-permute-done.18.refs_5_ = bf16[2,64,1792]{2,1,0:T(8,128)(2,1)} collective-permute-done((bf16[2,64,1792]{2,1,0:T(8,128)(2,1)}, bf16[2,64,1792]{2,1,0:T(8,128)(2,1)}, u32[]{:S(2)}, u32[]{:S(2)}) %collective-permute-start.18) | collective-permute-done | bytes 458784 | tf_op jit(solution)/shard_map/ppermute | solution.py:772
  202.5 4.9 %collective-permute-done.17.refs_3_ = bf16[2,64,1792]{2,1,0:T(8,128)(2,1)} collective-permute-done((bf16[2,64,1792]{2,1,0:T(8,128)(2,1)}, bf16[2,64,1792]{2,1,0:T(8,128)(2,1)}, u32[]{:S(2)}, u32[]{:S(2)}) %collective-permute-start.17) | collective-permute-done | bytes 458784 | tf_op jit(solution)/shard_map/ppermute | solution.py:775
  207.4 2.1 collective-permute-done.22.refs_9_
  209.6 8.9 %merge.1 = bf16[64,16,1792]{2,1,0:T(8,128)(2,1)} custom-call(s32[1]{0:T(128)} %bitcast.19.device_ref, s32[8]{0:T(128)} %count_ref.5, s32[16]{0:T(128)} %bitcast.43, s32[94]{0:T(128)S(1)} %plan.1.table_ref, s32[1]{0:T(128)} %convert_element_type.13.slow_ref, bf16[64,16,1792]{2,1,0:T(8,128)(2,1)} %bitcast.41, bf16[3,64,1792]{2,1,0:T(8,128)(2,1)} %add.61.refs_0_, ...), custom_call_target="tpu_custom_call" | custom-call | flops 1000 | bytes 1000 | tf_op jit(solution)/shard_map/merge/pallas_call | solution.py:285
  (87 shorter events, 22.7 us)
Async XLA Ops:
  11.1 3.9 %collective-permute-start.1 = (bf16[8,64,1792]{2,1,0:T(8,128)(2,1)S(1)}, bf16[8,64,1792]{2,1,0:T(8,128)(2,1)S(1)}, u32[]{:S(2)}, u32[]{:S(2)}) collective-permute-start(bf16[8,64,1792]{2,1,0:T(8,128)(2,1)S(1)} %get-tuple-element.92), channel_id=1, source_target_pairs={{0,2},{2,0},{4,6},{6,4},{8,10},{10,8},{12,14},{14,12},{1,3},{3,1},... | collective-permute-start | bytes 5505032 | tf_op jit(solution)/shard_map/ppermute | solution.py:769
  19.6 20.7 %collective-permute-start.3 = (bf16[3,64,1792]{2,1,0:T(8,128)(2,1)S(1)}, bf16[3,64,1792]{2,1,0:T(8,128)(2,1)}, u32[]{:S(2)}, u32[]{:S(2)}) collective-permute-start(bf16[3,64,1792]{2,1,0:T(8,128)(2,1)S(1)} %get-tuple-element.94), channel_id=1, source_target_pairs={{4,0},{6,2},{8,4},{10,6},{12,8},{14,10},{5,1},{7,3},{9,5},{11,7},{... | collective-permute-start | bytes 2064392 | tf_op jit(solution)/shard_map/ppermute | solution.py:775
  20.9 20.5 %collective-permute-start.2 = (bf16[3,64,1792]{2,1,0:T(8,128)(2,1)S(1)}, bf16[3,64,1792]{2,1,0:T(8,128)(2,1)}, u32[]{:S(2)}, u32[]{:S(2)}) collective-permute-start(bf16[3,64,1792]{2,1,0:T(8,128)(2,1)S(1)} %get-tuple-element.93.refs_0_), channel_id=1, source_target_pairs={{0,4},{2,6},{4,8},{6,10},{8,12},{10,14},{1,5},{3,7},{5,9},{7,11},{... | collective-permute-start | bytes 2064392 | tf_op jit(solution)/shard_map/ppermute | solution.py:772
  28.5 34.7 %collective-permute-start.6 = (bf16[224,1792]{1,0:T(8,128)(2,1)S(1)}, bf16[224,1792]{1,0:T(8,128)(2,1)S(1)}, u32[]{:S(2)}, u32[]{:S(2)}) collective-permute-start(bf16[224,1792]{1,0:T(8,128)(2,1)S(1)} %w_piece.1), channel_id=1, source_target_pairs={{0,1},{1,0},{2,3},{3,2},{4,5},{5,4},{6,7},{7,6},{8,9},{9,8},{10,11... | collective-permute-start | bytes 2408456 | tf_op jit(solution)/shard_map/ppermute | solution.py:647
  31.8 3.7 %collective-permute-start = (f32[1]{0:T(128)}, f32[1]{0:T(128)}, u32[]{:S(2)}, u32[]{:S(2)}) collective-permute-start(f32[1]{0:T(128)} %convert_element_type.12), channel_id=1, source_target_pairs={{0,16},{16,0},{1,17},{17,1},{2,18},{18,2},{3,19},{19,3},{4,20},{20... | collective-permute-start | bytes 20 | tf_op jit(solution)/shard_map/ppermute | solution.py:782
  43.8 22.3 %copy-start.18 = (f32[1792]{0:T(1024)S(1)}, f32[1792]{0:T(1024)}, u32[]{:S(2)}) copy-start(f32[1792]{0:T(1024)} %param.26) | copy-start | bytes 21508
  43.8 22.3 %copy-start.19 = (f32[1792]{0:T(1024)S(1)}, f32[1792]{0:T(1024)}, u32[]{:S(2)}) copy-start(f32[1792]{0:T(1024)} %param.27) | copy-start | bytes 21508
  43.8 22.3 %copy-start.20 = (f32[1792]{0:T(1024)S(1)}, f32[1792]{0:T(1024)}, u32[]{:S(2)}) copy-start(f32[1792]{0:T(1024)} %param.31) | copy-start | bytes 21508
  43.8 22.4 %copy-start.21 = (f32[1792]{0:T(1024)S(1)}, f32[1792]{0:T(1024)}, u32[]{:S(2)}) copy-start(f32[1792]{0:T(1024)} %param.32) | copy-start | bytes 21508
  43.8 22.4 %copy-start.22 = (f32[1792]{0:T(1024)S(1)}, f32[1792]{0:T(1024)}, u32[]{:S(2)}) copy-start(f32[1792]{0:T(1024)} %param.33) | copy-start | bytes 21508
  43.8 22.4 %copy-start.23 = (f32[1792]{0:T(1024)S(1)}, f32[1792]{0:T(1024)}, u32[]{:S(2)}) copy-start(f32[1792]{0:T(1024)} %param.37) | copy-start | bytes 21508
  43.8 19.4 %collective-permute-start.4 = (bf16[3,64,1792]{2,1,0:T(8,128)(2,1)}, bf16[3,64,1792]{2,1,0:T(8,128)(2,1)S(1)}, u32[]{:S(2)}, u32[]{:S(2)}) collective-permute-start(bf16[3,64,1792]{2,1,0:T(8,128)(2,1)} %copy-done.13), channel_id=1, source_target_pairs={{0,1},{1,0},{2,3},{3,2},{4,5},{5,4},{6,7},{7,6},{8,9},{9,8},{10,11... | collective-permute-start | bytes 2064392 | tf_op jit(solution)/shard_map/ppermute | solution.py:647
  45.5 13.6 %collective-permute-start.7 = (bf16[2,64,1792]{2,1,0:T(8,128)(2,1)S(1)}, bf16[2,64,1792]{2,1,0:T(8,128)(2,1)S(1)}, u32[]{:S(2)}, u32[]{:S(2)}) collective-permute-start(bf16[2,64,1792]{2,1,0:T(8,128)(2,1)S(1)} %copy-done.4), channel_id=1, source_target_pairs={{0,4},{2,6},{4,8},{6,10},{8,12},{10,14},{1,5},{3,7},{5,9},{7,11},{... | collective-permute-start | bytes 1376264 | tf_op jit(solution)/shard_map/ppermute | solution.py:772
  50.5 12.7 %collective-permute-start.8 = (bf16[2,64,1792]{2,1,0:T(8,128)(2,1)S(1)}, bf16[2,64,1792]{2,1,0:T(8,128)(2,1)S(1)}, u32[]{:S(2)}, u32[]{:S(2)}) collective-permute-start(bf16[2,64,1792]{2,1,0:T(8,128)(2,1)S(1)} %get-tuple-element.96), channel_id=1, source_target_pairs={{4,0},{6,2},{8,4},{10,6},{12,8},{14,10},{5,1},{7,3},{9,5},{11,7},{... | collective-permute-start | bytes 1376264 | tf_op jit(solution)/shard_map/ppermute | solution.py:775
  64.3 18.7 %collective-permute-start.9 = (bf16[1,224,1792]{2,1,0:T(8,128)(2,1)}, bf16[1,224,1792]{2,1,0:T(8,128)(2,1)S(1)}, u32[]{:S(2)}, u32[]{:S(2)}) collective-permute-start(bf16[1,224,1792]{2,1,0:T(8,128)(2,1)} %w_near.1), channel_id=1, source_target_pairs={{0,16},{16,0},{1,17},{17,1},{2,18},{18,2},{3,19},{19,3},{4,20},{20... | collective-permute-start | bytes 2408456 | tf_op jit(solution)/shard_map/ppermute | solution.py:711
  84.4 37.8 %collective-permute-start.10 = (bf16[2,224,1792]{2,1,0:T(8,128)(2,1)}, bf16[2,224,1792]{2,1,0:T(8,128)(2,1)}, u32[]{:S(2)}, u32[]{:S(2)}) collective-permute-start(bf16[2,224,1792]{2,1,0:T(8,128)(2,1)} %w_both.1), channel_id=1, source_target_pairs={{0,2},{2,0},{4,6},{6,4},{8,10},{10,8},{12,14},{14,12},{1,3},{3,1},... | collective-permute-start | bytes 4816904 | tf_op jit(solution)/shard_map/ppermute | solution.py:713
  84.4 39.8 %collective-permute-start.5 = (bf16[2,3,64,896]{3,2,1,0:T(8,128)(2,1)S(1)}, bf16[2,3,64,896]{3,2,1,0:T(8,128)(2,1)}, u32[]{:S(2)}, u32[]{:S(2)}) collective-permute-start(bf16[2,3,64,896]{3,2,1,0:T(8,128)(2,1)S(1)} %attend.2.refs_2_.mine_ref), channel_id=1, source_target_pairs={{0,1},{1,0},{2,3},{3,2},{4,5},{5,4},{6,7},{7,6},{8,9},{9,8},{10,11... | collective-permute-start | bytes 2064392 | tf_op jit(solution)/shard_map/ppermute | solution.py:647
  85.8 26.3 %collective-permute-start.11 = (bf16[2,64,1792]{2,1,0:T(8,128)(2,1)}, bf16[2,64,1792]{2,1,0:T(8,128)(2,1)S(1)}, u32[]{:S(2)}, u32[]{:S(2)}) collective-permute-start(bf16[2,64,1792]{2,1,0:T(8,128)(2,1)} %copy-done.11), channel_id=1, source_target_pairs={{0,1},{1,0},{2,3},{3,2},{4,5},{5,4},{6,7},{7,6},{8,9},{9,8},{10,11... | collective-permute-start | bytes 1376264 | tf_op jit(solution)/shard_map/ppermute | solution.py:647
  120.8 29.0 %collective-permute-start.13 = (bf16[2,2,64,896]{3,2,1,0:T(8,128)(2,1)S(1)}, bf16[2,2,64,896]{3,2,1,0:T(8,128)(2,1)S(1)}, u32[]{:S(2)}, u32[]{:S(2)}) collective-permute-start(bf16[2,2,64,896]{3,2,1,0:T(8,128)(2,1)S(1)} %attend.3.refs_0_.mine_ref), channel_id=1, source_target_pairs={{0,1},{1,0},{2,3},{3,2},{4,5},{5,4},{6,7},{7,6},{8,9},{9,8},{10,11... | collective-permute-start | bytes 1376264 | tf_op jit(solution)/shard_map/ppermute | solution.py:647
  124.3 25.5 %copy-start.12 = (bf16[2,64,1792]{2,1,0:T(8,128)(2,1)S(1)}, bf16[2,64,1792]{2,1,0:T(8,128)(2,1)}, u32[]{:S(2)}) copy-start(bf16[2,64,1792]{2,1,0:T(8,128)(2,1)} %copy-done.11) | copy-start | bytes 1376260
  149.0 18.3 %collective-permute-start.12 = (bf16[3,64,1792]{2,1,0:T(8,128)(2,1)S(1)}, bf16[3,64,1792]{2,1,0:T(8,128)(2,1)S(1)}, u32[]{:S(2)}, u32[]{:S(2)}) collective-permute-start(bf16[3,64,1792]{2,1,0:T(8,128)(2,1)S(1)} %get-tuple-element.98), channel_id=1, source_target_pairs={{0,1},{1,0},{2,3},{3,2},{4,5},{5,4},{6,7},{7,6},{8,9},{9,8},{10,11... | collective-permute-start | bytes 2064392 | tf_op jit(solution)/shard_map/ppermute | solution.py:647
  168.2 17.9 %collective-permute-start.16 = (bf16[3,64,1792]{2,1,0:T(8,128)(2,1)}, bf16[3,64,1792]{2,1,0:T(8,128)(2,1)S(1)}, u32[]{:S(2)}, u32[]{:S(2)}) collective-permute-start(bf16[3,64,1792]{2,1,0:T(8,128)(2,1)} %add.61.refs_0_), channel_id=1, source_target_pairs={{0,4},{2,6},{4,8},{6,10},{8,12},{10,14},{1,5},{3,7},{5,9},{7,11},{... | collective-permute-start | bytes 2064392 | tf_op jit(solution)/shard_map/ppermute | solution.py:772
  171.9 18.3 %collective-permute-start.15 = (bf16[3,64,1792]{2,1,0:T(8,128)(2,1)}, bf16[3,64,1792]{2,1,0:T(8,128)(2,1)S(1)}, u32[]{:S(2)}, u32[]{:S(2)}) collective-permute-start(bf16[3,64,1792]{2,1,0:T(8,128)(2,1)} %add.61.refs_0_), channel_id=1, source_target_pairs={{4,0},{6,2},{8,4},{10,6},{12,8},{14,10},{5,1},{7,3},{9,5},{11,7},{... | collective-permute-start | bytes 2064392 | tf_op jit(solution)/shard_map/ppermute | solution.py:775
  173.2 11.3 %collective-permute-start.14 = (bf16[2,64,1792]{2,1,0:T(8,128)(2,1)S(1)}, bf16[2,64,1792]{2,1,0:T(8,128)(2,1)S(1)}, u32[]{:S(2)}, u32[]{:S(2)}) collective-permute-start(bf16[2,64,1792]{2,1,0:T(8,128)(2,1)S(1)} %get-tuple-element.100), channel_id=1, source_target_pairs={{0,1},{1,0},{2,3},{3,2},{4,5},{5,4},{6,7},{7,6},{8,9},{9,8},{10,11... | collective-permute-start | bytes 1376264 | tf_op jit(solution)/shard_map/ppermute | solution.py:647
  173.8 23.2 %collective-permute-start.19 = (bf16[3,64,1792]{2,1,0:T(8,128)(2,1)}, bf16[3,64,1792]{2,1,0:T(8,128)(2,1)S(1)}, u32[]{:S(2)}, u32[]{:S(2)}) collective-permute-start(bf16[3,64,1792]{2,1,0:T(8,128)(2,1)} %add.61.refs_0_), channel_id=1, source_target_pairs={{0,2},{2,0},{4,6},{6,4},{8,10},{10,8},{12,14},{14,12},{1,3},{3,1},... | collective-permute-start | bytes 2064392 | tf_op jit(solution)/shard_map/ppermute | solution.py:769
  191.1 11.5 %collective-permute-start.18 = (bf16[2,64,1792]{2,1,0:T(8,128)(2,1)}, bf16[2,64,1792]{2,1,0:T(8,128)(2,1)}, u32[]{:S(2)}, u32[]{:S(2)}) collective-permute-start(bf16[2,64,1792]{2,1,0:T(8,128)(2,1)} %add.62.refs_1_), channel_id=1, source_target_pairs={{0,4},{2,6},{4,8},{6,10},{8,12},{10,14},{1,5},{3,7},{5,9},{7,11},{... | collective-permute-start | bytes 1376264 | tf_op jit(solution)/shard_map/ppermute | solution.py:772
  195.2 12.2 %collective-permute-start.17 = (bf16[2,64,1792]{2,1,0:T(8,128)(2,1)}, bf16[2,64,1792]{2,1,0:T(8,128)(2,1)}, u32[]{:S(2)}, u32[]{:S(2)}) collective-permute-start(bf16[2,64,1792]{2,1,0:T(8,128)(2,1)} %add.62.refs_1_), channel_id=1, source_target_pairs={{4,0},{6,2},{8,4},{10,6},{12,8},{14,10},{5,1},{7,3},{9,5},{11,7},{... | collective-permute-start | bytes 1376264 | tf_op jit(solution)/shard_map/ppermute | solution.py:775
  196.5 11.0 %collective-permute-start.23 = (bf16[3,64,1792]{2,1,0:T(8,128)(2,1)S(1)}, bf16[3,64,1792]{2,1,0:T(8,128)(2,1)S(1)}, u32[]{:S(2)}, u32[]{:S(2)}) collective-permute-start(bf16[3,64,1792]{2,1,0:T(8,128)(2,1)S(1)} %collective-permute-done.16.refs_1_.refs_4_), channel_id=1, source_target_pairs={{0,2},{2,0},{4,6},{6,4},{8,10},{10,8},{12,14},{14,12},{1,3},{3,1},... | collective-permute-start | bytes 2064392 | tf_op jit(solution)/shard_map/ppermute | solution.py:769
  196.5 10.9 %collective-permute-start.21 = (bf16[3,64,1792]{2,1,0:T(8,128)(2,1)S(1)}, bf16[3,64,1792]{2,1,0:T(8,128)(2,1)S(1)}, u32[]{:S(2)}, u32[]{:S(2)}) collective-permute-start(bf16[3,64,1792]{2,1,0:T(8,128)(2,1)S(1)} %collective-permute-done.15.refs_0_.refs_2_), channel_id=1, source_target_pairs={{0,2},{2,0},{4,6},{6,4},{8,10},{10,8},{12,14},{14,12},{1,3},{3,1},... | collective-permute-start | bytes 2064392 | tf_op jit(solution)/shard_map/ppermute | solution.py:769
  197.0 10.4 %collective-permute-start.20 = (bf16[2,64,1792]{2,1,0:T(8,128)(2,1)}, bf16[2,64,1792]{2,1,0:T(8,128)(2,1)}, u32[]{:S(2)}, u32[]{:S(2)}) collective-permute-start(bf16[2,64,1792]{2,1,0:T(8,128)(2,1)} %add.62.refs_1_), channel_id=1, source_target_pairs={{0,2},{2,0},{4,6},{6,4},{8,10},{10,8},{12,14},{14,12},{1,3},{3,1},... | collective-permute-start | bytes 1376264 | tf_op jit(solution)/shard_map/ppermute | solution.py:769
  202.5 4.9 %collective-permute-start.24 = (bf16[2,64,1792]{2,1,0:T(8,128)(2,1)}, bf16[2,64,1792]{2,1,0:T(8,128)(2,1)}, u32[]{:S(2)}, u32[]{:S(2)}) collective-permute-start(bf16[2,64,1792]{2,1,0:T(8,128)(2,1)} %collective-permute-done.18.refs_5_), channel_id=1, source_target_pairs={{0,2},{2,0},{4,6},{6,4},{8,10},{10,8},{12,14},{14,12},{1,3},{3,1},... | collective-permute-start | bytes 1376264 | tf_op jit(solution)/shard_map/ppermute | solution.py:769
  207.4 2.2 collective-permute-start.22
  (13 other events, 78.8 us)

commit v2 on v1

--- a/solution.py
+++ b/solution.py
@@ -70,9 +70,9 @@
     return held, dealt, short
 
 
-AT_RIGHT = 0
-AT_LEFT = AT_RIGHT + ROOM
-AT_DEALT = AT_LEFT + ROOM
+AT_PAIR = 0
+AT_NEXT = AT_PAIR + ROOM
+AT_DEALT = AT_NEXT + ROOM
 AT_HOME = AT_DEALT + ROOM
 AT_SHORT = AT_HOME + 2 * PAGE_HALF
 AT_SLOW_SOURCE = AT_SHORT + 1
@@ -113,20 +113,24 @@
         number, place = chunk_of(count)
         return (source + number) * 16 + place
 
+    sides = len(CHUNKS)
+    odd = chip & 1
+    right_side, left_side = sides * odd, sides * (1 - odd)
+
     for slot in range(ROOM):
-        table_ref[AT_RIGHT + slot] = local_code(high - 1 - slot)
-        table_ref[AT_LEFT + slot] = local_code(low + slot)
+        rightwards, leftwards = local_code(high - 1 - slot), local_code(low + slot)
+        table_ref[AT_PAIR + slot] = jnp.where(odd > 0, leftwards, rightwards)
+        table_ref[AT_NEXT + slot] = jnp.where(odd > 0, rightwards, leftwards)
         offset = turned(jnp.int32(slot), falls_here)
         rank = first + offset
-        code = jnp.where(rank < low, part_code(low - 1 - rank, 2), local_code(rank))
-        code = jnp.where(rank >= high, part_code(rank - high, 2 + len(CHUNKS)), code)
+        code = jnp.where(rank < low, part_code(low - 1 - rank, 2 + left_side), local_code(rank))
+        code = jnp.where(rank >= high, part_code(rank - high, 2 + right_side), code)
         table_ref[AT_DEALT + slot] = code
         node = jnp.int32(0)
         for place in range(1, chips):
             node = node + jnp.where(held[place] <= rank, 1, 0)
         table_ref[AT_SLOW_SOURCE + slot] = 2 * node + core
         table_ref[AT_SLOW_PLACE + slot] = offset
-    sides = len(CHUNKS)
     for half, (ranks_dealt, turns) in enumerate(((dealt, falls), (dealt_mate, falls_mate))):
         lane = core ^ half
         here, there = pick_at(ranks_dealt, chip), pick_at(ranks_dealt, chip + 1)
@@ -137,8 +141,8 @@
             at = half * PAGE_HALF + slot
             base = 3 * sides * half
             code = part_code(turned(rank - here, turns_here), base)
-            right = part_code(turned(rank - there, turns_right), base + sides)
-            left = part_code(turned(rank - before, turns_left), base + 2 * sides)
+            right = part_code(turned(rank - there, turns_right), base + sides + right_side)
+            left = part_code(turned(rank - before, turns_left), base + sides + left_side)
             code = jnp.where(rank >= there, right, code)
             table_ref[AT_HOME + at] = jnp.where(rank < here, left, code)
             node, start_there, turns_there = jnp.int32(0), jnp.int32(0), turns[0]
@@ -482,7 +486,9 @@
             pltpu.SemaphoreType.DMA((3,)),
         ],
         compiler_params=pltpu.CompilerParams(vmem_limit_bytes=28 * MIB),
-        cost_estimate=SMALL_COST,
+        cost_estimate=pl.CostEstimate(
+            flops=24 * total * width * span, bytes_accessed=6 * width * span, transcendentals=0
+        ),
         name="attend",
     )(own, other, rows_params, b_qkv, in_hbm(w_qkv), *after)
 
@@ -614,7 +620,7 @@
         ],
         compiler_params=pltpu.CompilerParams(vmem_limit_bytes=46 * MIB),
         cost_estimate=pl.CostEstimate(
-            flops=4 * total * width * (span + hidden),
+            flops=8 * total * width * (span + hidden),
             bytes_accessed=4 * width * (span + hidden),
             transcendentals=0,
         ),
@@ -762,17 +768,17 @@
     dp_size = lax.axis_size("dp")
     device = lax.axis_index("dp").astype(jnp.int32).reshape(1)
     mates = [(d, d ^ 1) for d in range(dp_size)]
-    rightwards = [(d, d + 2) for d in range(dp_size - 2)]
-    leftwards = [(d + 2, d) for d in range(dp_size - 2)]
+    pairs = [(d, d ^ 2) for d in range(dp_size)]
+    nexts = [(d, min(max(((d + 2) ^ 2) - 2, d & 1), dp_size - 2 + (d & 1))) for d in range(dp_size)]
 
     def to_mate(value):
         return lax.ppermute(value, "dp", mates)
 
-    def to_right(value):
-        return lax.ppermute(value, "dp", rightwards)
-
-    def to_left(value):
-        return lax.ppermute(value, "dp", leftwards)
+    def to_pair(value):
+        return lax.ppermute(value, "dp", pairs)
+
+    def to_next(value):
+        return lax.ppermute(value, "dp", nexts)
 
     mine, for_mate = pack(device, kept_count, keep_row, home)
     from_mate = to_mate(for_mate)
@@ -785,16 +791,16 @@
     short = short[0] > 0
 
     parts = tuple(zip(STARTS, CHUNKS))
-    sends = [(AT_RIGHT + at, size) for at, size in parts] + [(AT_LEFT + at, size) for at, size in parts]
+    sends = [(AT_PAIR + at, size) for at, size in parts] + [(AT_NEXT + at, size) for at, size in parts]
     going = choose(table, sends, [mine, from_mate], "send")
-    came_right = [to_right(value) for value in going[: len(parts)]]
-    came_left = [to_left(value) for value in going[len(parts) :]]
+    came_pair = [to_pair(value) for value in going[: len(parts)]]
+    came_next = [to_next(value) for value in going[len(parts) :]]
 
     def deal_fast(chunk, after):
-        right = [came_right[min(part, chunk)] for part in range(len(parts))]
-        left = [came_left[min(part, chunk)] for part in range(len(parts))]
+        came = [came_pair[min(part, chunk)] for part in range(len(parts))]
+        came = came + [came_next[min(part, chunk)] for part in range(len(parts))]
         at, size = parts[chunk]
-        sources = [mine, from_mate] + right + left
+        sources = [mine, from_mate] + came
         return choose(table, [(AT_DEALT + at, size)], sources, "deal_%d" % chunk, after)[0]
 
     def deal_slow(chunk):
@@ -833,22 +839,22 @@
         state_0 = start(deal(0), [])
         state_1 = start(deal(1), [])
         w_theirs = other_w_out(
-            w_out, w_near, [state_0[1], came_right[1], came_left[1]], [state_0[2], state_1[0]]
+            w_out, w_near, [state_0[0]], [state_0[2], state_1[0]]
         )
         weights = (w_out, w_theirs, w_up, w_down)
         done_0 = finish(state_0, [state_1[2]])
         done_1 = finish(state_1, [done_0[0]])
-        results, from_right, from_left = [], [], []
+        results, from_pair, from_next = [], [], []
         for done, beside in ((done_0, done_1[:1]), (done_1, ())):
-            results.append(add(*done, list(beside) + from_right[-1:] + from_left[-1:]))
-            from_right.append(to_left(results[-1]))
-            from_left.append(to_right(results[-1]))
+            results.append(add(*done, list(beside) + from_pair[-1:] + from_next[-1:]))
+            from_pair.append(to_pair(results[-1]))
+            from_next.append(to_next(results[-1]))
     else:
         results = [encode_split(deal(chunk), params) for chunk in range(len(parts))]
-        from_right = [to_left(value) for value in results]
-        from_left = [to_right(value) for value in results]
-
-    back = results + from_right + from_left
+        from_pair = [to_pair(value) for value in results]
+        from_next = [to_next(value) for value in results]
+
+    back = results + from_pair + from_next
     back = back + [to_mate(value) for value in back]
 
     def home_slow():

time: 227 us -> 209 us (0.921)
  waiting for transfers between devices: 76.7 us -> 59.5 us
    ppermute x7, waiting for transfers between devices: 36.2 us -> 26.4 us  [swap(): return lax.ppermute(value, 'tensor', [(0, 1), (1, 0)])]
    ppermute x8, waiting for transfers between devices: 32.6 us -> 24.1 us  [the longest x4 24 us: to_pair(): return lax.ppermute(value, 'dp', pairs)]
    ppermute x8, starting transfers between devices: 24.2 us -> 27.2 us  [the longest x4 13.9 us: to_pair(): return lax.ppermute(value, 'dp', pairs)]
  transfers between devices with their start and end apart: 25 -> 25, of which waited for: 14 -> 12; matrix products, arithmetic and copies ran while one was open for 0% -> 0% of each run, Pallas kernels for 32% -> 34%
where the time goes in v2:
time: 209 us; the launch traced here: 208 us
  Pallas kernels  91.8 us (44%)
  waiting for transfers between devices  59.5 us (28%)
  starting transfers between devices  40.8 us (20%)
  between operations  15.1 us (7%)
    pallas_call x2, Pallas kernels, mlp(): pl.pallas_call(functools.partial(mlp_kernel, len(after)), out_shape=(jax....  42.1 us
    ppermute x7, waiting for transfers between devices, swap(): return lax.ppermute(value, 'tensor', [(0, 1), (1, 0)])  26.4 us
    ppermute x4, waiting for transfers between devices, to_pair(): return lax.ppermute(value, 'dp', pairs)  24 us
    pallas_call x2, Pallas kernels, attend(): pl.pallas_call(functools.partial(attend_kernel, len(after)), out_shape=ja...  18.9 us
    ppermute x4, starting transfers between devices, to_pair(): return lax.ppermute(value, 'dp', pairs)  13.9 us
    ppermute x4, starting transfers between devices, to_next(): return lax.ppermute(value, 'dp', nexts)  13.3 us
    pallas_call x1, Pallas kernels, merge(): pl.pallas_call(functools.partial(merge_kernel, kept_count.shape[0], len(s...  10.2 us
    ppermute x7, starting transfers between devices, swap(): return lax.ppermute(value, 'tensor', [(0, 1), (1, 0)])  7.9 us
  transfers between devices with their start and end apart: 25, of which 12 were waited for; matrix products, arithmetic and copies ran while one was open for 0% of the time, Pallas kernels for 34%

profile of v2, /device:TPU:0, one launch (start us, length us, event | category | flops | bytes accessed | tf_op | source)
XLA Modules:
  0.0 208.2 jit_solution(3356785953132803966)
XLA Ops:
  6.5 5.5 %pack.1 = (bf16[8,64,1792]{2,1,0:T(8,128)(2,1)}, bf16[8,64,1792]{2,1,0:T(8,128)(2,1)S(1)}) custom-call(s32[1]{0:T(128)} %bitcast.19.device_ref, s32[8]{0:T(128)} %count_ref.5, s32[16]{0:T(128)} %bitcast.42, bf16[64,16,1792]{2,1,0:T(8,128)(2,1)} %bitcast.40), custom_call_target="tpu_custom_call" | custom-call | tf_op jit(solution)/shard_map/pack/pallas_call | solution.py:224
  12.5 2.0 plan.1.table_ref
  15.9 3.3 %send.1 = (bf16[3,64,1792]{2,1,0:T(8,128)(2,1)S(1)}, bf16[2,64,1792]{2,1,0:T(8,128)(2,1)}, bf16[3,64,1792]{2,1,0:T(8,128)(2,1)S(1)}, bf16[2,64,1792]{2,1,0:T(8,128)(2,1)}) custom-call(s32[94]{0:T(128)S(1)} %plan.1.table_ref, bf16[8,64,1792]{2,1,0:T(8,128)(2,1)} %get-tuple-element.91.refs_0_, bf16[8,64,1792]{2,1,0:T(8,128)(2,1)S(1)} %collective-permute-done.1.refs_1_), custom_call_target="tpu_custom_call" | custom-call | flops 1000 | bytes 1000 | tf_op jit(solution)/shard_map/send/pallas_call | solution.py:346
  19.2 1.5 collective-permute-start.3
  20.7 5.9 %collective-permute-start.2 = (bf16[3,64,1792]{2,1,0:T(8,128)(2,1)S(1)}, bf16[3,64,1792]{2,1,0:T(8,128)(2,1)}, u32[]{:S(2)}, u32[]{:S(2)}) collective-permute-start(bf16[3,64,1792]{2,1,0:T(8,128)(2,1)S(1)} %get-tuple-element.93.refs_0_), channel_id=1, source_target_pairs={{0,4},{2,6},{4,0},{6,2},{8,12},{10,14},{12,8},{14,10},{1,5},{3,7},... | collective-permute-start | bytes 2064392 | tf_op jit(solution)/shard_map/ppermute | solution.py:778
  27.9 1.6 collective-permute-start.6
  30.7 3.0 %collective-permute-start = (f32[1]{0:T(128)}, f32[1]{0:T(128)}, u32[]{:S(2)}, u32[]{:S(2)}) collective-permute-start(f32[1]{0:T(128)} %convert_element_type.12), channel_id=1, source_target_pairs={{0,16},{16,0},{1,17},{17,1},{2,18},{18,2},{3,19},{19,3},{4,20},{20... | collective-permute-start | bytes 20 | tf_op jit(solution)/shard_map/ppermute | solution.py:788
  34.9 6.4 %collective-permute-done.2 = bf16[3,64,1792]{2,1,0:T(8,128)(2,1)} collective-permute-done((bf16[3,64,1792]{2,1,0:T(8,128)(2,1)S(1)}, bf16[3,64,1792]{2,1,0:T(8,128)(2,1)}, u32[]{:S(2)}, u32[]{:S(2)}) %collective-permute-start.2) | collective-permute-done | bytes 688160 | tf_op jit(solution)/shard_map/ppermute | solution.py:778
  41.4 1.9 conditional.3
  41.4 1.9 deal_0.1
  43.3 1.6 collective-permute-start.4
  44.9 1.8 collective-permute-start.8
  46.7 5.0 %collective-permute-start.9 = (bf16[2,64,1792]{2,1,0:T(8,128)(2,1)}, bf16[2,64,1792]{2,1,0:T(8,128)(2,1)}, u32[]{:S(2)}, u32[]{:S(2)}) collective-permute-start(bf16[2,64,1792]{2,1,0:T(8,128)(2,1)} %get-tuple-element.96), channel_id=1, source_target_pairs={{0,0},{2,2},{4,8},{6,10},{8,4},{10,6},{12,12},{14,14},{1,1},{3,3},... | collective-permute-start | bytes 1376264 | tf_op jit(solution)/shard_map/ppermute | solution.py:781
  52.0 4.2 %collective-permute-done.8 = bf16[2,64,1792]{2,1,0:T(8,128)(2,1)} collective-permute-done((bf16[2,64,1792]{2,1,0:T(8,128)(2,1)}, bf16[2,64,1792]{2,1,0:T(8,128)(2,1)}, u32[]{:S(2)}, u32[]{:S(2)}) %collective-permute-start.8) | collective-permute-done | bytes 458784 | tf_op jit(solution)/shard_map/ppermute | solution.py:778
  56.2 2.6 %conditional.4 = (bf16[2,64,1792]{2,1,0:T(8,128)(2,1)}) conditional(s32[]{:T(128)} %bitcast.22, (s32[94]{0:T(128)S(1)}, bf16[8,64,1792]{2,1,0:T(8,128)(2,1)}, bf16[8,64,1792]{2,1,0:T(8,128)(2,1)}, bf16[3,64,1792]{2,1,0:T(8,128)(2,1)}, bf16[2,64,1792]{2,1,0:T(8,128)(2,1)}, /*index=5*/bf16[3,64,1792]{2,1,0:T(8,128)(2,1)}, ...), branch_computations={%region_2.0_spmd, %region_3.0_spmd} | conditional | flops 230388 | bytes 61474012 | solution.py:821
  56.2 2.4 %deal_1.1 = bf16[2,64,1792]{2,1,0:T(8,128)(2,1)} custom-call(s32[94]{0:T(128)S(1)} %get-tuple-element.66.table_ref, bf16[8,64,1792]{2,1,0:T(8,128)(2,1)} %get-tuple-element.67.refs_0_, bf16[8,64,1792]{2,1,0:T(8,128)(2,1)} %get-tuple-element.68.refs_1_, bf16[3,64,1792]{2,1,0:T(8,128)(2,1)} %get-tuple-element.69.refs_2_, ...), custom_call_target="tpu_custom_call" | custom-call | flops 1000 | bytes 1000 | tf_op jit(solution)/shard_map/cond/branch_0_fun/deal_1/pallas_call | solution.py:346
  61.3 10.2 %attend.2.refs_2_.mine_ref = bf16[2,3,64,896]{3,2,1,0:T(8,128)(2,1)S(1)} custom-call(bf16[3,64,1792]{2,1,0:T(8,128)(2,1)S(1)} %get-tuple-element.130.own_ref.refs_1_, bf16[3,64,1792]{2,1,0:T(8,128)(2,1)S(1)} %collective-permute-done.4.other_ref, f32[6,1792]{1,0:T(8,128)S(1)} %stack.48.rows_ref, f32[3,896]{1,0:T(4,128)S(1)} %copy-done.6, ...), custom_call_target="tpu_custom_call" | custom-call | flops 14797504512 | bytes 9633792 | tf_op jit(solution)/shard_map/attend/pallas_call | solution.py:477
  71.5 5.0 %collective-permute-done.7 = bf16[1,224,1792]{2,1,0:T(8,128)(2,1)S(1)} collective-permute-done((bf16[1,224,1792]{2,1,0:T(8,128)(2,1)S(1)}, bf16[1,224,1792]{2,1,0:T(8,128)(2,1)S(1)}, u32[]{:S(2)}, u32[]{:S(2)}) %collective-permute-start.7) | collective-permute-done | bytes 802848 | tf_op jit(solution)/shard_map/ppermute | solution.py:717
  78.5 1.5 collective-permute-start.5
  80.0 11.5 %collective-permute-done.11.other_ref = bf16[2,64,1792]{2,1,0:T(8,128)(2,1)} collective-permute-done((bf16[2,64,1792]{2,1,0:T(8,128)(2,1)}, bf16[2,64,1792]{2,1,0:T(8,128)(2,1)}, u32[]{:S(2)}, u32[]{:S(2)}) %collective-permute-start.11) | collective-permute-done | bytes 458784 | tf_op jit(solution)/shard_map/ppermute | solution.py:653
  91.5 8.8 %attend.3.refs_0_.mine_ref = bf16[2,2,64,896]{3,2,1,0:T(8,128)(2,1)S(1)} custom-call(bf16[2,64,1792]{2,1,0:T(8,128)(2,1)} %get-tuple-element.131.refs_3_.own_ref, bf16[2,64,1792]{2,1,0:T(8,128)(2,1)} %collective-permute-done.11.other_ref, f32[6,1792]{1,0:T(8,128)S(1)} %stack.48.rows_ref, f32[3,896]{1,0:T(4,128)S(1)} %copy-done.6, bf16[3,1792,896]{2,1,0:T(8,128)(2,1)} %w_ref.5), custom_call_target="tpu_custom_call" | custom-call | flops 9865003008 | bytes 9633792 | tf_op jit(solution)/shard_map/attend/pallas_call | solution.py:477
  101.8 4.4 %collective-permute-done.5.theirs_ref = bf16[2,3,64,896]{3,2,1,0:T(8,128)(2,1)S(1)} collective-permute-done((bf16[2,3,64,896]{3,2,1,0:T(8,128)(2,1)}, bf16[2,3,64,896]{3,2,1,0:T(8,128)(2,1)S(1)}, u32[]{:S(2)}, u32[]{:S(2)}) %collective-permute-start.5) | collective-permute-done | bytes 688160 | tf_op jit(solution)/shard_map/ppermute | solution.py:653
  106.2 23.5 %mlp.2 = (f32[3,64,1792]{2,1,0:T(8,128)S(1)}, bf16[3,64,1792]{2,1,0:T(8,128)(2,1)S(1)}) custom-call(bf16[3,64,1792]{2,1,0:T(8,128)(2,1)S(1)} %copy-done.11, bf16[3,64,1792]{2,1,0:T(8,128)(2,1)S(1)} %copy-done.5, bf16[2,3,64,896]{3,2,1,0:T(8,128)(2,1)S(1)} %copy-done.3, bf16[2,3,64,896]{3,2,1,0:T(8,128)(2,1)S(1)} %collective-permute-done.5.theirs_ref, ...), custom_call_target="tpu_custom_call" | custom-call | flops 30299652096 | bytes 39452672 | tf_op jit(solution)/shard_map/mlp/pallas_call | solution.py:602
  130.3 18.6 %mlp.3 = (f32[2,64,1792]{2,1,0:T(8,128)S(1)}, bf16[2,64,1792]{2,1,0:T(8,128)(2,1)S(1)}) custom-call(bf16[2,64,1792]{2,1,0:T(8,128)(2,1)} %get-tuple-element.131.refs_3_.own_ref, bf16[2,64,1792]{2,1,0:T(8,128)(2,1)} %collective-permute-done.11.other_ref, bf16[2,2,64,896]{3,2,1,0:T(8,128)(2,1)S(1)} %attend.3.refs_0_.mine_ref, ...), custom_call_target="tpu_custom_call" | custom-call | flops 20199768064 | bytes 39452672 | tf_op jit(solution)/shard_map/mlp/pallas_call | solution.py:602
  149.9 1.7 collective-permute-start.16
  151.7 6.2 %collective-permute-start.15 = (bf16[3,64,1792]{2,1,0:T(8,128)(2,1)}, bf16[3,64,1792]{2,1,0:T(8,128)(2,1)S(1)}, u32[]{:S(2)}, u32[]{:S(2)}) collective-permute-start(bf16[3,64,1792]{2,1,0:T(8,128)(2,1)} %add.61.refs_0_), channel_id=1, source_target_pairs={{0,4},{2,6},{4,0},{6,2},{8,12},{10,14},{12,8},{14,10},{1,5},{3,7},... | collective-permute-start | bytes 2064392 | tf_op jit(solution)/shard_map/ppermute | solution.py:778
  159.3 9.3 %collective-permute-done.14.came_ref = bf16[2,64,1792]{2,1,0:T(8,128)(2,1)S(1)} collective-permute-done((bf16[2,64,1792]{2,1,0:T(8,128)(2,1)S(1)}, bf16[2,64,1792]{2,1,0:T(8,128)(2,1)S(1)}, u32[]{:S(2)}, u32[]{:S(2)}) %collective-permute-start.14) | collective-permute-done | bytes 458784 | tf_op jit(solution)/shard_map/ppermute | solution.py:653
  168.6 3.7 %collective-permute-done.15.refs_0_.refs_2_ = bf16[3,64,1792]{2,1,0:T(8,128)(2,1)S(1)} collective-permute-done((bf16[3,64,1792]{2,1,0:T(8,128)(2,1)}, bf16[3,64,1792]{2,1,0:T(8,128)(2,1)S(1)}, u32[]{:S(2)}, u32[]{:S(2)}) %collective-permute-start.15) | collective-permute-done | bytes 688160 | tf_op jit(solution)/shard_map/ppermute | solution.py:778
  173.2 5.0 %collective-permute-start.18 = (bf16[2,64,1792]{2,1,0:T(8,128)(2,1)}, bf16[2,64,1792]{2,1,0:T(8,128)(2,1)}, u32[]{:S(2)}, u32[]{:S(2)}) collective-permute-start(bf16[2,64,1792]{2,1,0:T(8,128)(2,1)} %add.62.refs_1_), channel_id=1, source_target_pairs={{0,0},{2,2},{4,8},{6,10},{8,4},{10,6},{12,12},{14,14},{1,1},{3,3},... | collective-permute-start | bytes 1376264 | tf_op jit(solution)/shard_map/ppermute | solution.py:781
  179.2 9.7 %collective-permute-done.17.refs_3_ = bf16[2,64,1792]{2,1,0:T(8,128)(2,1)} collective-permute-done((bf16[2,64,1792]{2,1,0:T(8,128)(2,1)}, bf16[2,64,1792]{2,1,0:T(8,128)(2,1)}, u32[]{:S(2)}, u32[]{:S(2)}) %collective-permute-start.17) | collective-permute-done | bytes 458784 | tf_op jit(solution)/shard_map/ppermute | solution.py:778
  189.0 2.1 %collective-permute-done.22.refs_9_ = bf16[2,64,1792]{2,1,0:T(8,128)(2,1)} collective-permute-done((bf16[2,64,1792]{2,1,0:T(8,128)(2,1)}, bf16[2,64,1792]{2,1,0:T(8,128)(2,1)}, u32[]{:S(2)}, u32[]{:S(2)}) %collective-permute-start.22) | collective-permute-done | bytes 458784 | tf_op jit(solution)/shard_map/ppermute | solution.py:775
  191.1 10.2 %merge.1 = bf16[64,16,1792]{2,1,0:T(8,128)(2,1)} custom-call(s32[1]{0:T(128)} %bitcast.19.device_ref, s32[8]{0:T(128)} %count_ref.5, s32[16]{0:T(128)} %bitcast.43, s32[94]{0:T(128)S(1)} %plan.1.table_ref, s32[1]{0:T(128)} %convert_element_type.13.slow_ref, bf16[64,16,1792]{2,1,0:T(8,128)(2,1)} %bitcast.41, bf16[3,64,1792]{2,1,0:T(8,128)(2,1)} %add.61.refs_0_, ...), custom_call_target="tpu_custom_call" | custom-call | flops 1000 | bytes 1000 | tf_op jit(solution)/shard_map/merge/pallas_call | solution.py:289
  (79 shorter events, 15.4 us)
Async XLA Ops:
  12.0 3.9 %collective-permute-start.1 = (bf16[8,64,1792]{2,1,0:T(8,128)(2,1)S(1)}, bf16[8,64,1792]{2,1,0:T(8,128)(2,1)S(1)}, u32[]{:S(2)}, u32[]{:S(2)}) collective-permute-start(bf16[8,64,1792]{2,1,0:T(8,128)(2,1)S(1)} %get-tuple-element.92), channel_id=1, source_target_pairs={{0,2},{2,0},{4,6},{6,4},{8,10},{10,8},{12,14},{14,12},{1,3},{3,1},... | collective-permute-start | bytes 5505032 | tf_op jit(solution)/shard_map/ppermute | solution.py:775
  19.2 15.7 %collective-permute-start.3 = (bf16[3,64,1792]{2,1,0:T(8,128)(2,1)S(1)}, bf16[3,64,1792]{2,1,0:T(8,128)(2,1)}, u32[]{:S(2)}, u32[]{:S(2)}) collective-permute-start(bf16[3,64,1792]{2,1,0:T(8,128)(2,1)S(1)} %get-tuple-element.94), channel_id=1, source_target_pairs={{0,0},{2,2},{4,8},{6,10},{8,4},{10,6},{12,12},{14,14},{1,1},{3,3},... | collective-permute-start | bytes 2064392 | tf_op jit(solution)/shard_map/ppermute | solution.py:781
  20.7 20.7 %collective-permute-start.2 = (bf16[3,64,1792]{2,1,0:T(8,128)(2,1)S(1)}, bf16[3,64,1792]{2,1,0:T(8,128)(2,1)}, u32[]{:S(2)}, u32[]{:S(2)}) collective-permute-start(bf16[3,64,1792]{2,1,0:T(8,128)(2,1)S(1)} %get-tuple-element.93.refs_0_), channel_id=1, source_target_pairs={{0,4},{2,6},{4,0},{6,2},{8,12},{10,14},{12,8},{14,10},{1,5},{3,7},... | collective-permute-start | bytes 2064392 | tf_op jit(solution)/shard_map/ppermute | solution.py:778
  26.6 14.8 %copy-start.8 = (bf16[8,64,1792]{2,1,0:T(8,128)(2,1)S(1)}, bf16[8,64,1792]{2,1,0:T(8,128)(2,1)}, u32[]{:S(2)}) copy-start(bf16[8,64,1792]{2,1,0:T(8,128)(2,1)} %copy-done.7) | copy-start | bytes 5505028
  27.9 30.9 %collective-permute-start.6 = (bf16[224,1792]{1,0:T(8,128)(2,1)S(1)}, bf16[224,1792]{1,0:T(8,128)(2,1)S(1)}, u32[]{:S(2)}, u32[]{:S(2)}) collective-permute-start(bf16[224,1792]{1,0:T(8,128)(2,1)S(1)} %w_piece.1), channel_id=1, source_target_pairs={{0,1},{1,0},{2,3},{3,2},{4,5},{5,4},{6,7},{7,6},{8,9},{9,8},{10,11... | collective-permute-start | bytes 2408456 | tf_op jit(solution)/shard_map/ppermute | solution.py:653
  30.7 3.6 %collective-permute-start = (f32[1]{0:T(128)}, f32[1]{0:T(128)}, u32[]{:S(2)}, u32[]{:S(2)}) collective-permute-start(f32[1]{0:T(128)} %convert_element_type.12), channel_id=1, source_target_pairs={{0,16},{16,0},{1,17},{17,1},{2,18},{18,2},{3,19},{19,3},{4,20},{20... | collective-permute-start | bytes 20 | tf_op jit(solution)/shard_map/ppermute | solution.py:788
  41.4 10.4 %copy-start.14 = (f32[1792]{0:T(1024)S(1)}, f32[1792]{0:T(1024)}, u32[]{:S(2)}) copy-start(f32[1792]{0:T(1024)} %param.27) | copy-start | bytes 21508
  41.4 10.4 %copy-start.15 = (f32[1792]{0:T(1024)S(1)}, f32[1792]{0:T(1024)}, u32[]{:S(2)}) copy-start(f32[1792]{0:T(1024)} %param.31) | copy-start | bytes 21508
  41.4 10.4 %copy-start.16 = (f32[1792]{0:T(1024)S(1)}, f32[1792]{0:T(1024)}, u32[]{:S(2)}) copy-start(f32[1792]{0:T(1024)} %param.32) | copy-start | bytes 21508
  41.4 10.4 %copy-start.17 = (f32[1792]{0:T(1024)S(1)}, f32[1792]{0:T(1024)}, u32[]{:S(2)}) copy-start(f32[1792]{0:T(1024)} %param.33) | copy-start | bytes 21508
  41.4 10.4 %copy-start.18 = (f32[1792]{0:T(1024)S(1)}, f32[1792]{0:T(1024)}, u32[]{:S(2)}) copy-start(f32[1792]{0:T(1024)} %param.37) | copy-start | bytes 21508
  43.3 18.0 %copy-start.10 = (bf16[3,64,1792]{2,1,0:T(8,128)(2,1)}, bf16[3,64,1792]{2,1,0:T(8,128)(2,1)S(1)}, u32[]{:S(2)}) copy-start(bf16[3,64,1792]{2,1,0:T(8,128)(2,1)S(1)} %get-tuple-element.130.own_ref.refs_1_) | copy-start | bytes 2064388
  43.3 18.0 %collective-permute-start.4 = (bf16[3,64,1792]{2,1,0:T(8,128)(2,1)S(1)}, bf16[3,64,1792]{2,1,0:T(8,128)(2,1)S(1)}, u32[]{:S(2)}, u32[]{:S(2)}) collective-permute-start(bf16[3,64,1792]{2,1,0:T(8,128)(2,1)S(1)} %get-tuple-element.130.own_ref.refs_1_), channel_id=1, source_target_pairs={{0,1},{1,0},{2,3},{3,2},{4,5},{5,4},{6,7},{7,6},{8,9},{9,8},{10,11... | collective-permute-start | bytes 2064392 | tf_op jit(solution)/shard_map/ppermute | solution.py:653
  44.9 11.3 %collective-permute-start.8 = (bf16[2,64,1792]{2,1,0:T(8,128)(2,1)}, bf16[2,64,1792]{2,1,0:T(8,128)(2,1)}, u32[]{:S(2)}, u32[]{:S(2)}) collective-permute-start(bf16[2,64,1792]{2,1,0:T(8,128)(2,1)} %get-tuple-element.95), channel_id=1, source_target_pairs={{0,4},{2,6},{4,0},{6,2},{8,12},{10,14},{12,8},{14,10},{1,5},{3,7},... | collective-permute-start | bytes 1376264 | tf_op jit(solution)/shard_map/ppermute | solution.py:778
  46.7 9.5 %collective-permute-start.9 = (bf16[2,64,1792]{2,1,0:T(8,128)(2,1)}, bf16[2,64,1792]{2,1,0:T(8,128)(2,1)}, u32[]{:S(2)}, u32[]{:S(2)}) collective-permute-start(bf16[2,64,1792]{2,1,0:T(8,128)(2,1)} %get-tuple-element.96), channel_id=1, source_target_pairs={{0,0},{2,2},{4,8},{6,10},{8,4},{10,6},{12,12},{14,14},{1,1},{3,3},... | collective-permute-start | bytes 1376264 | tf_op jit(solution)/shard_map/ppermute | solution.py:781
  58.9 17.5 %collective-permute-start.7 = (bf16[1,224,1792]{2,1,0:T(8,128)(2,1)S(1)}, bf16[1,224,1792]{2,1,0:T(8,128)(2,1)S(1)}, u32[]{:S(2)}, u32[]{:S(2)}) collective-permute-start(bf16[1,224,1792]{2,1,0:T(8,128)(2,1)S(1)} %w_near.1), channel_id=1, source_target_pairs={{0,16},{16,0},{1,17},{17,1},{2,18},{18,2},{3,19},{19,3},{4,20},{20... | collective-permute-start | bytes 2408456 | tf_op jit(solution)/shard_map/ppermute | solution.py:717
  77.8 23.2 %collective-permute-start.10 = (bf16[2,224,1792]{2,1,0:T(8,128)(2,1)}, bf16[2,224,1792]{2,1,0:T(8,128)(2,1)S(1)}, u32[]{:S(2)}, u32[]{:S(2)}) collective-permute-start(bf16[2,224,1792]{2,1,0:T(8,128)(2,1)} %w_both.1), channel_id=1, source_target_pairs={{0,2},{2,0},{4,6},{6,4},{8,10},{10,8},{12,14},{14,12},{1,3},{3,1},... | collective-permute-start | bytes 4816904 | tf_op jit(solution)/shard_map/ppermute | solution.py:719
  77.8 13.7 %collective-permute-start.11 = (bf16[2,64,1792]{2,1,0:T(8,128)(2,1)}, bf16[2,64,1792]{2,1,0:T(8,128)(2,1)}, u32[]{:S(2)}, u32[]{:S(2)}) collective-permute-start(bf16[2,64,1792]{2,1,0:T(8,128)(2,1)} %get-tuple-element.131.refs_3_.own_ref), channel_id=1, source_target_pairs={{0,1},{1,0},{2,3},{3,2},{4,5},{5,4},{6,7},{7,6},{8,9},{9,8},{10,11... | collective-permute-start | bytes 1376264 | tf_op jit(solution)/shard_map/ppermute | solution.py:653
  78.5 27.6 %collective-permute-start.5 = (bf16[2,3,64,896]{3,2,1,0:T(8,128)(2,1)}, bf16[2,3,64,896]{3,2,1,0:T(8,128)(2,1)S(1)}, u32[]{:S(2)}, u32[]{:S(2)}) collective-permute-start(bf16[2,3,64,896]{3,2,1,0:T(8,128)(2,1)} %copy-done.2), channel_id=1, source_target_pairs={{0,1},{1,0},{2,3},{3,2},{4,5},{5,4},{6,7},{7,6},{8,9},{9,8},{10,11... | collective-permute-start | bytes 2064392 | tf_op jit(solution)/shard_map/ppermute | solution.py:653
  100.3 30.0 %collective-permute-start.13 = (bf16[2,2,64,896]{3,2,1,0:T(8,128)(2,1)S(1)}, bf16[2,2,64,896]{3,2,1,0:T(8,128)(2,1)S(1)}, u32[]{:S(2)}, u32[]{:S(2)}) collective-permute-start(bf16[2,2,64,896]{3,2,1,0:T(8,128)(2,1)S(1)} %attend.3.refs_0_.mine_ref), channel_id=1, source_target_pairs={{0,1},{1,0},{2,3},{3,2},{4,5},{5,4},{6,7},{7,6},{8,9},{9,8},{10,11... | collective-permute-start | bytes 1376264 | tf_op jit(solution)/shard_map/ppermute | solution.py:653
  129.7 19.2 %collective-permute-start.12 = (bf16[3,64,1792]{2,1,0:T(8,128)(2,1)S(1)}, bf16[3,64,1792]{2,1,0:T(8,128)(2,1)S(1)}, u32[]{:S(2)}, u32[]{:S(2)}) collective-permute-start(bf16[3,64,1792]{2,1,0:T(8,128)(2,1)S(1)} %get-tuple-element.98), channel_id=1, source_target_pairs={{0,1},{1,0},{2,3},{3,2},{4,5},{5,4},{6,7},{7,6},{8,9},{9,8},{10,11... | collective-permute-start | bytes 2064392 | tf_op jit(solution)/shard_map/ppermute | solution.py:653
  149.9 18.7 %collective-permute-start.16 = (bf16[3,64,1792]{2,1,0:T(8,128)(2,1)}, bf16[3,64,1792]{2,1,0:T(8,128)(2,1)S(1)}, u32[]{:S(2)}, u32[]{:S(2)}) collective-permute-start(bf16[3,64,1792]{2,1,0:T(8,128)(2,1)} %add.61.refs_0_), channel_id=1, source_target_pairs={{0,0},{2,2},{4,8},{6,10},{8,4},{10,6},{12,12},{14,14},{1,1},{3,3},... | collective-permute-start | bytes 2064392 | tf_op jit(solution)/shard_map/ppermute | solution.py:781
  151.7 20.6 %collective-permute-start.15 = (bf16[3,64,1792]{2,1,0:T(8,128)(2,1)}, bf16[3,64,1792]{2,1,0:T(8,128)(2,1)S(1)}, u32[]{:S(2)}, u32[]{:S(2)}) collective-permute-start(bf16[3,64,1792]{2,1,0:T(8,128)(2,1)} %add.61.refs_0_), channel_id=1, source_target_pairs={{0,4},{2,6},{4,0},{6,2},{8,12},{10,14},{12,8},{14,10},{1,5},{3,7},... | collective-permute-start | bytes 2064392 | tf_op jit(solution)/shard_map/ppermute | solution.py:778
  157.8 10.8 %collective-permute-start.14 = (bf16[2,64,1792]{2,1,0:T(8,128)(2,1)S(1)}, bf16[2,64,1792]{2,1,0:T(8,128)(2,1)S(1)}, u32[]{:S(2)}, u32[]{:S(2)}) collective-permute-start(bf16[2,64,1792]{2,1,0:T(8,128)(2,1)S(1)} %get-tuple-element.100), channel_id=1, source_target_pairs={{0,1},{1,0},{2,3},{3,2},{4,5},{5,4},{6,7},{7,6},{8,9},{9,8},{10,11... | collective-permute-start | bytes 1376264 | tf_op jit(solution)/shard_map/ppermute | solution.py:653
  159.3 19.4 %collective-permute-start.19 = (bf16[3,64,1792]{2,1,0:T(8,128)(2,1)}, bf16[3,64,1792]{2,1,0:T(8,128)(2,1)S(1)}, u32[]{:S(2)}, u32[]{:S(2)}) collective-permute-start(bf16[3,64,1792]{2,1,0:T(8,128)(2,1)} %add.61.refs_0_), channel_id=1, source_target_pairs={{0,2},{2,0},{4,6},{6,4},{8,10},{10,8},{12,14},{14,12},{1,3},{3,1},... | collective-permute-start | bytes 2064392 | tf_op jit(solution)/shard_map/ppermute | solution.py:775
  173.2 5.6 %collective-permute-start.18 = (bf16[2,64,1792]{2,1,0:T(8,128)(2,1)}, bf16[2,64,1792]{2,1,0:T(8,128)(2,1)}, u32[]{:S(2)}, u32[]{:S(2)}) collective-permute-start(bf16[2,64,1792]{2,1,0:T(8,128)(2,1)} %add.62.refs_1_), channel_id=1, source_target_pairs={{0,0},{2,2},{4,8},{6,10},{8,4},{10,6},{12,12},{14,14},{1,1},{3,3},... | collective-permute-start | bytes 1376264 | tf_op jit(solution)/shard_map/ppermute | solution.py:781
  178.2 10.7 %collective-permute-start.17 = (bf16[2,64,1792]{2,1,0:T(8,128)(2,1)}, bf16[2,64,1792]{2,1,0:T(8,128)(2,1)}, u32[]{:S(2)}, u32[]{:S(2)}) collective-permute-start(bf16[2,64,1792]{2,1,0:T(8,128)(2,1)} %add.62.refs_1_), channel_id=1, source_target_pairs={{0,4},{2,6},{4,0},{6,2},{8,12},{10,14},{12,8},{14,10},{1,5},{3,7},... | collective-permute-start | bytes 1376264 | tf_op jit(solution)/shard_map/ppermute | solution.py:778
  178.2 10.8 %collective-permute-start.23 = (bf16[3,64,1792]{2,1,0:T(8,128)(2,1)S(1)}, bf16[3,64,1792]{2,1,0:T(8,128)(2,1)S(1)}, u32[]{:S(2)}, u32[]{:S(2)}) collective-permute-start(bf16[3,64,1792]{2,1,0:T(8,128)(2,1)S(1)} %collective-permute-done.16.refs_1_.refs_4_), channel_id=1, source_target_pairs={{0,2},{2,0},{4,6},{6,4},{8,10},{10,8},{12,14},{14,12},{1,3},{3,1},... | collective-permute-start | bytes 2064392 | tf_op jit(solution)/shard_map/ppermute | solution.py:775
  178.2 10.8 %collective-permute-start.21 = (bf16[3,64,1792]{2,1,0:T(8,128)(2,1)S(1)}, bf16[3,64,1792]{2,1,0:T(8,128)(2,1)S(1)}, u32[]{:S(2)}, u32[]{:S(2)}) collective-permute-start(bf16[3,64,1792]{2,1,0:T(8,128)(2,1)S(1)} %collective-permute-done.15.refs_0_.refs_2_), channel_id=1, source_target_pairs={{0,2},{2,0},{4,6},{6,4},{8,10},{10,8},{12,14},{14,12},{1,3},{3,1},... | collective-permute-start | bytes 2064392 | tf_op jit(solution)/shard_map/ppermute | solution.py:775
  178.7 10.2 %collective-permute-start.20 = (bf16[2,64,1792]{2,1,0:T(8,128)(2,1)}, bf16[2,64,1792]{2,1,0:T(8,128)(2,1)}, u32[]{:S(2)}, u32[]{:S(2)}) collective-permute-start(bf16[2,64,1792]{2,1,0:T(8,128)(2,1)} %add.62.refs_1_), channel_id=1, source_target_pairs={{0,2},{2,0},{4,6},{6,4},{8,10},{10,8},{12,14},{14,12},{1,3},{3,1},... | collective-permute-start | bytes 1376264 | tf_op jit(solution)/shard_map/ppermute | solution.py:775
  178.8 10.2 %collective-permute-start.24 = (bf16[2,64,1792]{2,1,0:T(8,128)(2,1)}, bf16[2,64,1792]{2,1,0:T(8,128)(2,1)}, u32[]{:S(2)}, u32[]{:S(2)}) collective-permute-start(bf16[2,64,1792]{2,1,0:T(8,128)(2,1)} %collective-permute-done.18.refs_5_), channel_id=1, source_target_pairs={{0,2},{2,0},{4,6},{6,4},{8,10},{10,8},{12,14},{14,12},{1,3},{3,1},... | collective-permute-start | bytes 1376264 | tf_op jit(solution)/shard_map/ppermute | solution.py:775
  188.9 2.2 %collective-permute-start.22 = (bf16[2,64,1792]{2,1,0:T(8,128)(2,1)}, bf16[2,64,1792]{2,1,0:T(8,128)(2,1)}, u32[]{:S(2)}, u32[]{:S(2)}) collective-permute-start(bf16[2,64,1792]{2,1,0:T(8,128)(2,1)} %collective-permute-done.17.refs_3_), channel_id=1, source_target_pairs={{0,2},{2,0},{4,6},{6,4},{8,10},{10,8},{12,14},{14,12},{1,3},{3,1},... | collective-permute-start | bytes 1376264 | tf_op jit(solution)/shard_map/ppermute | solution.py:775
  (9 other events, 52.4 us)

commit v3 on v2

--- a/solution.py
+++ b/solution.py
@@ -251,6 +251,7 @@
         start_copies(
             sources,
             [(table_ref[at + slot], landed.at[slot], sems.at[slot]) for slot in range(slots)],
+            landed.shape[1] // GROUP_ROWS,
         )
 
     blocks = kept_blocks_once(device_ref, count_ref, keep_ref, pages, held)
@@ -269,17 +270,19 @@
         (row // page_blocks == column % GROUP_ROWS) & (row % page_blocks == wanted), 1.0, 0.0
     ).astype(BF16)
 
-    @pl.when(step == 0)
-    def _():
-        for slot in range(slots):
-            pltpu.make_async_copy(sources[0].at[0], landed.at[slot], sems.at[slot]).wait()
-
+    same = lax.broadcasted_iota(jnp.int32, (span, span), 0) == lax.broadcasted_iota(
+        jnp.int32, (span, span), 1
+    )
+    stays = jnp.where(same & (kept == 0), 1.0, 0.0).astype(BF16)
     rows = pl.ds(pl.multiple_of(step * GROUP_ROWS, GROUP_ROWS), GROUP_ROWS)
+    for slot in range(slots):
+        pltpu.make_async_copy(
+            sources[0].at[0, rows, :], landed.at[slot, rows, :], sems.at[slot, step]
+        ).wait()
     source = landed[:, rows, :].reshape(depth, width)
     result = jnp.dot(chosen, source, preferred_element_type=F32)
-    home = home_ref[...].reshape(span, width).astype(F32)
-    merged = jnp.where(kept > 0, result, home).astype(BF16)
-    out_ref[...] = merged.reshape(GROUP_ROWS, page_blocks, width)
+    result += jnp.dot(stays, home_ref[...].reshape(span, width), preferred_element_type=F32)
+    out_ref[...] = result.astype(BF16).reshape(GROUP_ROWS, page_blocks, width)
 
 
 def merge(device, kept_count, keep_row, table, slow, home, sources):
@@ -297,7 +300,7 @@
             scratch_shapes=[
                 pltpu.SMEM((slots,), jnp.int32),
                 pltpu.VMEM((slots, rows, width), BF16),
-                pltpu.SemaphoreType.DMA((slots,)),
+                pltpu.SemaphoreType.DMA((slots, rows // GROUP_ROWS)),
             ],
         ),
         compiler_params=pltpu.CompilerParams(vmem_limit_bytes=20 * MIB),
@@ -306,7 +309,7 @@
     )(device, kept_count, keep_row, table, slow, home, *sources)
 
 
-def start_copies(sources, wanted):
+def start_copies(sources, wanted, groups=0):
     for code, target, sem in wanted:
         which, place = code >> 4, code & 15
         for index, source in enumerate(sources):
@@ -322,7 +325,15 @@
             @pl.when(here)
             def _(source=source, place=place, target=target, sem=sem):
                 inside = jnp.minimum(place, source.shape[0] - 1)
-                pltpu.make_async_copy(source.at[inside], target, sem).start()
+                if groups == 0:
+                    pltpu.make_async_copy(source.at[inside], target, sem).start()
+                    return
+                size = source.shape[1] // groups
+                for group in range(groups):
+                    rows = pl.ds(group * size, size)
+                    pltpu.make_async_copy(
+                        source.at[inside, rows, :], target.at[rows, :], sem.at[group]
+                    ).start()
 
 
 def choose_kernel(parts, n_sources, table_ref, *refs):
@@ -523,8 +534,7 @@
     ]
     for load in out_loads:
         load.start()
-    for slot in range(SLOTS):
-        load_up(jnp.int32(slot)).start()
+    load_up(jnp.int32(0)).start()
     gain, shift = rows_ref[2:3, :], rows_ref[3:4, :]
     mine = mine_ref[...].reshape(2 * half, span)
     theirs = jnp.concatenate(
@@ -532,6 +542,8 @@
     )
     for number, attended in enumerate((mine, theirs)):
         out_loads[number].wait()
+        for slot in (range(1, 3), range(3, SLOTS))[number]:
+            load_up(jnp.int32(slot)).start()
         for column in range(0, width, DOWN_TILE):
             columns = slice(column, column + DOWN_TILE)
             part = jnp.dot(attended, outs[number, :, columns], preferred_element_type=F32)
@@ -710,12 +722,10 @@
     )(number.astype(jnp.int32).reshape(1), in_hbm(w_out), *after)
 
 
-def other_w_out(w_out, near, early, late):
+def other_w_out(w_out, near, side, after):
     number, other, _ = w_out_place(w_out)
     dp_size = lax.axis_size("dp")
-    sent = line_up([near], early, "w_near")
-    side = lax.ppermute(sent, "groups", [(0, 1), (1, 0)])[0]
-    both = line_up([near, side], late, "w_both")
+    both = line_up([near, side], after, "w_both")
     mate = lax.ppermute(both, "dp", [(d, d ^ 1) for d in range(dp_size)])
     spots = jnp.stack([number, other, number ^ 1, other ^ 1]).astype(jnp.int32)
     return join(spots, near, side, mate)
@@ -825,7 +835,7 @@
          b_down) = params
         rows_params = jnp.stack([pre_gain, pre_shift, mlp_gain, mlp_shift, b_out, b_down])
         b_up = b_up.reshape(1, -1)
-        w_near = swap(w_out_piece(w_out, [going[0]]))
+        w_near = swap(w_out_piece(w_out, [for_mate]))
 
         def start(own, after):
             other = swap(own)
@@ -836,11 +846,13 @@
             keep, send = mlp(*state, rows_params, b_up, weights, after)
             return keep, swap(send)
 
-        state_0 = start(deal(0), [])
-        state_1 = start(deal(1), [])
-        w_theirs = other_w_out(
-            w_out, w_near, [state_0[0]], [state_0[2], state_1[0]]
-        )
+        blocks_0 = deal(0)
+        state_0 = start(blocks_0, [])
+        w_sent = line_up([w_near], [blocks_0], "w_near")
+        blocks_1 = deal(1, [w_sent])
+        state_1 = start(blocks_1, [])
+        w_side = lax.ppermute(w_sent, "groups", [(0, 1), (1, 0)])[0]
+        w_theirs = other_w_out(w_out, w_near, w_side, [blocks_1])
         weights = (w_out, w_theirs, w_up, w_down)
         done_0 = finish(state_0, [state_1[2]])
         done_1 = finish(state_1, [done_0[0]])

time: 209 us -> 187 us (0.89)
  waiting for transfers between devices: 59.5 us -> 33.6 us
  local copies, waits for them, and re-layouts: 0.78 us -> 6.5 us
  Pallas kernels: 91.8 us -> 89.7 us
    ppermute x7, waiting for transfers between devices: 26.4 us -> 15.5 us  [swap(): return lax.ppermute(value, 'tensor', [(0, 1), (1, 0)])]
    ppermute x4, waiting for transfers between devices: 24 us -> 14.4 us  [to_pair(): return lax.ppermute(value, 'dp', pairs)]
    ppermute x1, waiting for transfers between devices: 4.95 us -> 0.29 us  [per_device(): w_side = lax.ppermute(w_sent, 'groups', [(0, 1), (1, 0)])[0]]
    another operation x7, local copies, waits for them, and re-layouts: 0.12 us -> 2.62 us  [per_device(): jnp.stack([pre_gain, pre_shift, mlp_gain, mlp_shift, b_out, b_down])]
    unnamed x32 -> x24, local copies, waits for them, and re-layouts: 0.07 us -> 2.51 us
  transfers between devices with their start and end apart: 25 -> 25, of which waited for: 12 -> 12; matrix products, arithmetic and copies ran while one was open for 0% -> 2% of each run, Pallas kernels for 34% -> 36%
where the time goes in v3:
time: 187 us; the launch traced here: 186 us
  Pallas kernels  89.7 us (48%)
  starting transfers between devices  41.3 us (22%)
  waiting for transfers between devices  33.6 us (18%)
  between operations  15 us (8%)
  local copies, waits for them, and re-layouts  6.5 us (3%)
    pallas_call x2, Pallas kernels, mlp(): pl.pallas_call(functools.partial(mlp_kernel, len(after)), out_shape=(jax....  41 us
    pallas_call x2, Pallas kernels, attend(): pl.pallas_call(functools.partial(attend_kernel, len(after)), out_shape=ja...  17.7 us
    ppermute x7, waiting for transfers between devices, swap(): return lax.ppermute(value, 'tensor', [(0, 1), (1, 0)])  15.5 us
    ppermute x4, waiting for transfers between devices, to_pair(): return lax.ppermute(value, 'dp', pairs)  14.4 us
    ppermute x4, starting transfers between devices, to_next(): return lax.ppermute(value, 'dp', nexts)  13.4 us
    ppermute x4, starting transfers between devices, to_pair(): return lax.ppermute(value, 'dp', pairs)  12.9 us
    pallas_call x1, Pallas kernels, merge(): pl.pallas_call(functools.partial(merge_kernel, kept_count.shape[0], len(s...  12 us
    ppermute x7, starting transfers between devices, swap(): return lax.ppermute(value, 'tensor', [(0, 1), (1, 0)])  8.97 us
  transfers between devices with their start and end apart: 25, of which 12 were waited for; matrix products, arithmetic and copies ran while one was open for 2% of the time, Pallas kernels for 36%

profile of v3, /device:TPU:0, one launch (start us, length us, event | category | flops | bytes accessed | tf_op | source)
XLA Modules:
  0.0 186.3 jit_solution(14794244646756365465)
XLA Ops:
  6.5 5.6 %pack.1 = (bf16[8,64,1792]{2,1,0:T(8,128)(2,1)}, bf16[8,64,1792]{2,1,0:T(8,128)(2,1)S(1)}) custom-call(s32[1]{0:T(128)} %bitcast.19.device_ref, s32[8]{0:T(128)} %count_ref.5, s32[16]{0:T(128)} %bitcast.42, bf16[64,16,1792]{2,1,0:T(8,128)(2,1)} %bitcast.40), custom_call_target="tpu_custom_call" | custom-call | tf_op jit(solution)/shard_map/pack/pallas_call | solution.py:224
  13.7 2.6 %collective-permute-start.6 = (bf16[224,1792]{1,0:T(8,128)(2,1)S(1)}, bf16[224,1792]{1,0:T(8,128)(2,1)S(1)}, u32[]{:S(2)}, u32[]{:S(2)}) collective-permute-start(bf16[224,1792]{1,0:T(8,128)(2,1)S(1)} %w_piece.1), channel_id=1, source_target_pairs={{0,1},{1,0},{2,3},{3,2},{4,5},{5,4},{6,7},{7,6},{8,9},{9,8},{10,11... | collective-permute-start | bytes 2408456 | tf_op jit(solution)/shard_map/ppermute | solution.py:665
  16.3 2.0 %plan.1.table_ref = s32[94]{0:T(128)S(1)} custom-call(s32[1]{0:T(128)} %bitcast.19.device_ref, s32[8]{0:T(128)} %count_ref.5), custom_call_target="tpu_custom_call" | custom-call | flops 1000 | bytes 1000 | tf_op jit(solution)/shard_map/plan/pallas_call | solution.py:166
  18.3 3.3 %send.1 = (bf16[3,64,1792]{2,1,0:T(8,128)(2,1)S(1)}, bf16[2,64,1792]{2,1,0:T(8,128)(2,1)}, bf16[3,64,1792]{2,1,0:T(8,128)(2,1)S(1)}, bf16[2,64,1792]{2,1,0:T(8,128)(2,1)}) custom-call(s32[94]{0:T(128)S(1)} %plan.1.table_ref, bf16[8,64,1792]{2,1,0:T(8,128)(2,1)} %get-tuple-element.94.refs_0_, bf16[8,64,1792]{2,1,0:T(8,128)(2,1)} %collective-permute-done.1.refs_1_), custom_call_target="tpu_custom_call" | custom-call | flops 1000 | bytes 1000 | tf_op jit(solution)/shard_map/send/pallas_call | solution.py:357
  21.7 1.6 collective-permute-start.2
  23.3 1.5 collective-permute-start.3
  26.0 2.9 %collective-permute-start = (f32[1]{0:T(128)}, f32[1]{0:T(128)}, u32[]{:S(2)}, u32[]{:S(2)}) collective-permute-start(f32[1]{0:T(128)} %convert_element_type.12), channel_id=1, source_target_pairs={{0,16},{16,0},{1,17},{17,1},{2,18},{18,2},{3,19},{19,3},{4,20},{20... | collective-permute-start | bytes 20 | tf_op jit(solution)/shard_map/ppermute | solution.py:798
  30.3 9.0 %collective-permute-done.2 = bf16[3,64,1792]{2,1,0:T(8,128)(2,1)S(1)} collective-permute-done((bf16[3,64,1792]{2,1,0:T(8,128)(2,1)S(1)}, bf16[3,64,1792]{2,1,0:T(8,128)(2,1)S(1)}, u32[]{:S(2)}, u32[]{:S(2)}) %collective-permute-start.2) | collective-permute-done | bytes 688160 | tf_op jit(solution)/shard_map/ppermute | solution.py:788
  40.2 1.7 conditional.3
  40.2 1.7 deal_0.1
  43.7 1.6 collective-permute-start.7
  45.9 3.6 %collective-permute-start.8 = (bf16[2,64,1792]{2,1,0:T(8,128)(2,1)}, bf16[2,64,1792]{2,1,0:T(8,128)(2,1)S(1)}, u32[]{:S(2)}, u32[]{:S(2)}) collective-permute-start(bf16[2,64,1792]{2,1,0:T(8,128)(2,1)} %get-tuple-element.98), channel_id=1, source_target_pairs={{0,4},{2,6},{4,0},{6,2},{8,12},{10,14},{12,8},{14,10},{1,5},{3,7},... | collective-permute-start | bytes 1376264 | tf_op jit(solution)/shard_map/ppermute | solution.py:788
  49.5 5.1 %collective-permute-start.9 = (bf16[2,64,1792]{2,1,0:T(8,128)(2,1)}, bf16[2,64,1792]{2,1,0:T(8,128)(2,1)}, u32[]{:S(2)}, u32[]{:S(2)}) collective-permute-start(bf16[2,64,1792]{2,1,0:T(8,128)(2,1)} %get-tuple-element.99), channel_id=1, source_target_pairs={{0,0},{2,2},{4,8},{6,10},{8,4},{10,6},{12,12},{14,14},{1,1},{3,3},... | collective-permute-start | bytes 1376264 | tf_op jit(solution)/shard_map/ppermute | solution.py:791
  57.4 1.8 collective-permute-done.8
  59.2 2.1 %conditional.4 = (bf16[2,64,1792]{2,1,0:T(8,128)(2,1)S(1)}) conditional(s32[]{:T(128)} %bitcast.22, (s32[94]{0:T(128)S(1)}, bf16[8,64,1792]{2,1,0:T(8,128)(2,1)}, bf16[8,64,1792]{2,1,0:T(8,128)(2,1)}, bf16[3,64,1792]{2,1,0:T(8,128)(2,1)S(1)}, bf16[2,64,1792]{2,1,0:T(8,128)(2,1)S(1)}, /*index=5*/bf16[3,64,1792]{2,1,0:T(8,128)(2,1)}, ...), branch_computations={%region_2.0_spmd, %region_3.0_spmd} | conditional | flops 230388 | bytes 61474012 | solution.py:831
  59.9 1.2 deal_1.1
  61.3 1.6 collective-permute-start.11
  64.3 10.1 %attend.2.mine_ref = bf16[2,3,64,896]{3,2,1,0:T(8,128)(2,1)S(1)} custom-call(bf16[3,64,1792]{2,1,0:T(8,128)(2,1)S(1)} %copy-done.6, bf16[3,64,1792]{2,1,0:T(8,128)(2,1)S(1)} %collective-permute-done.4.other_ref, f32[6,1792]{1,0:T(8,128)S(1)} %stack.48.rows_ref, f32[3,896]{1,0:T(4,128)S(1)} %copy-done.2, bf16[3,1792,896]{2,1,0:T(8,128)(2,1)} %w_ref.5), custom_call_target="tpu_custom_call" | custom-call | flops 14797504512 | bytes 9633792 | tf_op jit(solution)/shard_map/attend/pallas_call | solution.py:488
  75.0 7.6 %attend.3.refs_0_.mine_ref = bf16[2,2,64,896]{3,2,1,0:T(8,128)(2,1)S(1)} custom-call(bf16[2,64,1792]{2,1,0:T(8,128)(2,1)S(1)} %get-tuple-element.134.refs_2_.own_ref, bf16[2,64,1792]{2,1,0:T(8,128)(2,1)S(1)} %collective-permute-done.11.other_ref, f32[6,1792]{1,0:T(8,128)S(1)} %stack.48.rows_ref, f32[3,896]{1,0:T(4,128)S(1)} %copy-done.2, ...), custom_call_target="tpu_custom_call" | custom-call | flops 9865003008 | bytes 9633792 | tf_op jit(solution)/shard_map/attend/pallas_call | solution.py:488
  82.6 1.6 collective-permute-start.13
  85.2 7.7 %collective-permute-done.5.theirs_ref = bf16[2,3,64,896]{3,2,1,0:T(8,128)(2,1)S(1)} collective-permute-done((bf16[2,3,64,896]{3,2,1,0:T(8,128)(2,1)S(1)}, bf16[2,3,64,896]{3,2,1,0:T(8,128)(2,1)S(1)}, u32[]{:S(2)}, u32[]{:S(2)}) %collective-permute-start.5) | collective-permute-done | bytes 688160 | tf_op jit(solution)/shard_map/ppermute | solution.py:665
  92.9 23.5 %mlp.2 = (f32[3,64,1792]{2,1,0:T(8,128)S(1)}, bf16[3,64,1792]{2,1,0:T(8,128)(2,1)S(1)}) custom-call(bf16[3,64,1792]{2,1,0:T(8,128)(2,1)S(1)} %copy-done.6, bf16[3,64,1792]{2,1,0:T(8,128)(2,1)S(1)} %collective-permute-done.4.other_ref, bf16[2,3,64,896]{3,2,1,0:T(8,128)(2,1)S(1)} %attend.2.mine_ref, ...), custom_call_target="tpu_custom_call" | custom-call | flops 30299652096 | bytes 39452672 | tf_op jit(solution)/shard_map/mlp/pallas_call | solution.py:614
  117.0 17.5 %mlp.3 = (f32[2,64,1792]{2,1,0:T(8,128)S(1)}, bf16[2,64,1792]{2,1,0:T(8,128)(2,1)S(1)}) custom-call(bf16[2,64,1792]{2,1,0:T(8,128)(2,1)S(1)} %get-tuple-element.134.refs_2_.own_ref, bf16[2,64,1792]{2,1,0:T(8,128)(2,1)S(1)} %collective-permute-done.11.other_ref, bf16[2,2,64,896]{3,2,1,0:T(8,128)(2,1)S(1)} %attend.3.refs_0_.mine_ref, ...), custom_call_target="tpu_custom_call" | custom-call | flops 20199768064 | bytes 39452672 | tf_op jit(solution)/shard_map/mlp/pallas_call | solution.py:614
  135.5 3.9 %collective-permute-start.15 = (bf16[3,64,1792]{2,1,0:T(8,128)(2,1)}, bf16[3,64,1792]{2,1,0:T(8,128)(2,1)S(1)}, u32[]{:S(2)}, u32[]{:S(2)}) collective-permute-start(bf16[3,64,1792]{2,1,0:T(8,128)(2,1)} %add.61.refs_0_), channel_id=1, source_target_pairs={{0,4},{2,6},{4,0},{6,2},{8,12},{10,14},{12,8},{14,10},{1,5},{3,7},... | collective-permute-start | bytes 2064392 | tf_op jit(solution)/shard_map/ppermute | solution.py:788
  139.4 1.7 collective-permute-start.16
  141.1 1.5 collective-permute-start.14
  142.6 7.7 %collective-permute-done.14.came_ref = bf16[2,64,1792]{2,1,0:T(8,128)(2,1)S(1)} collective-permute-done((bf16[2,64,1792]{2,1,0:T(8,128)(2,1)S(1)}, bf16[2,64,1792]{2,1,0:T(8,128)(2,1)S(1)}, u32[]{:S(2)}, u32[]{:S(2)}) %collective-permute-start.14) | collective-permute-done | bytes 458784 | tf_op jit(solution)/shard_map/ppermute | solution.py:665
  150.3 1.9 %collective-permute-done.15.refs_0_.refs_2_ = bf16[3,64,1792]{2,1,0:T(8,128)(2,1)S(1)} collective-permute-done((bf16[3,64,1792]{2,1,0:T(8,128)(2,1)}, bf16[3,64,1792]{2,1,0:T(8,128)(2,1)S(1)}, u32[]{:S(2)}, u32[]{:S(2)}) %collective-permute-start.15) | collective-permute-done | bytes 688160 | tf_op jit(solution)/shard_map/ppermute | solution.py:788
  153.1 3.8 %collective-permute-start.17 = (bf16[2,64,1792]{2,1,0:T(8,128)(2,1)}, bf16[2,64,1792]{2,1,0:T(8,128)(2,1)}, u32[]{:S(2)}, u32[]{:S(2)}) collective-permute-start(bf16[2,64,1792]{2,1,0:T(8,128)(2,1)} %add.62.refs_1_), channel_id=1, source_target_pairs={{0,4},{2,6},{4,0},{6,2},{8,12},{10,14},{12,8},{14,10},{1,5},{3,7},... | collective-permute-start | bytes 1376264 | tf_op jit(solution)/shard_map/ppermute | solution.py:788
  156.9 5.1 %collective-permute-start.18 = (bf16[2,64,1792]{2,1,0:T(8,128)(2,1)}, bf16[2,64,1792]{2,1,0:T(8,128)(2,1)}, u32[]{:S(2)}, u32[]{:S(2)}) collective-permute-start(bf16[2,64,1792]{2,1,0:T(8,128)(2,1)} %add.62.refs_1_), channel_id=1, source_target_pairs={{0,0},{2,2},{4,8},{6,10},{8,4},{10,6},{12,12},{14,14},{1,1},{3,3},... | collective-permute-start | bytes 1376264 | tf_op jit(solution)/shard_map/ppermute | solution.py:791
  162.5 1.7 collective-permute-done.17.refs_3_
  167.4 12.0 %merge.1 = bf16[64,16,1792]{2,1,0:T(8,128)(2,1)} custom-call(s32[1]{0:T(128)} %bitcast.19.device_ref, s32[8]{0:T(128)} %count_ref.5, s32[16]{0:T(128)} %bitcast.43, s32[94]{0:T(128)S(1)} %plan.1.table_ref, s32[1]{0:T(128)} %convert_element_type.13.slow_ref, bf16[64,16,1792]{2,1,0:T(8,128)(2,1)} %bitcast.41, bf16[3,64,1792]{2,1,0:T(8,128)(2,1)} %add.61.refs_0_, ...), custom_call_target="tpu_custom_call" | custom-call | flops 1000 | bytes 1000 | tf_op jit(solution)/shard_map/merge/pallas_call | solution.py:292
  (73 shorter events, 18.5 us)
Async XLA Ops:
  12.1 6.2 %collective-permute-start.1 = (bf16[8,64,1792]{2,1,0:T(8,128)(2,1)S(1)}, bf16[8,64,1792]{2,1,0:T(8,128)(2,1)}, u32[]{:S(2)}, u32[]{:S(2)}) collective-permute-start(bf16[8,64,1792]{2,1,0:T(8,128)(2,1)S(1)} %get-tuple-element.95.refs_0_), channel_id=1, source_target_pairs={{0,2},{2,0},{4,6},{6,4},{8,10},{10,8},{12,14},{14,12},{1,3},{3,1},... | collective-permute-start | bytes 5505032 | tf_op jit(solution)/shard_map/ppermute | solution.py:785
  13.7 28.3 %collective-permute-start.6 = (bf16[224,1792]{1,0:T(8,128)(2,1)S(1)}, bf16[224,1792]{1,0:T(8,128)(2,1)S(1)}, u32[]{:S(2)}, u32[]{:S(2)}) collective-permute-start(bf16[224,1792]{1,0:T(8,128)(2,1)S(1)} %w_piece.1), channel_id=1, source_target_pairs={{0,1},{1,0},{2,3},{3,2},{4,5},{5,4},{6,7},{7,6},{8,9},{9,8},{10,11... | collective-permute-start | bytes 2408456 | tf_op jit(solution)/shard_map/ppermute | solution.py:665
  21.7 17.6 %collective-permute-start.2 = (bf16[3,64,1792]{2,1,0:T(8,128)(2,1)S(1)}, bf16[3,64,1792]{2,1,0:T(8,128)(2,1)S(1)}, u32[]{:S(2)}, u32[]{:S(2)}) collective-permute-start(bf16[3,64,1792]{2,1,0:T(8,128)(2,1)S(1)} %get-tuple-element.96), channel_id=1, source_target_pairs={{0,4},{2,6},{4,0},{6,2},{8,12},{10,14},{12,8},{14,10},{1,5},{3,7},... | collective-permute-start | bytes 2064392 | tf_op jit(solution)/shard_map/ppermute | solution.py:788
  23.3 16.0 %collective-permute-start.3 = (bf16[3,64,1792]{2,1,0:T(8,128)(2,1)S(1)}, bf16[3,64,1792]{2,1,0:T(8,128)(2,1)}, u32[]{:S(2)}, u32[]{:S(2)}) collective-permute-start(bf16[3,64,1792]{2,1,0:T(8,128)(2,1)S(1)} %get-tuple-element.97), channel_id=1, source_target_pairs={{0,0},{2,2},{4,8},{6,10},{8,4},{10,6},{12,12},{14,14},{1,1},{3,3},... | collective-permute-start | bytes 2064392 | tf_op jit(solution)/shard_map/ppermute | solution.py:791
  26.0 3.6 %collective-permute-start = (f32[1]{0:T(128)}, f32[1]{0:T(128)}, u32[]{:S(2)}, u32[]{:S(2)}) collective-permute-start(f32[1]{0:T(128)} %convert_element_type.12), channel_id=1, source_target_pairs={{0,16},{16,0},{1,17},{17,1},{2,18},{18,2},{3,19},{19,3},{4,20},{20... | collective-permute-start | bytes 20 | tf_op jit(solution)/shard_map/ppermute | solution.py:798
  41.9 12.7 %copy-start.9 = (f32[1792]{0:T(1024)S(1)}, f32[1792]{0:T(1024)}, u32[]{:S(2)}) copy-start(f32[1792]{0:T(1024)} %param.26) | copy-start | bytes 21508
  41.9 12.7 %copy-start.11 = (f32[1792]{0:T(1024)S(1)}, f32[1792]{0:T(1024)}, u32[]{:S(2)}) copy-start(f32[1792]{0:T(1024)} %param.32) | copy-start | bytes 21508
  42.0 12.7 %copy-start.12 = (f32[1792]{0:T(1024)S(1)}, f32[1792]{0:T(1024)}, u32[]{:S(2)}) copy-start(f32[1792]{0:T(1024)} %param.33) | copy-start | bytes 21508
  42.0 13.3 %copy-start.13 = (f32[1792]{0:T(1024)S(1)}, f32[1792]{0:T(1024)}, u32[]{:S(2)}) copy-start(f32[1792]{0:T(1024)} %param.31) | copy-start | bytes 21508
  42.0 13.9 %copy-start.14 = (f32[1792]{0:T(1024)S(1)}, f32[1792]{0:T(1024)}, u32[]{:S(2)}) copy-start(f32[1792]{0:T(1024)} %param.37) | copy-start | bytes 21508
  42.0 14.5 %copy-start.8 = (f32[4608]{0:T(1024)S(1)}, f32[4608]{0:T(1024)}, u32[]{:S(2)}) copy-start(f32[4608]{0:T(1024)} %param.35) | copy-start | bytes 55300
  42.8 16.4 %copy-start.4 = (bf16[3,64,1792]{2,1,0:T(8,128)(2,1)S(1)}, bf16[3,64,1792]{2,1,0:T(8,128)(2,1)}, u32[]{:S(2)}) copy-start(bf16[3,64,1792]{2,1,0:T(8,128)(2,1)} %copy-done.3) | copy-start | bytes 2064388
  43.7 19.5 %collective-permute-start.7 = (bf16[1,224,1792]{2,1,0:T(8,128)(2,1)}, bf16[1,224,1792]{2,1,0:T(8,128)(2,1)S(1)}, u32[]{:S(2)}, u32[]{:S(2)}) collective-permute-start(bf16[1,224,1792]{2,1,0:T(8,128)(2,1)} %w_near.1), channel_id=1, source_target_pairs={{0,16},{16,0},{1,17},{17,1},{2,18},{18,2},{3,19},{19,3},{4,20},{20... | collective-permute-start | bytes 2408456 | tf_op jit(solution)/shard_map/ppermute | solution.py:854
  45.3 18.2 %collective-permute-start.4 = (bf16[3,64,1792]{2,1,0:T(8,128)(2,1)}, bf16[3,64,1792]{2,1,0:T(8,128)(2,1)S(1)}, u32[]{:S(2)}, u32[]{:S(2)}) collective-permute-start(bf16[3,64,1792]{2,1,0:T(8,128)(2,1)} %copy-done.5), channel_id=1, source_target_pairs={{0,1},{1,0},{2,3},{3,2},{4,5},{5,4},{6,7},{7,6},{8,9},{9,8},{10,11... | collective-permute-start | bytes 2064392 | tf_op jit(solution)/shard_map/ppermute | solution.py:665
  45.9 13.3 %collective-permute-start.8 = (bf16[2,64,1792]{2,1,0:T(8,128)(2,1)}, bf16[2,64,1792]{2,1,0:T(8,128)(2,1)S(1)}, u32[]{:S(2)}, u32[]{:S(2)}) collective-permute-start(bf16[2,64,1792]{2,1,0:T(8,128)(2,1)} %get-tuple-element.98), channel_id=1, source_target_pairs={{0,4},{2,6},{4,0},{6,2},{8,12},{10,14},{12,8},{14,10},{1,5},{3,7},... | collective-permute-start | bytes 1376264 | tf_op jit(solution)/shard_map/ppermute | solution.py:788
  49.5 9.6 %collective-permute-start.9 = (bf16[2,64,1792]{2,1,0:T(8,128)(2,1)}, bf16[2,64,1792]{2,1,0:T(8,128)(2,1)}, u32[]{:S(2)}, u32[]{:S(2)}) collective-permute-start(bf16[2,64,1792]{2,1,0:T(8,128)(2,1)} %get-tuple-element.99), channel_id=1, source_target_pairs={{0,0},{2,2},{4,8},{6,10},{8,4},{10,6},{12,12},{14,14},{1,1},{3,3},... | collective-permute-start | bytes 1376264 | tf_op jit(solution)/shard_map/ppermute | solution.py:791
  61.3 13.7 %collective-permute-start.11 = (bf16[2,64,1792]{2,1,0:T(8,128)(2,1)S(1)}, bf16[2,64,1792]{2,1,0:T(8,128)(2,1)S(1)}, u32[]{:S(2)}, u32[]{:S(2)}) collective-permute-start(bf16[2,64,1792]{2,1,0:T(8,128)(2,1)S(1)} %get-tuple-element.134.refs_2_.own_ref), channel_id=1, source_target_pairs={{0,1},{1,0},{2,3},{3,2},{4,5},{5,4},{6,7},{7,6},{8,9},{9,8},{10,11... | collective-permute-start | bytes 1376264 | tf_op jit(solution)/shard_map/ppermute | solution.py:665
  63.4 20.9 %collective-permute-start.10 = (bf16[2,224,1792]{2,1,0:T(8,128)(2,1)S(1)}, bf16[2,224,1792]{2,1,0:T(8,128)(2,1)S(1)}, u32[]{:S(2)}, u32[]{:S(2)}) collective-permute-start(bf16[2,224,1792]{2,1,0:T(8,128)(2,1)S(1)} %w_both.1), channel_id=1, source_target_pairs={{0,2},{2,0},{4,6},{6,4},{8,10},{10,8},{12,14},{14,12},{1,3},{3,1},... | collective-permute-start | bytes 4816904 | tf_op jit(solution)/shard_map/ppermute | solution.py:729
  74.5 18.4 %collective-permute-start.5 = (bf16[2,3,64,896]{3,2,1,0:T(8,128)(2,1)S(1)}, bf16[2,3,64,896]{3,2,1,0:T(8,128)(2,1)S(1)}, u32[]{:S(2)}, u32[]{:S(2)}) collective-permute-start(bf16[2,3,64,896]{3,2,1,0:T(8,128)(2,1)S(1)} %attend.2.mine_ref), channel_id=1, source_target_pairs={{0,1},{1,0},{2,3},{3,2},{4,5},{5,4},{6,7},{7,6},{8,9},{9,8},{10,11... | collective-permute-start | bytes 2064392 | tf_op jit(solution)/shard_map/ppermute | solution.py:665
  82.6 34.4 %collective-permute-start.13 = (bf16[2,2,64,896]{3,2,1,0:T(8,128)(2,1)S(1)}, bf16[2,2,64,896]{3,2,1,0:T(8,128)(2,1)S(1)}, u32[]{:S(2)}, u32[]{:S(2)}) collective-permute-start(bf16[2,2,64,896]{3,2,1,0:T(8,128)(2,1)S(1)} %attend.3.refs_0_.mine_ref), channel_id=1, source_target_pairs={{0,1},{1,0},{2,3},{3,2},{4,5},{5,4},{6,7},{7,6},{8,9},{9,8},{10,11... | collective-permute-start | bytes 1376264 | tf_op jit(solution)/shard_map/ppermute | solution.py:665
  116.5 18.0 %collective-permute-start.12 = (bf16[3,64,1792]{2,1,0:T(8,128)(2,1)S(1)}, bf16[3,64,1792]{2,1,0:T(8,128)(2,1)S(1)}, u32[]{:S(2)}, u32[]{:S(2)}) collective-permute-start(bf16[3,64,1792]{2,1,0:T(8,128)(2,1)S(1)} %get-tuple-element.101), channel_id=1, source_target_pairs={{0,1},{1,0},{2,3},{3,2},{4,5},{5,4},{6,7},{7,6},{8,9},{9,8},{10,11... | collective-permute-start | bytes 2064392 | tf_op jit(solution)/shard_map/ppermute | solution.py:665
  135.5 16.8 %collective-permute-start.15 = (bf16[3,64,1792]{2,1,0:T(8,128)(2,1)}, bf16[3,64,1792]{2,1,0:T(8,128)(2,1)S(1)}, u32[]{:S(2)}, u32[]{:S(2)}) collective-permute-start(bf16[3,64,1792]{2,1,0:T(8,128)(2,1)} %add.61.refs_0_), channel_id=1, source_target_pairs={{0,4},{2,6},{4,0},{6,2},{8,12},{10,14},{12,8},{14,10},{1,5},{3,7},... | collective-permute-start | bytes 2064392 | tf_op jit(solution)/shard_map/ppermute | solution.py:788
  139.4 12.9 %collective-permute-start.16 = (bf16[3,64,1792]{2,1,0:T(8,128)(2,1)}, bf16[3,64,1792]{2,1,0:T(8,128)(2,1)S(1)}, u32[]{:S(2)}, u32[]{:S(2)}) collective-permute-start(bf16[3,64,1792]{2,1,0:T(8,128)(2,1)} %add.61.refs_0_), channel_id=1, source_target_pairs={{0,0},{2,2},{4,8},{6,10},{8,4},{10,6},{12,12},{14,14},{1,1},{3,3},... | collective-permute-start | bytes 2064392 | tf_op jit(solution)/shard_map/ppermute | solution.py:791
  141.1 9.2 %collective-permute-start.14 = (bf16[2,64,1792]{2,1,0:T(8,128)(2,1)S(1)}, bf16[2,64,1792]{2,1,0:T(8,128)(2,1)S(1)}, u32[]{:S(2)}, u32[]{:S(2)}) collective-permute-start(bf16[2,64,1792]{2,1,0:T(8,128)(2,1)S(1)} %get-tuple-element.103), channel_id=1, source_target_pairs={{0,1},{1,0},{2,3},{3,2},{4,5},{5,4},{6,7},{7,6},{8,9},{9,8},{10,11... | collective-permute-start | bytes 1376264 | tf_op jit(solution)/shard_map/ppermute | solution.py:665
  142.6 19.8 %collective-permute-start.19 = (bf16[3,64,1792]{2,1,0:T(8,128)(2,1)}, bf16[3,64,1792]{2,1,0:T(8,128)(2,1)S(1)}, u32[]{:S(2)}, u32[]{:S(2)}) collective-permute-start(bf16[3,64,1792]{2,1,0:T(8,128)(2,1)} %add.61.refs_0_), channel_id=1, source_target_pairs={{0,2},{2,0},{4,6},{6,4},{8,10},{10,8},{12,14},{14,12},{1,3},{3,1},... | collective-permute-start | bytes 2064392 | tf_op jit(solution)/shard_map/ppermute | solution.py:785
  153.1 11.1 %collective-permute-start.17 = (bf16[2,64,1792]{2,1,0:T(8,128)(2,1)}, bf16[2,64,1792]{2,1,0:T(8,128)(2,1)}, u32[]{:S(2)}, u32[]{:S(2)}) collective-permute-start(bf16[2,64,1792]{2,1,0:T(8,128)(2,1)} %add.62.refs_1_), channel_id=1, source_target_pairs={{0,4},{2,6},{4,0},{6,2},{8,12},{10,14},{12,8},{14,10},{1,5},{3,7},... | collective-permute-start | bytes 1376264 | tf_op jit(solution)/shard_map/ppermute | solution.py:788
  156.9 7.3 %collective-permute-start.18 = (bf16[2,64,1792]{2,1,0:T(8,128)(2,1)}, bf16[2,64,1792]{2,1,0:T(8,128)(2,1)}, u32[]{:S(2)}, u32[]{:S(2)}) collective-permute-start(bf16[2,64,1792]{2,1,0:T(8,128)(2,1)} %add.62.refs_1_), channel_id=1, source_target_pairs={{0,0},{2,2},{4,8},{6,10},{8,4},{10,6},{12,12},{14,14},{1,1},{3,3},... | collective-permute-start | bytes 1376264 | tf_op jit(solution)/shard_map/ppermute | solution.py:791
  162.0 3.8 %collective-permute-start.21 = (bf16[3,64,1792]{2,1,0:T(8,128)(2,1)S(1)}, bf16[3,64,1792]{2,1,0:T(8,128)(2,1)S(1)}, u32[]{:S(2)}, u32[]{:S(2)}) collective-permute-start(bf16[3,64,1792]{2,1,0:T(8,128)(2,1)S(1)} %collective-permute-done.15.refs_0_.refs_2_), channel_id=1, source_target_pairs={{0,2},{2,0},{4,6},{6,4},{8,10},{10,8},{12,14},{14,12},{1,3},{3,1},... | collective-permute-start | bytes 2064392 | tf_op jit(solution)/shard_map/ppermute | solution.py:785
  162.0 4.1 %collective-permute-start.23 = (bf16[3,64,1792]{2,1,0:T(8,128)(2,1)S(1)}, bf16[3,64,1792]{2,1,0:T(8,128)(2,1)S(1)}, u32[]{:S(2)}, u32[]{:S(2)}) collective-permute-start(bf16[3,64,1792]{2,1,0:T(8,128)(2,1)S(1)} %collective-permute-done.16.refs_1_.refs_4_), channel_id=1, source_target_pairs={{0,2},{2,0},{4,6},{6,4},{8,10},{10,8},{12,14},{14,12},{1,3},{3,1},... | collective-permute-start | bytes 2064392 | tf_op jit(solution)/shard_map/ppermute | solution.py:785
  162.5 3.3 %collective-permute-start.20 = (bf16[2,64,1792]{2,1,0:T(8,128)(2,1)}, bf16[2,64,1792]{2,1,0:T(8,128)(2,1)}, u32[]{:S(2)}, u32[]{:S(2)}) collective-permute-start(bf16[2,64,1792]{2,1,0:T(8,128)(2,1)} %add.62.refs_1_), channel_id=1, source_target_pairs={{0,2},{2,0},{4,6},{6,4},{8,10},{10,8},{12,14},{14,12},{1,3},{3,1},... | collective-permute-start | bytes 1376264 | tf_op jit(solution)/shard_map/ppermute | solution.py:785
  164.2 2.6 %collective-permute-start.22 = (bf16[2,64,1792]{2,1,0:T(8,128)(2,1)}, bf16[2,64,1792]{2,1,0:T(8,128)(2,1)}, u32[]{:S(2)}, u32[]{:S(2)}) collective-permute-start(bf16[2,64,1792]{2,1,0:T(8,128)(2,1)} %collective-permute-done.17.refs_3_), channel_id=1, source_target_pairs={{0,2},{2,0},{4,6},{6,4},{8,10},{10,8},{12,14},{14,12},{1,3},{3,1},... | collective-permute-start | bytes 1376264 | tf_op jit(solution)/shard_map/ppermute | solution.py:785
  164.2 3.2 %collective-permute-start.24 = (bf16[2,64,1792]{2,1,0:T(8,128)(2,1)}, bf16[2,64,1792]{2,1,0:T(8,128)(2,1)}, u32[]{:S(2)}, u32[]{:S(2)}) collective-permute-start(bf16[2,64,1792]{2,1,0:T(8,128)(2,1)} %collective-permute-done.18.refs_5_), channel_id=1, source_target_pairs={{0,2},{2,0},{4,6},{6,4},{8,10},{10,8},{12,14},{14,12},{1,3},{3,1},... | collective-permute-start | bytes 1376264 | tf_op jit(solution)/shard_map/ppermute | solution.py:785
  (6 other events, 17.0 us)

commit v4 on v3

--- a/solution.py
+++ b/solution.py
@@ -238,78 +238,81 @@
     )(device, kept_count, keep_row, home)
 
 
-def merge_kernel(pages, total, device_ref, count_ref, keep_ref, table_ref, slow_ref, home_ref, *refs):
-    sources = refs[:total]
-    out_ref, held, landed, sems = refs[total:]
+LATE = (3, 5, 9, 11)
+
+
+def merge_kernel(pages, device_ref, count_ref, keep_ref, code_ref, home_ref, found_ref, *refs):
+    late, out_ref, held = refs[:-2], refs[-2], refs[-1]
     page_blocks, width = home_ref.shape[1], home_ref.shape[2]
-    step = pl.program_id(0)
-    slots = 2 * PAGE_HALF
-
-    @pl.when(step == 0)
+    slots, size = 2 * PAGE_HALF, CHUNKS[-1]
+    places = slots + size * len(LATE)
+
+    @pl.when(pl.program_id(0) == 0)
     def _():
-        at = jnp.where(slow_ref[0] > 0, AT_IN_ORDER, AT_HOME)
-        start_copies(
-            sources,
-            [(table_ref[at + slot], landed.at[slot], sems.at[slot]) for slot in range(slots)],
-            landed.shape[1] // GROUP_ROWS,
-        )
-
-    blocks = kept_blocks_once(device_ref, count_ref, keep_ref, pages, held)
+        blocks = kept_blocks(device_ref, count_ref, keep_ref, pages)
+        spots = []
+        for slot in range(slots):
+            code = code_ref[slot]
+            spot = jnp.int32(slot)
+            for number, source in enumerate(LATE):
+                spot = jnp.where(code >> 4 == source, slots + number * size + (code & 15), spot)
+            spots.append(jnp.where(blocks[slot] >= 0, spot, -1))
+        for place in range(places):
+            block = jnp.int32(-1)
+            for slot in range(slots) if place >= slots else (place,):
+                block = jnp.where(spots[slot] == place, blocks[slot], block)
+            held[place] = block
+
     span = GROUP_ROWS * page_blocks
-    depth = slots * GROUP_ROWS
+    depth = places * GROUP_ROWS
     row = lax.broadcasted_iota(jnp.int32, (span, depth), 0)
     column = lax.broadcasted_iota(jnp.int32, (span, depth), 1)
-    slot_id = lax.broadcasted_iota(jnp.int32, (1, depth), 1) // GROUP_ROWS
+    place_id = lax.broadcasted_iota(jnp.int32, (1, depth), 1) // GROUP_ROWS
     block_id = lax.broadcasted_iota(jnp.int32, (span, 1), 0) % page_blocks
     wanted = jnp.full((1, depth), -1, jnp.int32)
     kept = jnp.zeros((span, 1), jnp.int32)
-    for place, block in enumerate(blocks):
-        wanted = jnp.where(slot_id == place, block, wanted)
+    for place in range(places):
+        block = held[place]
+        wanted = jnp.where(place_id == place, block, wanted)
         kept = kept + jnp.where(block_id == block, 1, 0)
     chosen = jnp.where(
         (row // page_blocks == column % GROUP_ROWS) & (row % page_blocks == wanted), 1.0, 0.0
     ).astype(BF16)
-
-    same = lax.broadcasted_iota(jnp.int32, (span, span), 0) == lax.broadcasted_iota(
-        jnp.int32, (span, span), 1
-    )
-    stays = jnp.where(same & (kept == 0), 1.0, 0.0).astype(BF16)
-    rows = pl.ds(pl.multiple_of(step * GROUP_ROWS, GROUP_ROWS), GROUP_ROWS)
-    for slot in range(slots):
-        pltpu.make_async_copy(
-            sources[0].at[0, rows, :], landed.at[slot, rows, :], sems.at[slot, step]
-        ).wait()
-    source = landed[:, rows, :].reshape(depth, width)
-    result = jnp.dot(chosen, source, preferred_element_type=F32)
-    result += jnp.dot(stays, home_ref[...].reshape(span, width), preferred_element_type=F32)
-    out_ref[...] = result.astype(BF16).reshape(GROUP_ROWS, page_blocks, width)
-
-
-def merge(device, kept_count, keep_row, table, slow, home, sources):
+    source = jnp.concatenate(
+        [ref[...].reshape(-1, width) for ref in (found_ref,) + tuple(late)], axis=0
+    )
+    landed = jnp.dot(chosen, source, preferred_element_type=F32)
+    home = home_ref[...].reshape(span, width).astype(F32)
+    merged = jnp.where(kept > 0, landed, home).astype(BF16)
+    out_ref[...] = merged.reshape(GROUP_ROWS, page_blocks, width)
+
+
+def merge(device, kept_count, keep_row, codes, home, found, late):
     rows, page_blocks, width = home.shape
     page = pl.BlockSpec((GROUP_ROWS, page_blocks, width), lambda step, *_: (step, 0, 0))
-    slots = 2 * PAGE_HALF
+
+    def some(array):
+        return pl.BlockSpec((array.shape[0], GROUP_ROWS, width), lambda step, *_: (0, step, 0))
+
     return pl.pallas_call(
-        functools.partial(merge_kernel, kept_count.shape[0], len(sources)),
+        functools.partial(merge_kernel, kept_count.shape[0]),
         out_shape=jax.ShapeDtypeStruct(home.shape, BF16),
         grid_spec=pltpu.PrefetchScalarGridSpec(
-            num_scalar_prefetch=5,
+            num_scalar_prefetch=4,
             grid=(rows // GROUP_ROWS,),
-            in_specs=[page] + [pl.BlockSpec(memory_space=pl.ANY)] * len(sources),
+            in_specs=[page, some(found)] + [some(array) for array in late],
             out_specs=page,
             scratch_shapes=[
-                pltpu.SMEM((slots,), jnp.int32),
-                pltpu.VMEM((slots, rows, width), BF16),
-                pltpu.SemaphoreType.DMA((slots, rows // GROUP_ROWS)),
+                pltpu.SMEM((found.shape[0] + CHUNKS[-1] * len(LATE),), jnp.int32)
             ],
         ),
         compiler_params=pltpu.CompilerParams(vmem_limit_bytes=20 * MIB),
         cost_estimate=SMALL_COST,
         name="merge",
-    )(device, kept_count, keep_row, table, slow, home, *sources)
-
-
-def start_copies(sources, wanted, groups=0):
+    )(device, kept_count, keep_row, codes, home, found, *late)
+
+
+def start_copies(sources, wanted):
     for code, target, sem in wanted:
         which, place = code >> 4, code & 15
         for index, source in enumerate(sources):
@@ -325,15 +328,7 @@
             @pl.when(here)
             def _(source=source, place=place, target=target, sem=sem):
                 inside = jnp.minimum(place, source.shape[0] - 1)
-                if groups == 0:
-                    pltpu.make_async_copy(source.at[inside], target, sem).start()
-                    return
-                size = source.shape[1] // groups
-                for group in range(groups):
-                    rows = pl.ds(group * size, size)
-                    pltpu.make_async_copy(
-                        source.at[inside, rows, :], target.at[rows, :], sem.at[group]
-                    ).start()
+                pltpu.make_async_copy(source.at[inside], target, sem).start()
 
 
 def choose_kernel(parts, n_sources, table_ref, *refs):
@@ -504,9 +499,9 @@
     )(own, other, rows_params, b_qkv, in_hbm(w_qkv), *after)
 
 
-UP_TILE = 512
+UP_TILE = 768
 DOWN_TILE = 256
-SLOTS = 5
+SLOTS = 4
 
 
 def mlp_kernel(n_after, own_ref, other_ref, mine_ref, theirs_ref, rows_ref, b_up_ref, w_mine, w_theirs,
@@ -779,7 +774,9 @@
     device = lax.axis_index("dp").astype(jnp.int32).reshape(1)
     mates = [(d, d ^ 1) for d in range(dp_size)]
     pairs = [(d, d ^ 2) for d in range(dp_size)]
-    nexts = [(d, min(max(((d + 2) ^ 2) - 2, d & 1), dp_size - 2 + (d & 1))) for d in range(dp_size)]
+    nexts = [
+        (d, d ^ 1 if d < 2 or d >= dp_size - 2 else ((d + 2) ^ 2) - 2) for d in range(dp_size)
+    ]
 
     def to_mate(value):
         return lax.ppermute(value, "dp", mates)
@@ -867,7 +864,11 @@
         from_next = [to_next(value) for value in results]
 
     back = results + from_pair + from_next
-    back = back + [to_mate(value) for value in back]
+    last = len(parts) - 1
+    back = back + [
+        back[place] if place + len(back) in LATE else to_mate(value)
+        for place, value in enumerate(back)
+    ]
 
     def home_slow():
         spread = lax.all_gather(jnp.concatenate(results), "dp", axis=0, tiled=True)
@@ -878,8 +879,16 @@
         )
 
     found = lax.cond(short, home_slow, lambda: (mine, from_mate))
-    slow = short.astype(jnp.int32).reshape(1)
-    return merge(device, kept_count, keep_row, table, slow, home, back + list(found))[None]
+    slots = 2 * PAGE_HALF
+    codes = jnp.where(
+        short, table[AT_IN_ORDER : AT_IN_ORDER + slots], table[AT_HOME : AT_HOME + slots]
+    )
+    early = [results[0] if place in LATE else value for place, value in enumerate(back)]
+    (gathered,) = choose(codes, [(0, slots)], early + list(found), "gather")
+    late = [from_pair[last], from_next[last]]
+    mates_late = to_mate(line_up(late, [gathered], "late"))
+    late.append(mates_late.reshape((-1,) + mates_late.shape[2:]))
+    return merge(device, kept_count, keep_row, codes, home, gathered, late)[None]
 
 
 def solution(mesh):

time: 187 us -> 180 us (0.963)
  starting transfers between devices: 41.3 us -> 22.3 us
  waiting for transfers between devices: 33.6 us -> 49.1 us
  local copies, waits for them, and re-layouts: 6.5 us -> 4.52 us
    ppermute x4, waiting for transfers between devices: 14.4 us -> 36.8 us  [to_pair(): return lax.ppermute(value, 'dp', pairs)]
    ppermute x4, starting transfers between devices: 13.4 us -> 0.38 us  [to_next(): return lax.ppermute(value, 'dp', nexts)]
    ppermute x7, waiting for transfers between devices: 15.5 us -> 7.71 us  [swap(): return lax.ppermute(value, 'tensor', [(0, 1), (1, 0)])]
    ppermute x4, starting transfers between devices: 12.9 us -> 6.75 us  [to_pair(): return lax.ppermute(value, 'dp', pairs)]
    pallas_call x3 -> x4, Pallas kernels: 6.26 us -> 11.6 us  [choose(): pl.pallas_call(functools.partial(choose_kernel, parts, len(sources)), out...]
    pallas_call x1, Pallas kernels: 12 us -> 7.04 us  [merge(): pl.pallas_call(functools.partial(merge_kernel, kept_count.shape[0]), out_...]
    pallas_call x2, Pallas kernels: 41 us -> 39 us  [mlp(): pl.pallas_call(functools.partial(mlp_kernel, len(after)), out_shape=(jax....]
    unnamed x24 -> x22, local copies, waits for them, and re-layouts: 2.51 us -> 0.5 us
  transfers between devices with their start and end apart: 25 -> 24, of which waited for: 12 -> 9; matrix products, arithmetic and copies ran while one was open for 2% -> 2% of each run, Pallas kernels for 36% -> 38%
where the time goes in v4:
time: 180 us
  Pallas kernels  88.6 us (49%)
  waiting for transfers between devices  49.1 us (27%)
  starting transfers between devices  22.3 us (12%)
  between operations  15 us (8%)
  local copies, waits for them, and re-layouts  4.52 us (3%)
    pallas_call x2, Pallas kernels, mlp(): pl.pallas_call(functools.partial(mlp_kernel, len(after)), out_shape=(jax....  39 us
    ppermute x4, waiting for transfers between devices, to_pair(): return lax.ppermute(value, 'dp', pairs)  36.8 us
    pallas_call x2, Pallas kernels, attend(): pl.pallas_call(functools.partial(attend_kernel, len(after)), out_shape=ja...  17.7 us
    pallas_call x4, Pallas kernels, choose(): pl.pallas_call(functools.partial(choose_kernel, parts, len(sources)), out...  11.6 us
    ppermute x7, starting transfers between devices, swap(): return lax.ppermute(value, 'tensor', [(0, 1), (1, 0)])  8.68 us
    ppermute x7, waiting for transfers between devices, swap(): return lax.ppermute(value, 'tensor', [(0, 1), (1, 0)])  7.71 us
    pallas_call x1, Pallas kernels, merge(): pl.pallas_call(functools.partial(merge_kernel, kept_count.shape[0]), out_...  7.04 us
    ppermute x4, starting transfers between devices, to_pair(): return lax.ppermute(value, 'dp', pairs)  6.75 us
  transfers between devices with their start and end apart: 24, of which 9 were waited for; matrix products, arithmetic and copies ran while one was open for 2% of the time, Pallas kernels for 38%

profile of v4, /device:TPU:0, one launch (start us, length us, event | category | flops | bytes accessed | tf_op | source)
XLA Modules:
  0.0 179.9 jit_solution(10746564710627139217)
XLA Ops:
  6.5 5.5 %pack.1 = (bf16[8,64,1792]{2,1,0:T(8,128)(2,1)}, bf16[8,64,1792]{2,1,0:T(8,128)(2,1)S(1)}) custom-call(s32[1]{0:T(128)} %bitcast.19.device_ref, s32[8]{0:T(128)} %count_ref.5, s32[16]{0:T(128)} %bitcast.44, bf16[64,16,1792]{2,1,0:T(8,128)(2,1)} %bitcast.42), custom_call_target="tpu_custom_call" | custom-call | tf_op jit(solution)/shard_map/pack/pallas_call | solution.py:224
  12.5 1.3 w_piece.1
  13.7 2.6 %collective-permute-start.6 = (bf16[224,1792]{1,0:T(8,128)(2,1)S(1)}, bf16[224,1792]{1,0:T(8,128)(2,1)S(1)}, u32[]{:S(2)}, u32[]{:S(2)}) collective-permute-start(bf16[224,1792]{1,0:T(8,128)(2,1)S(1)} %w_piece.1), channel_id=1, source_target_pairs={{0,1},{1,0},{2,3},{3,2},{4,5},{5,4},{6,7},{7,6},{8,9},{9,8},{10,11... | collective-permute-start | bytes 2408456 | tf_op jit(solution)/shard_map/ppermute | solution.py:660
  16.3 2.0 %plan.1.table_ref = s32[94]{0:T(128)S(1)} custom-call(s32[1]{0:T(128)} %bitcast.19.device_ref, s32[8]{0:T(128)} %count_ref.5), custom_call_target="tpu_custom_call" | custom-call | flops 1000 | bytes 1000 | tf_op jit(solution)/shard_map/plan/pallas_call | solution.py:166
  18.3 4.4 %send.1 = (bf16[3,64,1792]{2,1,0:T(8,128)(2,1)S(1)}, bf16[2,64,1792]{2,1,0:T(8,128)(2,1)}, bf16[3,64,1792]{2,1,0:T(8,128)(2,1)S(1)}, bf16[2,64,1792]{2,1,0:T(8,128)(2,1)}) custom-call(s32[94]{0:T(128)S(1)} %plan.1.table_ref, bf16[8,64,1792]{2,1,0:T(8,128)(2,1)S(1)} %copy-done.3, bf16[8,64,1792]{2,1,0:T(8,128)(2,1)} %collective-permute-done.1.refs_1_), custom_call_target="tpu_custom_call" | custom-call | flops 1000 | bytes 1000 | tf_op jit(solution)/shard_map/send/pallas_call | solution.py:352
  25.1 3.3 %collective-permute-start = (f32[1]{0:T(128)}, f32[1]{0:T(128)}, u32[]{:S(2)}, u32[]{:S(2)}) collective-permute-start(f32[1]{0:T(128)} %convert_element_type.8), channel_id=1, source_target_pairs={{0,16},{16,0},{1,17},{17,1},{2,18},{18,2},{3,19},{19,3},{4,20},{20... | collective-permute-start | bytes 20 | tf_op jit(solution)/shard_map/ppermute | solution.py:795
  29.4 11.0 %collective-permute-done.2 = bf16[3,64,1792]{2,1,0:T(8,128)(2,1)} collective-permute-done((bf16[3,64,1792]{2,1,0:T(8,128)(2,1)S(1)}, bf16[3,64,1792]{2,1,0:T(8,128)(2,1)}, u32[]{:S(2)}, u32[]{:S(2)}) %collective-permute-start.2) | collective-permute-done | bytes 688160 | tf_op jit(solution)/shard_map/ppermute | solution.py:785
  40.4 1.7 conditional.3
  40.4 1.7 deal_0.1
  42.3 1.0 w_near.1
  43.2 1.6 collective-permute-start.7
  45.4 1.7 collective-permute-start.8
  49.9 7.5 %collective-permute-done.8 = bf16[2,64,1792]{2,1,0:T(8,128)(2,1)S(1)} collective-permute-done((bf16[2,64,1792]{2,1,0:T(8,128)(2,1)}, bf16[2,64,1792]{2,1,0:T(8,128)(2,1)S(1)}, u32[]{:S(2)}, u32[]{:S(2)}) %collective-permute-start.8) | collective-permute-done | bytes 458784 | tf_op jit(solution)/shard_map/ppermute | solution.py:785
  57.4 2.6 %conditional.4 = (bf16[2,64,1792]{2,1,0:T(8,128)(2,1)S(1)}) conditional(s32[]{:T(128)} %convert_element_type.9, (s32[94]{0:T(128)S(1)}, bf16[8,64,1792]{2,1,0:T(8,128)(2,1)}, bf16[8,64,1792]{2,1,0:T(8,128)(2,1)}, bf16[3,64,1792]{2,1,0:T(8,128)(2,1)}, bf16[2,64,1792]{2,1,0:T(8,128)(2,1)S(1)}, /*index=5*/bf16[3,64,1792]{2,1,0:T(8,128)(2,1)}, ...), branch_computations={%region_2.0_spmd, %region_3.0_spmd} | conditional | flops 230388 | bytes 61474012 | solution.py:828
  58.1 1.6 deal_1.1
  60.0 1.6 collective-permute-start.11
  61.5 1.1 collective-permute-done.7
  63.4 10.1 %attend.2.mine_ref = bf16[2,3,64,896]{3,2,1,0:T(8,128)(2,1)S(1)} custom-call(bf16[3,64,1792]{2,1,0:T(8,128)(2,1)S(1)} %get-tuple-element.133.own_ref.refs_1_, bf16[3,64,1792]{2,1,0:T(8,128)(2,1)S(1)} %collective-permute-done.4.other_ref, f32[6,1792]{1,0:T(8,128)S(1)} %stack.48.rows_ref, f32[3,896]{1,0:T(4,128)S(1)} %copy-done.2, bf16[3,1792,896]{2,1,0:T(8,128)(2,1)} %w_ref.5), custom_call_target="tpu_custom_call" | custom-call | flops 14797504512 | bytes 9633792 | tf_op jit(solution)/shard_map/attend/pallas_call | solution.py:483
  73.9 7.6 %attend.3.refs_0_.mine_ref = bf16[2,2,64,896]{3,2,1,0:T(8,128)(2,1)S(1)} custom-call(bf16[2,64,1792]{2,1,0:T(8,128)(2,1)S(1)} %get-tuple-element.134.refs_2_.own_ref, bf16[2,64,1792]{2,1,0:T(8,128)(2,1)S(1)} %collective-permute-done.11.other_ref, f32[6,1792]{1,0:T(8,128)S(1)} %stack.48.rows_ref, f32[3,896]{1,0:T(4,128)S(1)} %copy-done.2, ...), custom_call_target="tpu_custom_call" | custom-call | flops 9865003008 | bytes 9633792 | tf_op jit(solution)/shard_map/attend/pallas_call | solution.py:483
  81.5 1.8 collective-permute-start.13
  84.2 7.7 %collective-permute-done.5.theirs_ref = bf16[2,3,64,896]{3,2,1,0:T(8,128)(2,1)S(1)} collective-permute-done((bf16[2,3,64,896]{3,2,1,0:T(8,128)(2,1)S(1)}, bf16[2,3,64,896]{3,2,1,0:T(8,128)(2,1)S(1)}, u32[]{:S(2)}, u32[]{:S(2)}) %collective-permute-start.5) | collective-permute-done | bytes 688160 | tf_op jit(solution)/shard_map/ppermute | solution.py:660
  91.9 22.4 %mlp.2 = (f32[3,64,1792]{2,1,0:T(8,128)S(1)}, bf16[3,64,1792]{2,1,0:T(8,128)(2,1)S(1)}) custom-call(bf16[3,64,1792]{2,1,0:T(8,128)(2,1)S(1)} %get-tuple-element.133.own_ref.refs_1_, bf16[3,64,1792]{2,1,0:T(8,128)(2,1)S(1)} %collective-permute-done.4.other_ref, bf16[2,3,64,896]{3,2,1,0:T(8,128)(2,1)S(1)} %attend.2.mine_ref, ...), custom_call_target="tpu_custom_call" | custom-call | flops 30299652096 | bytes 39452672 | tf_op jit(solution)/shard_map/mlp/pallas_call | solution.py:609
  114.7 16.6 %mlp.3 = (f32[2,64,1792]{2,1,0:T(8,128)S(1)}, bf16[2,64,1792]{2,1,0:T(8,128)(2,1)S(1)}) custom-call(bf16[2,64,1792]{2,1,0:T(8,128)(2,1)S(1)} %get-tuple-element.134.refs_2_.own_ref, bf16[2,64,1792]{2,1,0:T(8,128)(2,1)S(1)} %collective-permute-done.11.other_ref, bf16[2,2,64,896]{3,2,1,0:T(8,128)(2,1)S(1)} %attend.3.refs_0_.mine_ref, ...), custom_call_target="tpu_custom_call" | custom-call | flops 20199768064 | bytes 39452672 | tf_op jit(solution)/shard_map/mlp/pallas_call | solution.py:609
  131.3 1.0 add.61.refs_0_.refs_3_.refs_5_.refs_9_.refs_11_
  132.2 2.3 %collective-permute-start.15 = (bf16[3,64,1792]{2,1,0:T(8,128)(2,1)}, bf16[3,64,1792]{2,1,0:T(8,128)(2,1)S(1)}, u32[]{:S(2)}, u32[]{:S(2)}) collective-permute-start(bf16[3,64,1792]{2,1,0:T(8,128)(2,1)} %add.61.refs_0_.refs_3_.refs_5_.refs_9_.refs_11_), channel_id=1, source_target_pairs={{0,4},{2,6},{4,0},{6,2},{8,12},{10,14},{12,8},{14,10},{1,5},{3,7},... | collective-permute-start | bytes 2064392 | tf_op jit(solution)/shard_map/ppermute | solution.py:785
  135.1 1.5 collective-permute-start.14
  136.6 11.8 %collective-permute-done.15.refs_0_.refs_2_ = bf16[3,64,1792]{2,1,0:T(8,128)(2,1)S(1)} collective-permute-done((bf16[3,64,1792]{2,1,0:T(8,128)(2,1)}, bf16[3,64,1792]{2,1,0:T(8,128)(2,1)S(1)}, u32[]{:S(2)}, u32[]{:S(2)}) %collective-permute-start.15) | collective-permute-done | bytes 688160 | tf_op jit(solution)/shard_map/ppermute | solution.py:785
  149.8 1.9 %collective-permute-start.21 = (bf16[2,64,1792]{2,1,0:T(8,128)(2,1)}, bf16[2,64,1792]{2,1,0:T(8,128)(2,1)S(1)}, u32[]{:S(2)}, u32[]{:S(2)}) collective-permute-start(bf16[2,64,1792]{2,1,0:T(8,128)(2,1)} %add.62.refs_1_), channel_id=1, source_target_pairs={{0,4},{2,6},{4,0},{6,2},{8,12},{10,14},{12,8},{14,10},{1,5},{3,7},... | collective-permute-start | bytes 1376264 | tf_op jit(solution)/shard_map/ppermute | solution.py:785
  152.4 3.9 %gather.11.refs_2_.found_ref = bf16[16,64,1792]{2,1,0:T(8,128)(2,1)S(1)} custom-call(s32[16]{0:T(128)S(1)} %broadcast_select_fusion.2.table_ref.code_ref, bf16[3,64,1792]{2,1,0:T(8,128)(2,1)} %add.61.refs_0_.refs_3_.refs_5_.refs_9_.refs_11_, bf16[2,64,1792]{2,1,0:T(8,128)(2,1)} %add.62.refs_1_, ...), custom_call_target="tpu_custom_call" | custom-call | flops 1000 | bytes 1000 | tf_op jit(solution)/shard_map/gather/pallas_call | solution.py:352
  156.3 6.6 %collective-permute-done.21.refs_0_ = bf16[2,64,1792]{2,1,0:T(8,128)(2,1)S(1)} collective-permute-done((bf16[2,64,1792]{2,1,0:T(8,128)(2,1)}, bf16[2,64,1792]{2,1,0:T(8,128)(2,1)S(1)}, u32[]{:S(2)}, u32[]{:S(2)}) %collective-permute-start.21) | collective-permute-done | bytes 458784 | tf_op jit(solution)/shard_map/ppermute | solution.py:785
  163.5 2.5 %collective-permute-done.23 = bf16[2,2,64,1792]{3,2,1,0:T(8,128)(2,1)S(1)} collective-permute-done((bf16[2,2,64,1792]{3,2,1,0:T(8,128)(2,1)S(1)}, bf16[2,2,64,1792]{3,2,1,0:T(8,128)(2,1)S(1)}, u32[]{:S(2)}, u32[]{:S(2)}) %collective-permute-start.23) | collective-permute-done | bytes 917536 | tf_op jit(solution)/shard_map/ppermute | solution.py:782
  166.0 7.0 %merge.1 = bf16[64,16,1792]{2,1,0:T(8,128)(2,1)} custom-call(s32[1]{0:T(128)} %bitcast.19.device_ref, s32[8]{0:T(128)} %count_ref.5, s32[16]{0:T(128)} %bitcast.45, s32[16]{0:T(128)S(1)} %broadcast_select_fusion.2.table_ref.code_ref, bf16[64,16,1792]{2,1,0:T(8,128)(2,1)} %bitcast.43, bf16[16,64,1792]{2,1,0:T(8,128)(2,1)S(1)} %gather.11.refs_2_.found_ref, ...), custom_call_target="tpu_custom_call" | custom-call | flops 1000 | bytes 1000 | tf_op jit(solution)/shard_map/merge/pallas_call | solution.py:297
  (72 shorter events, 12.2 us)
Async XLA Ops:
  12.0 6.3 %collective-permute-start.1 = (bf16[8,64,1792]{2,1,0:T(8,128)(2,1)S(1)}, bf16[8,64,1792]{2,1,0:T(8,128)(2,1)}, u32[]{:S(2)}, u32[]{:S(2)}) collective-permute-start(bf16[8,64,1792]{2,1,0:T(8,128)(2,1)S(1)} %get-tuple-element.95.refs_0_), channel_id=1, source_target_pairs={{0,2},{2,0},{4,6},{6,4},{8,10},{10,8},{12,14},{14,12},{1,3},{3,1},... | collective-permute-start | bytes 5505032 | tf_op jit(solution)/shard_map/ppermute | solution.py:782
  12.5 5.9 %copy-start.3 = (bf16[8,64,1792]{2,1,0:T(8,128)(2,1)S(1)}, bf16[8,64,1792]{2,1,0:T(8,128)(2,1)}, u32[]{:S(2)}) copy-start(bf16[8,64,1792]{2,1,0:T(8,128)(2,1)} %get-tuple-element.94.refs_0_) | copy-start | bytes 5505028
  13.7 28.5 %collective-permute-start.6 = (bf16[224,1792]{1,0:T(8,128)(2,1)S(1)}, bf16[224,1792]{1,0:T(8,128)(2,1)S(1)}, u32[]{:S(2)}, u32[]{:S(2)}) collective-permute-start(bf16[224,1792]{1,0:T(8,128)(2,1)S(1)} %w_piece.1), channel_id=1, source_target_pairs={{0,1},{1,0},{2,3},{3,2},{4,5},{5,4},{6,7},{7,6},{8,9},{9,8},{10,11... | collective-permute-start | bytes 2408456 | tf_op jit(solution)/shard_map/ppermute | solution.py:660
  18.3 39.0 %copy-start.5 = (s32[94]{0:T(128)}, s32[94]{0:T(128)S(1)}, u32[]{:S(2)}) copy-start(s32[94]{0:T(128)S(1)} %plan.1.table_ref) | copy-start | bytes 1132
  22.7 17.7 %collective-permute-start.2 = (bf16[3,64,1792]{2,1,0:T(8,128)(2,1)S(1)}, bf16[3,64,1792]{2,1,0:T(8,128)(2,1)}, u32[]{:S(2)}, u32[]{:S(2)}) collective-permute-start(bf16[3,64,1792]{2,1,0:T(8,128)(2,1)S(1)} %get-tuple-element.96), channel_id=1, source_target_pairs={{0,4},{2,6},{4,0},{6,2},{8,12},{10,14},{12,8},{14,10},{1,5},{3,7},... | collective-permute-start | bytes 2064392 | tf_op jit(solution)/shard_map/ppermute | solution.py:785
  23.6 16.9 %collective-permute-start.3 = (bf16[3,64,1792]{2,1,0:T(8,128)(2,1)S(1)}, bf16[3,64,1792]{2,1,0:T(8,128)(2,1)}, u32[]{:S(2)}, u32[]{:S(2)}) collective-permute-start(bf16[3,64,1792]{2,1,0:T(8,128)(2,1)S(1)} %get-tuple-element.97), channel_id=1, source_target_pairs={{0,2},{2,0},{4,8},{6,10},{8,4},{10,6},{12,14},{14,12},{1,3},{3,1},... | collective-permute-start | bytes 2064392 | tf_op jit(solution)/shard_map/ppermute | solution.py:788
  25.1 3.7 %collective-permute-start = (f32[1]{0:T(128)}, f32[1]{0:T(128)}, u32[]{:S(2)}, u32[]{:S(2)}) collective-permute-start(f32[1]{0:T(128)} %convert_element_type.8), channel_id=1, source_target_pairs={{0,16},{16,0},{1,17},{17,1},{2,18},{18,2},{3,19},{19,3},{4,20},{20... | collective-permute-start | bytes 20 | tf_op jit(solution)/shard_map/ppermute | solution.py:795
  42.2 5.0 %copy-start.10 = (f32[1792]{0:T(1024)S(1)}, f32[1792]{0:T(1024)}, u32[]{:S(2)}) copy-start(f32[1792]{0:T(1024)} %param.32) | copy-start | bytes 21508
  42.2 5.0 %copy-start.11 = (f32[1792]{0:T(1024)S(1)}, f32[1792]{0:T(1024)}, u32[]{:S(2)}) copy-start(f32[1792]{0:T(1024)} %param.33) | copy-start | bytes 21508
  42.2 5.6 %copy-start.12 = (f32[1792]{0:T(1024)S(1)}, f32[1792]{0:T(1024)}, u32[]{:S(2)}) copy-start(f32[1792]{0:T(1024)} %param.31) | copy-start | bytes 21508
  42.2 6.2 %copy-start.13 = (f32[1792]{0:T(1024)S(1)}, f32[1792]{0:T(1024)}, u32[]{:S(2)}) copy-start(f32[1792]{0:T(1024)} %param.37) | copy-start | bytes 21508
  42.2 6.8 %copy-start.7 = (f32[4608]{0:T(1024)S(1)}, f32[4608]{0:T(1024)}, u32[]{:S(2)}) copy-start(f32[4608]{0:T(1024)} %param.35) | copy-start | bytes 55300
  43.2 19.4 %collective-permute-start.7 = (bf16[1,224,1792]{2,1,0:T(8,128)(2,1)}, bf16[1,224,1792]{2,1,0:T(8,128)(2,1)S(1)}, u32[]{:S(2)}, u32[]{:S(2)}) collective-permute-start(bf16[1,224,1792]{2,1,0:T(8,128)(2,1)} %w_near.1), channel_id=1, source_target_pairs={{0,16},{16,0},{1,17},{17,1},{2,18},{18,2},{3,19},{19,3},{4,20},{20... | collective-permute-start | bytes 2408456 | tf_op jit(solution)/shard_map/ppermute | solution.py:851
  44.8 18.1 %collective-permute-start.4 = (bf16[3,64,1792]{2,1,0:T(8,128)(2,1)S(1)}, bf16[3,64,1792]{2,1,0:T(8,128)(2,1)S(1)}, u32[]{:S(2)}, u32[]{:S(2)}) collective-permute-start(bf16[3,64,1792]{2,1,0:T(8,128)(2,1)S(1)} %get-tuple-element.133.own_ref.refs_1_), channel_id=1, source_target_pairs={{0,1},{1,0},{2,3},{3,2},{4,5},{5,4},{6,7},{7,6},{8,9},{9,8},{10,11... | collective-permute-start | bytes 2064392 | tf_op jit(solution)/shard_map/ppermute | solution.py:660
  45.4 12.0 %collective-permute-start.8 = (bf16[2,64,1792]{2,1,0:T(8,128)(2,1)}, bf16[2,64,1792]{2,1,0:T(8,128)(2,1)S(1)}, u32[]{:S(2)}, u32[]{:S(2)}) collective-permute-start(bf16[2,64,1792]{2,1,0:T(8,128)(2,1)} %get-tuple-element.98), channel_id=1, source_target_pairs={{0,4},{2,6},{4,0},{6,2},{8,12},{10,14},{12,8},{14,10},{1,5},{3,7},... | collective-permute-start | bytes 1376264 | tf_op jit(solution)/shard_map/ppermute | solution.py:785
  47.1 10.2 %collective-permute-start.9 = (bf16[2,64,1792]{2,1,0:T(8,128)(2,1)}, bf16[2,64,1792]{2,1,0:T(8,128)(2,1)}, u32[]{:S(2)}, u32[]{:S(2)}) collective-permute-start(bf16[2,64,1792]{2,1,0:T(8,128)(2,1)} %get-tuple-element.99), channel_id=1, source_target_pairs={{0,2},{2,0},{4,8},{6,10},{8,4},{10,6},{12,14},{14,12},{1,3},{3,1},... | collective-permute-start | bytes 1376264 | tf_op jit(solution)/shard_map/ppermute | solution.py:788
  60.0 13.9 %collective-permute-start.11 = (bf16[2,64,1792]{2,1,0:T(8,128)(2,1)S(1)}, bf16[2,64,1792]{2,1,0:T(8,128)(2,1)S(1)}, u32[]{:S(2)}, u32[]{:S(2)}) collective-permute-start(bf16[2,64,1792]{2,1,0:T(8,128)(2,1)S(1)} %get-tuple-element.134.refs_2_.own_ref), channel_id=1, source_target_pairs={{0,1},{1,0},{2,3},{3,2},{4,5},{5,4},{6,7},{7,6},{8,9},{9,8},{10,11... | collective-permute-start | bytes 1376264 | tf_op jit(solution)/shard_map/ppermute | solution.py:660
  62.8 20.5 %collective-permute-start.10 = (bf16[2,224,1792]{2,1,0:T(8,128)(2,1)S(1)}, bf16[2,224,1792]{2,1,0:T(8,128)(2,1)S(1)}, u32[]{:S(2)}, u32[]{:S(2)}) collective-permute-start(bf16[2,224,1792]{2,1,0:T(8,128)(2,1)S(1)} %w_both.1), channel_id=1, source_target_pairs={{0,2},{2,0},{4,6},{6,4},{8,10},{10,8},{12,14},{14,12},{1,3},{3,1},... | collective-permute-start | bytes 4816904 | tf_op jit(solution)/shard_map/ppermute | solution.py:724
  73.5 18.4 %collective-permute-start.5 = (bf16[2,3,64,896]{3,2,1,0:T(8,128)(2,1)S(1)}, bf16[2,3,64,896]{3,2,1,0:T(8,128)(2,1)S(1)}, u32[]{:S(2)}, u32[]{:S(2)}) collective-permute-start(bf16[2,3,64,896]{3,2,1,0:T(8,128)(2,1)S(1)} %attend.2.mine_ref), channel_id=1, source_target_pairs={{0,1},{1,0},{2,3},{3,2},{4,5},{5,4},{6,7},{7,6},{8,9},{9,8},{10,11... | collective-permute-start | bytes 2064392 | tf_op jit(solution)/shard_map/ppermute | solution.py:660
  81.5 33.2 %collective-permute-start.13 = (bf16[2,2,64,896]{3,2,1,0:T(8,128)(2,1)S(1)}, bf16[2,2,64,896]{3,2,1,0:T(8,128)(2,1)S(1)}, u32[]{:S(2)}, u32[]{:S(2)}) collective-permute-start(bf16[2,2,64,896]{3,2,1,0:T(8,128)(2,1)S(1)} %attend.3.refs_0_.mine_ref), channel_id=1, source_target_pairs={{0,1},{1,0},{2,3},{3,2},{4,5},{5,4},{6,7},{7,6},{8,9},{9,8},{10,11... | collective-permute-start | bytes 1376264 | tf_op jit(solution)/shard_map/ppermute | solution.py:660
  114.3 16.9 %collective-permute-start.12 = (bf16[3,64,1792]{2,1,0:T(8,128)(2,1)S(1)}, bf16[3,64,1792]{2,1,0:T(8,128)(2,1)S(1)}, u32[]{:S(2)}, u32[]{:S(2)}) collective-permute-start(bf16[3,64,1792]{2,1,0:T(8,128)(2,1)S(1)} %get-tuple-element.101), channel_id=1, source_target_pairs={{0,1},{1,0},{2,3},{3,2},{4,5},{5,4},{6,7},{7,6},{8,9},{9,8},{10,11... | collective-permute-start | bytes 2064392 | tf_op jit(solution)/shard_map/ppermute | solution.py:660
  132.2 19.5 %copy-start.6 = (s32[94]{0:T(128)S(1)}, s32[94]{0:T(128)}, u32[]{:S(2)}) copy-start(s32[94]{0:T(128)} %copy-done.5) | copy-start | bytes 1132
  132.2 16.1 %collective-permute-start.15 = (bf16[3,64,1792]{2,1,0:T(8,128)(2,1)}, bf16[3,64,1792]{2,1,0:T(8,128)(2,1)S(1)}, u32[]{:S(2)}, u32[]{:S(2)}) collective-permute-start(bf16[3,64,1792]{2,1,0:T(8,128)(2,1)} %add.61.refs_0_.refs_3_.refs_5_.refs_9_.refs_11_), channel_id=1, source_target_pairs={{0,4},{2,6},{4,0},{6,2},{8,12},{10,14},{12,8},{14,10},{1,5},{3,7},... | collective-permute-start | bytes 2064392 | tf_op jit(solution)/shard_map/ppermute | solution.py:785
  134.6 13.8 %collective-permute-start.16 = (bf16[3,64,1792]{2,1,0:T(8,128)(2,1)}, bf16[3,64,1792]{2,1,0:T(8,128)(2,1)S(1)}, u32[]{:S(2)}, u32[]{:S(2)}) collective-permute-start(bf16[3,64,1792]{2,1,0:T(8,128)(2,1)} %add.61.refs_0_.refs_3_.refs_5_.refs_9_.refs_11_), channel_id=1, source_target_pairs={{0,2},{2,0},{4,8},{6,10},{8,4},{10,6},{12,14},{14,12},{1,3},{3,1},... | collective-permute-start | bytes 2064392 | tf_op jit(solution)/shard_map/ppermute | solution.py:788
  134.6 17.1 %collective-permute-start.17 = (bf16[3,64,1792]{2,1,0:T(8,128)(2,1)}, bf16[3,64,1792]{2,1,0:T(8,128)(2,1)S(1)}, u32[]{:S(2)}, u32[]{:S(2)}) collective-permute-start(bf16[3,64,1792]{2,1,0:T(8,128)(2,1)} %add.61.refs_0_.refs_3_.refs_5_.refs_9_.refs_11_), channel_id=1, source_target_pairs={{0,2},{2,0},{4,6},{6,4},{8,10},{10,8},{12,14},{14,12},{1,3},{3,1},... | collective-permute-start | bytes 2064392 | tf_op jit(solution)/shard_map/ppermute | solution.py:782
  135.1 13.8 %collective-permute-start.14 = (bf16[2,64,1792]{2,1,0:T(8,128)(2,1)S(1)}, bf16[2,64,1792]{2,1,0:T(8,128)(2,1)S(1)}, u32[]{:S(2)}, u32[]{:S(2)}) collective-permute-start(bf16[2,64,1792]{2,1,0:T(8,128)(2,1)S(1)} %get-tuple-element.103), channel_id=1, source_target_pairs={{0,1},{1,0},{2,3},{3,2},{4,5},{5,4},{6,7},{7,6},{8,9},{9,8},{10,11... | collective-permute-start | bytes 1376264 | tf_op jit(solution)/shard_map/ppermute | solution.py:660
  148.4 4.0 %collective-permute-start.19 = (bf16[3,64,1792]{2,1,0:T(8,128)(2,1)S(1)}, bf16[3,64,1792]{2,1,0:T(8,128)(2,1)}, u32[]{:S(2)}, u32[]{:S(2)}) collective-permute-start(bf16[3,64,1792]{2,1,0:T(8,128)(2,1)S(1)} %collective-permute-done.15.refs_0_.refs_2_), channel_id=1, source_target_pairs={{0,2},{2,0},{4,6},{6,4},{8,10},{10,8},{12,14},{14,12},{1,3},{3,1},... | collective-permute-start | bytes 2064392 | tf_op jit(solution)/shard_map/ppermute | solution.py:782
  148.4 4.0 %collective-permute-start.20 = (bf16[3,64,1792]{2,1,0:T(8,128)(2,1)S(1)}, bf16[3,64,1792]{2,1,0:T(8,128)(2,1)}, u32[]{:S(2)}, u32[]{:S(2)}) collective-permute-start(bf16[3,64,1792]{2,1,0:T(8,128)(2,1)S(1)} %collective-permute-done.16.refs_1_.refs_4_), channel_id=1, source_target_pairs={{0,2},{2,0},{4,6},{6,4},{8,10},{10,8},{12,14},{14,12},{1,3},{3,1},... | collective-permute-start | bytes 2064392 | tf_op jit(solution)/shard_map/ppermute | solution.py:782
  149.7 2.6 %collective-permute-start.18 = (bf16[2,64,1792]{2,1,0:T(8,128)(2,1)}, bf16[2,64,1792]{2,1,0:T(8,128)(2,1)S(1)}, u32[]{:S(2)}, u32[]{:S(2)}) collective-permute-start(bf16[2,64,1792]{2,1,0:T(8,128)(2,1)} %add.62.refs_1_), channel_id=1, source_target_pairs={{0,2},{2,0},{4,6},{6,4},{8,10},{10,8},{12,14},{14,12},{1,3},{3,1},... | collective-permute-start | bytes 1376264 | tf_op jit(solution)/shard_map/ppermute | solution.py:782
  149.8 13.1 %collective-permute-start.21 = (bf16[2,64,1792]{2,1,0:T(8,128)(2,1)}, bf16[2,64,1792]{2,1,0:T(8,128)(2,1)S(1)}, u32[]{:S(2)}, u32[]{:S(2)}) collective-permute-start(bf16[2,64,1792]{2,1,0:T(8,128)(2,1)} %add.62.refs_1_), channel_id=1, source_target_pairs={{0,4},{2,6},{4,0},{6,2},{8,12},{10,14},{12,8},{14,10},{1,5},{3,7},... | collective-permute-start | bytes 1376264 | tf_op jit(solution)/shard_map/ppermute | solution.py:785
  151.6 11.3 %collective-permute-start.22 = (bf16[2,64,1792]{2,1,0:T(8,128)(2,1)}, bf16[2,64,1792]{2,1,0:T(8,128)(2,1)S(1)}, u32[]{:S(2)}, u32[]{:S(2)}) collective-permute-start(bf16[2,64,1792]{2,1,0:T(8,128)(2,1)} %add.62.refs_1_), channel_id=1, source_target_pairs={{0,2},{2,0},{4,8},{6,10},{8,4},{10,6},{12,14},{14,12},{1,3},{3,1},... | collective-permute-start | bytes 1376264 | tf_op jit(solution)/shard_map/ppermute | solution.py:788
  163.5 2.5 %collective-permute-start.23 = (bf16[2,2,64,1792]{3,2,1,0:T(8,128)(2,1)S(1)}, bf16[2,2,64,1792]{3,2,1,0:T(8,128)(2,1)S(1)}, u32[]{:S(2)}, u32[]{:S(2)}) collective-permute-start(bf16[2,2,64,1792]{3,2,1,0:T(8,128)(2,1)S(1)} %late.1), channel_id=1, source_target_pairs={{0,2},{2,0},{4,6},{6,4},{8,10},{10,8},{12,14},{14,12},{1,3},{3,1},... | collective-permute-start | bytes 2752520 | tf_op jit(solution)/shard_map/ppermute | solution.py:782
  (4 other events, 11.4 us)

commit v5 on v4

--- a/solution.py
+++ b/solution.py
@@ -499,12 +499,50 @@
     )(own, other, rows_params, b_qkv, in_hbm(w_qkv), *after)
 
 
+def project_kernel(n_after, attended_ref, w_ref, *refs):
+    out_ref, held, sems = refs[n_after:]
+    sides, blocks, rows, span = attended_ref.shape
+    width = held.shape[1]
+    half = span // 2
+    loads = [
+        pltpu.make_async_copy(
+            w_ref.at[pl.ds(part * half, half), :], held.at[pl.ds(part * half, half), :], sems.at[part]
+        )
+        for part in range(2)
+    ]
+    for load in loads:
+        load.start()
+    for load in loads:
+        load.wait()
+    attended = attended_ref[...].reshape(sides * blocks * rows, span)
+    for column in range(0, width, 256):
+        columns = slice(column, column + 256)
+        part = jnp.dot(attended, held[:, columns], preferred_element_type=F32)
+        out_ref[:, :, :, columns] = part.astype(BF16).reshape(sides, blocks, rows, 256)
+
+
+def project(attended, w_out, after=()):
+    sides, blocks, rows, span = attended.shape
+    width = w_out.shape[1]
+    vmem = pl.BlockSpec(memory_space=pltpu.VMEM)
+    return pl.pallas_call(
+        functools.partial(project_kernel, len(after)),
+        out_shape=jax.ShapeDtypeStruct((sides, blocks, rows, width), BF16),
+        in_specs=[vmem] + [pl.BlockSpec(memory_space=pl.ANY)] * (1 + len(after)),
+        out_specs=vmem,
+        scratch_shapes=[pltpu.VMEM((span, width), BF16), pltpu.SemaphoreType.DMA((2,))],
+        compiler_params=pltpu.CompilerParams(vmem_limit_bytes=16 * MIB),
+        cost_estimate=SMALL_COST,
+        name="project",
+    )(attended, in_hbm(w_out), *after)
+
+
 UP_TILE = 768
 DOWN_TILE = 256
 SLOTS = 4
 
 
-def mlp_kernel(n_after, own_ref, other_ref, mine_ref, theirs_ref, rows_ref, b_up_ref, w_mine, w_theirs,
+def mlp_kernel(n_after, given, own_ref, other_ref, mine_ref, theirs_ref, rows_ref, b_up_ref, w_mine, w_theirs,
                w_up, w_down, *refs):
     (keep_ref, send_ref, residual, renormed, hidden, outs, ups, downs, out_sems, up_sems,
      down_sems) = refs[n_after:]
@@ -527,22 +565,26 @@
         pltpu.make_async_copy(source, outs.at[number], out_sems.at[number])
         for number, source in enumerate((w_mine, w_theirs))
     ]
-    for load in out_loads:
+    for load in out_loads[given:]:
         load.start()
     load_up(jnp.int32(0)).start()
     gain, shift = rows_ref[2:3, :], rows_ref[3:4, :]
-    mine = mine_ref[...].reshape(2 * half, span)
+    mine = mine_ref[...].reshape(2 * half, mine_ref.shape[3])
     theirs = jnp.concatenate(
         [theirs_ref[1].reshape(half, span), theirs_ref[0].reshape(half, span)], axis=0
     )
     for number, attended in enumerate((mine, theirs)):
-        out_loads[number].wait()
+        if number >= given:
+            out_loads[number].wait()
         for slot in (range(1, 3), range(3, SLOTS))[number]:
             load_up(jnp.int32(slot)).start()
         for column in range(0, width, DOWN_TILE):
             columns = slice(column, column + DOWN_TILE)
-            part = jnp.dot(attended, outs[number, :, columns], preferred_element_type=F32)
-            part = part.astype(BF16).astype(F32)
+            if number < given:
+                part = attended[:, columns].astype(F32)
+            else:
+                part = jnp.dot(attended, outs[number, :, columns], preferred_element_type=F32)
+                part = part.astype(BF16).astype(F32)
             if number == 0:
                 residual[:, columns] = part + rows_ref[4:5, columns]
             else:
@@ -600,14 +642,15 @@
 
 def mlp(own, other, mine, theirs, rows_params, b_up, weights, after):
     blocks, rows, width = own.shape
-    span = mine.shape[3]
+    span = theirs.shape[3]
+    given = int(mine.shape[3] != span)
     total = 2 * blocks * rows
     vmem = pl.BlockSpec(memory_space=pltpu.VMEM)
     hbm = pl.BlockSpec(memory_space=pl.ANY)
     w_mine, w_theirs, w_up, w_down = weights
     hidden = w_up.shape[1]
     return pl.pallas_call(
-        functools.partial(mlp_kernel, len(after)),
+        functools.partial(mlp_kernel, len(after), given),
         out_shape=(
             jax.ShapeDtypeStruct((blocks, rows, width), F32),
             jax.ShapeDtypeStruct((blocks, rows, width), BF16),
@@ -795,7 +838,8 @@
         short = short + lax.ppermute(short, "groups", [(0, 1), (1, 0)])
     else:
         short = lax.pmax(short, "groups")
-    short = short[0] > 0
+    flag = short
+    short = flag[0] > 0
 
     parts = tuple(zip(STARTS, CHUNKS))
     sends = [(AT_PAIR + at, size) for at, size in parts] + [(AT_NEXT + at, size) for at, size in parts]
@@ -845,12 +889,14 @@
 
         blocks_0 = deal(0)
         state_0 = start(blocks_0, [])
-        w_sent = line_up([w_near], [blocks_0], "w_near")
+        w_sent = line_up([w_near], [flag], "w_near")
         blocks_1 = deal(1, [w_sent])
         state_1 = start(blocks_1, [])
         w_side = lax.ppermute(w_sent, "groups", [(0, 1), (1, 0)])[0]
         w_theirs = other_w_out(w_out, w_near, w_side, [blocks_1])
         weights = (w_out, w_theirs, w_up, w_down)
+        own, other, mine_0, theirs = state_0
+        state_0 = own, other, project(mine_0, w_out, [state_1[2]]), theirs
         done_0 = finish(state_0, [state_1[2]])
         done_1 = finish(state_1, [done_0[0]])
         results, from_pair, from_next = [], [], []

time: 180 us -> 183 us (1.017)
  waiting for transfers between devices: 49.1 us -> 43.5 us
  Pallas kernels: 88.6 us -> 93.9 us
  starting transfers between devices: 22.3 us -> 25.7 us
    ppermute x4, waiting for transfers between devices: 36.8 us -> 30.9 us  [to_pair(): return lax.ppermute(value, 'dp', pairs)]
    pallas_call x2 -> x3, Pallas kernels: 39 us -> 44 us  [the longest x2 40.5 us: mlp(): pl.pallas_call(functools.partial(mlp_kernel, len(after), given), out_shap...]
    ppermute x4, starting transfers between devices: 6.75 us -> 9.4 us  [to_pair(): return lax.ppermute(value, 'dp', pairs)]
    another operation x7, local copies, waits for them, and re-layouts: 2.62 us -> 0.12 us  [per_device(): jnp.stack([pre_gain, pre_shift, mlp_gain, mlp_shift, b_out, b_down])]
    unnamed x22 -> x26, local copies, waits for them, and re-layouts: 0.5 us -> 2.55 us
    ppermute x7, waiting for transfers between devices: 7.71 us -> 9.75 us  [swap(): return lax.ppermute(value, 'tensor', [(0, 1), (1, 0)])]
  transfers between devices with their start and end apart: 24 -> 24, of which waited for: 9 -> 9; matrix products, arithmetic and copies ran while one was open for 2% -> 0% of each run, Pallas kernels for 38% -> 43%
where the time goes in v5:
time: 183 us; the launch traced here: 182 us
  Pallas kernels  93.9 us (51%)
  waiting for transfers between devices  43.5 us (24%)
  starting transfers between devices  25.7 us (14%)
  between operations  15 us (8%)
  local copies, waits for them, and re-layouts  3.26 us (2%)
    pallas_call x2, Pallas kernels, mlp(): pl.pallas_call(functools.partial(mlp_kernel, len(after), given), out_shap...  40.5 us
    ppermute x4, waiting for transfers between devices, to_pair(): return lax.ppermute(value, 'dp', pairs)  30.9 us
    pallas_call x2, Pallas kernels, attend(): pl.pallas_call(functools.partial(attend_kernel, len(after)), out_shape=ja...  18.8 us
    pallas_call x4, Pallas kernels, choose(): pl.pallas_call(functools.partial(choose_kernel, parts, len(sources)), out...  10.6 us
    ppermute x7, waiting for transfers between devices, swap(): return lax.ppermute(value, 'tensor', [(0, 1), (1, 0)])  9.75 us
    ppermute x4, starting transfers between devices, to_pair(): return lax.ppermute(value, 'dp', pairs)  9.4 us
    ppermute x7, starting transfers between devices, swap(): return lax.ppermute(value, 'tensor', [(0, 1), (1, 0)])  9.26 us
    pallas_call x1, Pallas kernels, merge(): pl.pallas_call(functools.partial(merge_kernel, kept_count.shape[0]), out_...  7.03 us
  transfers between devices with their start and end apart: 24, of which 9 were waited for; matrix products, arithmetic and copies ran while one was open for 0% of the time, Pallas kernels for 43%

profile of v5, /device:TPU:0, one launch (start us, length us, event | category | flops | bytes accessed | tf_op | source)
XLA Modules:
  0.0 181.8 jit_solution(17882685810270088485)
XLA Ops:
  6.5 5.5 %pack.1 = (bf16[8,64,1792]{2,1,0:T(8,128)(2,1)}, bf16[8,64,1792]{2,1,0:T(8,128)(2,1)S(1)}) custom-call(s32[1]{0:T(128)} %bitcast.19.device_ref, s32[8]{0:T(128)} %count_ref.5, s32[16]{0:T(128)} %bitcast.44, bf16[64,16,1792]{2,1,0:T(8,128)(2,1)} %bitcast.42), custom_call_target="tpu_custom_call" | custom-call | tf_op jit(solution)/shard_map/pack/pallas_call | solution.py:224
  13.8 2.6 %collective-permute-start.7 = (bf16[224,1792]{1,0:T(8,128)(2,1)S(1)}, bf16[224,1792]{1,0:T(8,128)(2,1)S(1)}, u32[]{:S(2)}, u32[]{:S(2)}) collective-permute-start(bf16[224,1792]{1,0:T(8,128)(2,1)S(1)} %w_piece.1), channel_id=1, source_target_pairs={{0,1},{1,0},{2,3},{3,2},{4,5},{5,4},{6,7},{7,6},{8,9},{9,8},{10,11... | collective-permute-start | bytes 2408456 | tf_op jit(solution)/shard_map/ppermute | solution.py:703
  16.4 2.0 %plan.1.table_ref = s32[94]{0:T(128)S(1)} custom-call(s32[1]{0:T(128)} %bitcast.19.device_ref, s32[8]{0:T(128)} %count_ref.5), custom_call_target="tpu_custom_call" | custom-call | flops 1000 | bytes 1000 | tf_op jit(solution)/shard_map/plan/pallas_call | solution.py:166
  18.4 2.3 %send.1 = (bf16[3,64,1792]{2,1,0:T(8,128)(2,1)S(1)}, bf16[2,64,1792]{2,1,0:T(8,128)(2,1)S(1)}, bf16[3,64,1792]{2,1,0:T(8,128)(2,1)S(1)}, bf16[2,64,1792]{2,1,0:T(8,128)(2,1)S(1)}) custom-call(s32[94]{0:T(128)S(1)} %plan.1.table_ref, bf16[8,64,1792]{2,1,0:T(8,128)(2,1)S(1)} %copy-done.7, bf16[8,64,1792]{2,1,0:T(8,128)(2,1)} %collective-permute-done.1.refs_1_), custom_call_target="tpu_custom_call" | custom-call | flops 1000 | bytes 1000 | tf_op jit(solution)/shard_map/send/pallas_call | solution.py:352
  24.4 3.9 %collective-permute-start = (f32[1]{0:T(128)}, f32[1]{0:T(128)}, u32[]{:S(2)}, u32[]{:S(2)}) collective-permute-start(f32[1]{0:T(128)} %convert_element_type.8), channel_id=1, source_target_pairs={{0,16},{16,0},{1,17},{17,1},{2,18},{18,2},{3,19},{19,3},{4,20},{20... | collective-permute-start | bytes 20 | tf_op jit(solution)/shard_map/ppermute | solution.py:838
  29.2 5.7 %collective-permute-done.7.refs_0_.near = bf16[224,1792]{1,0:T(8,128)(2,1)S(1)} collective-permute-done((bf16[224,1792]{1,0:T(8,128)(2,1)S(1)}, bf16[224,1792]{1,0:T(8,128)(2,1)S(1)}, u32[]{:S(2)}, u32[]{:S(2)}) %collective-permute-start.7) | collective-permute-done | bytes 802848 | tf_op jit(solution)/shard_map/ppermute | solution.py:703
  35.9 1.8 %collective-permute-start.10 = (bf16[1,224,1792]{2,1,0:T(8,128)(2,1)}, bf16[1,224,1792]{2,1,0:T(8,128)(2,1)S(1)}, u32[]{:S(2)}, u32[]{:S(2)}) collective-permute-start(bf16[1,224,1792]{2,1,0:T(8,128)(2,1)} %w_near.1), channel_id=1, source_target_pairs={{0,16},{16,0},{1,17},{17,1},{2,18},{18,2},{3,19},{19,3},{4,20},{20... | collective-permute-start | bytes 2408456 | tf_op jit(solution)/shard_map/ppermute | solution.py:895
  37.7 1.9 %collective-permute-done.2 = bf16[3,64,1792]{2,1,0:T(8,128)(2,1)} collective-permute-done((bf16[3,64,1792]{2,1,0:T(8,128)(2,1)S(1)}, bf16[3,64,1792]{2,1,0:T(8,128)(2,1)}, u32[]{:S(2)}, u32[]{:S(2)}) %collective-permute-start.2) | collective-permute-done | bytes 688160 | tf_op jit(solution)/shard_map/ppermute | solution.py:828
  39.7 2.6 %conditional.3 = (bf16[3,64,1792]{2,1,0:T(8,128)(2,1)}) conditional(s32[]{:T(128)} %convert_element_type.9, (s32[94]{0:T(128)S(1)}, bf16[8,64,1792]{2,1,0:T(8,128)(2,1)}, bf16[8,64,1792]{2,1,0:T(8,128)(2,1)}, bf16[3,64,1792]{2,1,0:T(8,128)(2,1)}, bf16[3,64,1792]{2,1,0:T(8,128)(2,1)}) %tuple.25, (s32[94]{0:T(128)S(1)}, bf16[8,64,1792]{2,1,0:T(8,128)(2,1)}, ...), branch_computations={%region_0.0_spmd, %region_1.0_spmd} | conditional | flops 689146 | bytes 62391604 | solution.py:872
  39.8 2.6 %deal_0.1 = bf16[3,64,1792]{2,1,0:T(8,128)(2,1)} custom-call(s32[94]{0:T(128)S(1)} %get-tuple-element.58.table_ref, bf16[8,64,1792]{2,1,0:T(8,128)(2,1)} %get-tuple-element.60.refs_0_, bf16[8,64,1792]{2,1,0:T(8,128)(2,1)} %get-tuple-element.62.refs_1_, bf16[3,64,1792]{2,1,0:T(8,128)(2,1)} %get-tuple-element.63.refs_2_.refs_3_, ...), custom_call_target="tpu_custom_call" | custom-call | flops 1000 | bytes 1000 | tf_op jit(solution)/shard_map/cond/branch_0_fun/deal_0/pallas_call | solution.py:352
  43.0 2.2 %collective-permute-start.5 = (bf16[2,64,1792]{2,1,0:T(8,128)(2,1)S(1)}, bf16[2,64,1792]{2,1,0:T(8,128)(2,1)}, u32[]{:S(2)}, u32[]{:S(2)}) collective-permute-start(bf16[2,64,1792]{2,1,0:T(8,128)(2,1)S(1)} %copy-done.5), channel_id=1, source_target_pairs={{0,4},{2,6},{4,0},{6,2},{8,12},{10,14},{12,8},{14,10},{1,5},{3,7},... | collective-permute-start | bytes 1376264 | tf_op jit(solution)/shard_map/ppermute | solution.py:828
  45.5 9.9 %collective-permute-done.5 = bf16[2,64,1792]{2,1,0:T(8,128)(2,1)} collective-permute-done((bf16[2,64,1792]{2,1,0:T(8,128)(2,1)S(1)}, bf16[2,64,1792]{2,1,0:T(8,128)(2,1)}, u32[]{:S(2)}, u32[]{:S(2)}) %collective-permute-start.5) | collective-permute-done | bytes 458784 | tf_op jit(solution)/shard_map/ppermute | solution.py:828
  55.4 1.8 conditional.4
  55.4 1.6 deal_1.1
  57.2 1.7 collective-permute-start.8
  59.2 1.7 collective-permute-done.4.other_ref
  60.9 11.2 %attend.2.attended_ref = bf16[2,3,64,896]{3,2,1,0:T(8,128)(2,1)S(1)} custom-call(bf16[3,64,1792]{2,1,0:T(8,128)(2,1)} %get-tuple-element.133.own_ref, bf16[3,64,1792]{2,1,0:T(8,128)(2,1)S(1)} %collective-permute-done.4.other_ref, f32[6,1792]{1,0:T(8,128)S(1)} %stack.46.rows_ref, f32[3,896]{1,0:T(4,128)S(1)} %copy-done.6, bf16[3,1792,896]{2,1,0:T(8,128)(2,1)} %w_ref.6), custom_call_target="tpu_custom_call" | custom-call | flops 14797504512 | bytes 9633792 | tf_op jit(solution)/shard_map/attend/pallas_call | solution.py:483
  72.3 7.6 %attend.3.refs_0_.mine_ref = bf16[2,2,64,896]{3,2,1,0:T(8,128)(2,1)S(1)} custom-call(bf16[2,64,1792]{2,1,0:T(8,128)(2,1)S(1)} %get-tuple-element.134.own_ref.refs_2_, bf16[2,64,1792]{2,1,0:T(8,128)(2,1)S(1)} %collective-permute-done.8.other_ref, f32[6,1792]{1,0:T(8,128)S(1)} %stack.46.rows_ref, f32[3,896]{1,0:T(4,128)S(1)} %copy-done.6, ...), custom_call_target="tpu_custom_call" | custom-call | flops 9865003008 | bytes 9633792 | tf_op jit(solution)/shard_map/attend/pallas_call | solution.py:483
  79.9 2.0 %collective-permute-start.13 = (bf16[2,2,64,896]{3,2,1,0:T(8,128)(2,1)S(1)}, bf16[2,2,64,896]{3,2,1,0:T(8,128)(2,1)S(1)}, u32[]{:S(2)}, u32[]{:S(2)}) collective-permute-start(bf16[2,2,64,896]{3,2,1,0:T(8,128)(2,1)S(1)} %attend.3.refs_0_.mine_ref), channel_id=1, source_target_pairs={{0,1},{1,0},{2,3},{3,2},{4,5},{5,4},{6,7},{7,6},{8,9},{9,8},{10,11... | collective-permute-start | bytes 1376264 | tf_op jit(solution)/shard_map/ppermute | solution.py:703
  81.9 3.5 %project.1.mine_ref = bf16[2,3,64,1792]{3,2,1,0:T(8,128)(2,1)S(1)} custom-call(bf16[2,3,64,896]{3,2,1,0:T(8,128)(2,1)S(1)} %attend.2.attended_ref, bf16[896,1792]{1,0:T(8,128)(2,1)} %w_mine.3, bf16[2,2,64,896]{3,2,1,0:T(8,128)(2,1)S(1)} %attend.3.refs_0_.mine_ref), custom_call_target="tpu_custom_call" | custom-call | flops 1000 | bytes 1000 | tf_op jit(solution)/shard_map/project/pallas_call | solution.py:528
  86.6 1.7 copy-done.2
  88.2 2.3 %collective-permute-done.9.theirs_ref = bf16[2,3,64,896]{3,2,1,0:T(8,128)(2,1)S(1)} collective-permute-done((bf16[2,3,64,896]{3,2,1,0:T(8,128)(2,1)S(1)}, bf16[2,3,64,896]{3,2,1,0:T(8,128)(2,1)S(1)}, u32[]{:S(2)}, u32[]{:S(2)}) %collective-permute-start.9) | collective-permute-done | bytes 688160 | tf_op jit(solution)/shard_map/ppermute | solution.py:703
  90.6 23.9 %mlp.2 = (f32[3,64,1792]{2,1,0:T(8,128)S(1)}, bf16[3,64,1792]{2,1,0:T(8,128)(2,1)S(1)}) custom-call(bf16[3,64,1792]{2,1,0:T(8,128)(2,1)} %get-tuple-element.133.own_ref, bf16[3,64,1792]{2,1,0:T(8,128)(2,1)S(1)} %collective-permute-done.4.other_ref, bf16[2,3,64,1792]{3,2,1,0:T(8,128)(2,1)S(1)} %project.1.mine_ref, ...), custom_call_target="tpu_custom_call" | custom-call | flops 30299652096 | bytes 39452672 | tf_op jit(solution)/shard_map/mlp/pallas_call | solution.py:652
  114.7 16.6 %mlp.3 = (f32[2,64,1792]{2,1,0:T(8,128)S(1)}, bf16[2,64,1792]{2,1,0:T(8,128)(2,1)S(1)}) custom-call(bf16[2,64,1792]{2,1,0:T(8,128)(2,1)S(1)} %get-tuple-element.134.own_ref.refs_2_, bf16[2,64,1792]{2,1,0:T(8,128)(2,1)S(1)} %collective-permute-done.8.other_ref, bf16[2,2,64,896]{3,2,1,0:T(8,128)(2,1)S(1)} %attend.3.refs_0_.mine_ref, ...), custom_call_target="tpu_custom_call" | custom-call | flops 20199768064 | bytes 39452672 | tf_op jit(solution)/shard_map/mlp/pallas_call | solution.py:652
  132.3 3.9 %collective-permute-start.15 = (bf16[3,64,1792]{2,1,0:T(8,128)(2,1)}, bf16[3,64,1792]{2,1,0:T(8,128)(2,1)S(1)}, u32[]{:S(2)}, u32[]{:S(2)}) collective-permute-start(bf16[3,64,1792]{2,1,0:T(8,128)(2,1)} %add.61.refs_0_.refs_3_.refs_5_.refs_9_.refs_11_), channel_id=1, source_target_pairs={{0,4},{2,6},{4,0},{6,2},{8,12},{10,14},{12,8},{14,10},{1,5},{3,7},... | collective-permute-start | bytes 2064392 | tf_op jit(solution)/shard_map/ppermute | solution.py:828
  136.2 2.0 %collective-permute-start.14 = (bf16[2,64,1792]{2,1,0:T(8,128)(2,1)S(1)}, bf16[2,64,1792]{2,1,0:T(8,128)(2,1)S(1)}, u32[]{:S(2)}, u32[]{:S(2)}) collective-permute-start(bf16[2,64,1792]{2,1,0:T(8,128)(2,1)S(1)} %get-tuple-element.103), channel_id=1, source_target_pairs={{0,1},{1,0},{2,3},{3,2},{4,5},{5,4},{6,7},{7,6},{8,9},{9,8},{10,11... | collective-permute-start | bytes 1376264 | tf_op jit(solution)/shard_map/ppermute | solution.py:703
  138.4 11.9 %collective-permute-done.15.refs_0_.refs_2_ = bf16[3,64,1792]{2,1,0:T(8,128)(2,1)S(1)} collective-permute-done((bf16[3,64,1792]{2,1,0:T(8,128)(2,1)}, bf16[3,64,1792]{2,1,0:T(8,128)(2,1)S(1)}, u32[]{:S(2)}, u32[]{:S(2)}) %collective-permute-start.15) | collective-permute-done | bytes 688160 | tf_op jit(solution)/shard_map/ppermute | solution.py:828
  151.7 1.7 collective-permute-start.21
  153.5 4.1 %gather.11.refs_2_.found_ref = bf16[16,64,1792]{2,1,0:T(8,128)(2,1)S(1)} custom-call(s32[16]{0:T(128)S(1)} %broadcast_select_fusion.2.table_ref.code_ref, bf16[3,64,1792]{2,1,0:T(8,128)(2,1)} %add.61.refs_0_.refs_3_.refs_5_.refs_9_.refs_11_, bf16[2,64,1792]{2,1,0:T(8,128)(2,1)} %add.62.refs_1_, ...), custom_call_target="tpu_custom_call" | custom-call | flops 1000 | bytes 1000 | tf_op jit(solution)/shard_map/gather/pallas_call | solution.py:352
  157.6 7.2 %collective-permute-done.21.refs_0_ = bf16[2,64,1792]{2,1,0:T(8,128)(2,1)S(1)} collective-permute-done((bf16[2,64,1792]{2,1,0:T(8,128)(2,1)}, bf16[2,64,1792]{2,1,0:T(8,128)(2,1)S(1)}, u32[]{:S(2)}, u32[]{:S(2)}) %collective-permute-start.21) | collective-permute-done | bytes 458784 | tf_op jit(solution)/shard_map/ppermute | solution.py:828
  165.5 2.5 %collective-permute-done.23 = bf16[2,2,64,1792]{3,2,1,0:T(8,128)(2,1)S(1)} collective-permute-done((bf16[2,2,64,1792]{3,2,1,0:T(8,128)(2,1)S(1)}, bf16[2,2,64,1792]{3,2,1,0:T(8,128)(2,1)S(1)}, u32[]{:S(2)}, u32[]{:S(2)}) %collective-permute-start.23) | collective-permute-done | bytes 917536 | tf_op jit(solution)/shard_map/ppermute | solution.py:825
  167.9 7.0 %merge.1 = bf16[64,16,1792]{2,1,0:T(8,128)(2,1)} custom-call(s32[1]{0:T(128)} %bitcast.19.device_ref, s32[8]{0:T(128)} %count_ref.5, s32[16]{0:T(128)} %bitcast.45, s32[16]{0:T(128)S(1)} %broadcast_select_fusion.2.table_ref.code_ref, bf16[64,16,1792]{2,1,0:T(8,128)(2,1)} %bitcast.43, bf16[16,64,1792]{2,1,0:T(8,128)(2,1)S(1)} %gather.11.refs_2_.found_ref, ...), custom_call_target="tpu_custom_call" | custom-call | flops 1000 | bytes 1000 | tf_op jit(solution)/shard_map/merge/pallas_call | solution.py:297
  (75 shorter events, 12.0 us)
Async XLA Ops:
  12.1 6.3 %collective-permute-start.1 = (bf16[8,64,1792]{2,1,0:T(8,128)(2,1)S(1)}, bf16[8,64,1792]{2,1,0:T(8,128)(2,1)}, u32[]{:S(2)}, u32[]{:S(2)}) collective-permute-start(bf16[8,64,1792]{2,1,0:T(8,128)(2,1)S(1)} %get-tuple-element.95.refs_0_), channel_id=1, source_target_pairs={{0,2},{2,0},{4,6},{6,4},{8,10},{10,8},{12,14},{14,12},{1,3},{3,1},... | collective-permute-start | bytes 5505032 | tf_op jit(solution)/shard_map/ppermute | solution.py:825
  12.5 5.9 %copy-start.7 = (bf16[8,64,1792]{2,1,0:T(8,128)(2,1)S(1)}, bf16[8,64,1792]{2,1,0:T(8,128)(2,1)}, u32[]{:S(2)}) copy-start(bf16[8,64,1792]{2,1,0:T(8,128)(2,1)} %get-tuple-element.94.refs_0_) | copy-start | bytes 5505028
  13.8 21.1 %collective-permute-start.7 = (bf16[224,1792]{1,0:T(8,128)(2,1)S(1)}, bf16[224,1792]{1,0:T(8,128)(2,1)S(1)}, u32[]{:S(2)}, u32[]{:S(2)}) collective-permute-start(bf16[224,1792]{1,0:T(8,128)(2,1)S(1)} %w_piece.1), channel_id=1, source_target_pairs={{0,1},{1,0},{2,3},{3,2},{4,5},{5,4},{6,7},{7,6},{8,9},{9,8},{10,11... | collective-permute-start | bytes 2408456 | tf_op jit(solution)/shard_map/ppermute | solution.py:703
  21.6 18.1 %collective-permute-start.2 = (bf16[3,64,1792]{2,1,0:T(8,128)(2,1)S(1)}, bf16[3,64,1792]{2,1,0:T(8,128)(2,1)}, u32[]{:S(2)}, u32[]{:S(2)}) collective-permute-start(bf16[3,64,1792]{2,1,0:T(8,128)(2,1)S(1)} %get-tuple-element.96), channel_id=1, source_target_pairs={{0,4},{2,6},{4,0},{6,2},{8,12},{10,14},{12,8},{14,10},{1,5},{3,7},... | collective-permute-start | bytes 2064392 | tf_op jit(solution)/shard_map/ppermute | solution.py:828
  23.2 16.5 %collective-permute-start.3 = (bf16[3,64,1792]{2,1,0:T(8,128)(2,1)S(1)}, bf16[3,64,1792]{2,1,0:T(8,128)(2,1)}, u32[]{:S(2)}, u32[]{:S(2)}) collective-permute-start(bf16[3,64,1792]{2,1,0:T(8,128)(2,1)S(1)} %get-tuple-element.97), channel_id=1, source_target_pairs={{0,2},{2,0},{4,8},{6,10},{8,4},{10,6},{12,14},{14,12},{1,3},{3,1},... | collective-permute-start | bytes 2064392 | tf_op jit(solution)/shard_map/ppermute | solution.py:831
  24.4 4.2 %collective-permute-start = (f32[1]{0:T(128)}, f32[1]{0:T(128)}, u32[]{:S(2)}, u32[]{:S(2)}) collective-permute-start(f32[1]{0:T(128)} %convert_element_type.8), channel_id=1, source_target_pairs={{0,16},{16,0},{1,17},{17,1},{2,18},{18,2},{3,19},{19,3},{4,20},{20... | collective-permute-start | bytes 20 | tf_op jit(solution)/shard_map/ppermute | solution.py:838
  35.9 23.0 %collective-permute-start.10 = (bf16[1,224,1792]{2,1,0:T(8,128)(2,1)}, bf16[1,224,1792]{2,1,0:T(8,128)(2,1)S(1)}, u32[]{:S(2)}, u32[]{:S(2)}) collective-permute-start(bf16[1,224,1792]{2,1,0:T(8,128)(2,1)} %w_near.1), channel_id=1, source_target_pairs={{0,16},{16,0},{1,17},{17,1},{2,18},{18,2},{3,19},{19,3},{4,20},{20... | collective-permute-start | bytes 2408456 | tf_op jit(solution)/shard_map/ppermute | solution.py:895
  39.7 5.5 %copy-start.10 = (f32[1792]{0:T(1024)S(1)}, f32[1792]{0:T(1024)}, u32[]{:S(2)}) copy-start(f32[1792]{0:T(1024)} %param.27) | copy-start | bytes 21508
  39.7 5.6 %copy-start.11 = (f32[1792]{0:T(1024)S(1)}, f32[1792]{0:T(1024)}, u32[]{:S(2)}) copy-start(f32[1792]{0:T(1024)} %param.31) | copy-start | bytes 21508
  39.7 5.6 %copy-start.12 = (f32[1792]{0:T(1024)S(1)}, f32[1792]{0:T(1024)}, u32[]{:S(2)}) copy-start(f32[1792]{0:T(1024)} %param.32) | copy-start | bytes 21508
  39.7 5.6 %copy-start.13 = (f32[1792]{0:T(1024)S(1)}, f32[1792]{0:T(1024)}, u32[]{:S(2)}) copy-start(f32[1792]{0:T(1024)} %param.33) | copy-start | bytes 21508
  39.7 5.6 %copy-start.14 = (f32[1792]{0:T(1024)S(1)}, f32[1792]{0:T(1024)}, u32[]{:S(2)}) copy-start(f32[1792]{0:T(1024)} %param.37) | copy-start | bytes 21508
  39.7 5.6 %copy-start.8 = (f32[4608]{0:T(1024)S(1)}, f32[4608]{0:T(1024)}, u32[]{:S(2)}) copy-start(f32[4608]{0:T(1024)} %param.35) | copy-start | bytes 55300
  42.4 18.5 %collective-permute-start.4 = (bf16[3,64,1792]{2,1,0:T(8,128)(2,1)}, bf16[3,64,1792]{2,1,0:T(8,128)(2,1)S(1)}, u32[]{:S(2)}, u32[]{:S(2)}) collective-permute-start(bf16[3,64,1792]{2,1,0:T(8,128)(2,1)} %get-tuple-element.133.own_ref), channel_id=1, source_target_pairs={{0,1},{1,0},{2,3},{3,2},{4,5},{5,4},{6,7},{7,6},{8,9},{9,8},{10,11... | collective-permute-start | bytes 2064392 | tf_op jit(solution)/shard_map/ppermute | solution.py:703
  43.0 12.4 %collective-permute-start.5 = (bf16[2,64,1792]{2,1,0:T(8,128)(2,1)S(1)}, bf16[2,64,1792]{2,1,0:T(8,128)(2,1)}, u32[]{:S(2)}, u32[]{:S(2)}) collective-permute-start(bf16[2,64,1792]{2,1,0:T(8,128)(2,1)S(1)} %copy-done.5), channel_id=1, source_target_pairs={{0,4},{2,6},{4,0},{6,2},{8,12},{10,14},{12,8},{14,10},{1,5},{3,7},... | collective-permute-start | bytes 1376264 | tf_op jit(solution)/shard_map/ppermute | solution.py:828
  45.2 10.2 %collective-permute-start.6 = (bf16[2,64,1792]{2,1,0:T(8,128)(2,1)S(1)}, bf16[2,64,1792]{2,1,0:T(8,128)(2,1)}, u32[]{:S(2)}, u32[]{:S(2)}) collective-permute-start(bf16[2,64,1792]{2,1,0:T(8,128)(2,1)S(1)} %get-tuple-element.99), channel_id=1, source_target_pairs={{0,2},{2,0},{4,8},{6,10},{8,4},{10,6},{12,14},{14,12},{1,3},{3,1},... | collective-permute-start | bytes 1376264 | tf_op jit(solution)/shard_map/ppermute | solution.py:831
  57.2 15.1 %collective-permute-start.8 = (bf16[2,64,1792]{2,1,0:T(8,128)(2,1)S(1)}, bf16[2,64,1792]{2,1,0:T(8,128)(2,1)S(1)}, u32[]{:S(2)}, u32[]{:S(2)}) collective-permute-start(bf16[2,64,1792]{2,1,0:T(8,128)(2,1)S(1)} %get-tuple-element.134.own_ref.refs_2_), channel_id=1, source_target_pairs={{0,1},{1,0},{2,3},{3,2},{4,5},{5,4},{6,7},{7,6},{8,9},{9,8},{10,11... | collective-permute-start | bytes 1376264 | tf_op jit(solution)/shard_map/ppermute | solution.py:703
  59.1 26.3 %collective-permute-start.11 = (bf16[2,224,1792]{2,1,0:T(8,128)(2,1)S(1)}, bf16[2,224,1792]{2,1,0:T(8,128)(2,1)S(1)}, u32[]{:S(2)}, u32[]{:S(2)}) collective-permute-start(bf16[2,224,1792]{2,1,0:T(8,128)(2,1)S(1)} %w_both.1), channel_id=1, source_target_pairs={{0,2},{2,0},{4,6},{6,4},{8,10},{10,8},{12,14},{14,12},{1,3},{3,1},... | collective-permute-start | bytes 4816904 | tf_op jit(solution)/shard_map/ppermute | solution.py:767
  72.1 18.4 %collective-permute-start.9 = (bf16[2,3,64,896]{3,2,1,0:T(8,128)(2,1)S(1)}, bf16[2,3,64,896]{3,2,1,0:T(8,128)(2,1)S(1)}, u32[]{:S(2)}, u32[]{:S(2)}) collective-permute-start(bf16[2,3,64,896]{3,2,1,0:T(8,128)(2,1)S(1)} %attend.2.attended_ref), channel_id=1, source_target_pairs={{0,1},{1,0},{2,3},{3,2},{4,5},{5,4},{6,7},{7,6},{8,9},{9,8},{10,11... | collective-permute-start | bytes 2064392 | tf_op jit(solution)/shard_map/ppermute | solution.py:703
  79.9 34.8 %collective-permute-start.13 = (bf16[2,2,64,896]{3,2,1,0:T(8,128)(2,1)S(1)}, bf16[2,2,64,896]{3,2,1,0:T(8,128)(2,1)S(1)}, u32[]{:S(2)}, u32[]{:S(2)}) collective-permute-start(bf16[2,2,64,896]{3,2,1,0:T(8,128)(2,1)S(1)} %attend.3.refs_0_.mine_ref), channel_id=1, source_target_pairs={{0,1},{1,0},{2,3},{3,2},{4,5},{5,4},{6,7},{7,6},{8,9},{9,8},{10,11... | collective-permute-start | bytes 1376264 | tf_op jit(solution)/shard_map/ppermute | solution.py:703
  90.6 24.1 %copy-start.3 = (bf16[896,1792]{1,0:T(8,128)(2,1)S(1)}, bf16[896,1792]{1,0:T(8,128)(2,1)}, u32[]{:S(2)}) copy-start(bf16[896,1792]{1,0:T(8,128)(2,1)} %copy-done.2) | copy-start | bytes 9633796
  114.5 16.8 %collective-permute-start.12 = (bf16[3,64,1792]{2,1,0:T(8,128)(2,1)S(1)}, bf16[3,64,1792]{2,1,0:T(8,128)(2,1)S(1)}, u32[]{:S(2)}, u32[]{:S(2)}) collective-permute-start(bf16[3,64,1792]{2,1,0:T(8,128)(2,1)S(1)} %get-tuple-element.101), channel_id=1, source_target_pairs={{0,1},{1,0},{2,3},{3,2},{4,5},{5,4},{6,7},{7,6},{8,9},{9,8},{10,11... | collective-permute-start | bytes 2064392 | tf_op jit(solution)/shard_map/ppermute | solution.py:703
  132.3 5.9 %collective-permute-start.16 = (bf16[3,64,1792]{2,1,0:T(8,128)(2,1)}, bf16[3,64,1792]{2,1,0:T(8,128)(2,1)S(1)}, u32[]{:S(2)}, u32[]{:S(2)}) collective-permute-start(bf16[3,64,1792]{2,1,0:T(8,128)(2,1)} %add.61.refs_0_.refs_3_.refs_5_.refs_9_.refs_11_), channel_id=1, source_target_pairs={{0,2},{2,0},{4,8},{6,10},{8,4},{10,6},{12,14},{14,12},{1,3},{3,1},... | collective-permute-start | bytes 2064392 | tf_op jit(solution)/shard_map/ppermute | solution.py:831
  132.3 18.1 %collective-permute-start.15 = (bf16[3,64,1792]{2,1,0:T(8,128)(2,1)}, bf16[3,64,1792]{2,1,0:T(8,128)(2,1)S(1)}, u32[]{:S(2)}, u32[]{:S(2)}) collective-permute-start(bf16[3,64,1792]{2,1,0:T(8,128)(2,1)} %add.61.refs_0_.refs_3_.refs_5_.refs_9_.refs_11_), channel_id=1, source_target_pairs={{0,4},{2,6},{4,0},{6,2},{8,12},{10,14},{12,8},{14,10},{1,5},{3,7},... | collective-permute-start | bytes 2064392 | tf_op jit(solution)/shard_map/ppermute | solution.py:828
  136.2 15.5 %collective-permute-start.17 = (bf16[3,64,1792]{2,1,0:T(8,128)(2,1)}, bf16[3,64,1792]{2,1,0:T(8,128)(2,1)S(1)}, u32[]{:S(2)}, u32[]{:S(2)}) collective-permute-start(bf16[3,64,1792]{2,1,0:T(8,128)(2,1)} %add.61.refs_0_.refs_3_.refs_5_.refs_9_.refs_11_), channel_id=1, source_target_pairs={{0,2},{2,0},{4,6},{6,4},{8,10},{10,8},{12,14},{14,12},{1,3},{3,1},... | collective-permute-start | bytes 2064392 | tf_op jit(solution)/shard_map/ppermute | solution.py:825
  136.2 14.2 %collective-permute-start.14 = (bf16[2,64,1792]{2,1,0:T(8,128)(2,1)S(1)}, bf16[2,64,1792]{2,1,0:T(8,128)(2,1)S(1)}, u32[]{:S(2)}, u32[]{:S(2)}) collective-permute-start(bf16[2,64,1792]{2,1,0:T(8,128)(2,1)S(1)} %get-tuple-element.103), channel_id=1, source_target_pairs={{0,1},{1,0},{2,3},{3,2},{4,5},{5,4},{6,7},{7,6},{8,9},{9,8},{10,11... | collective-permute-start | bytes 1376264 | tf_op jit(solution)/shard_map/ppermute | solution.py:703
  138.2 15.3 %collective-permute-start.20 = (bf16[3,64,1792]{2,1,0:T(8,128)(2,1)S(1)}, bf16[3,64,1792]{2,1,0:T(8,128)(2,1)}, u32[]{:S(2)}, u32[]{:S(2)}) collective-permute-start(bf16[3,64,1792]{2,1,0:T(8,128)(2,1)S(1)} %collective-permute-done.16.refs_1_.refs_4_), channel_id=1, source_target_pairs={{0,2},{2,0},{4,6},{6,4},{8,10},{10,8},{12,14},{14,12},{1,3},{3,1},... | collective-permute-start | bytes 2064392 | tf_op jit(solution)/shard_map/ppermute | solution.py:825
  150.3 3.2 %collective-permute-start.19 = (bf16[3,64,1792]{2,1,0:T(8,128)(2,1)S(1)}, bf16[3,64,1792]{2,1,0:T(8,128)(2,1)}, u32[]{:S(2)}, u32[]{:S(2)}) collective-permute-start(bf16[3,64,1792]{2,1,0:T(8,128)(2,1)S(1)} %collective-permute-done.15.refs_0_.refs_2_), channel_id=1, source_target_pairs={{0,2},{2,0},{4,6},{6,4},{8,10},{10,8},{12,14},{14,12},{1,3},{3,1},... | collective-permute-start | bytes 2064392 | tf_op jit(solution)/shard_map/ppermute | solution.py:825
  151.2 2.3 %collective-permute-start.18 = (bf16[2,64,1792]{2,1,0:T(8,128)(2,1)}, bf16[2,64,1792]{2,1,0:T(8,128)(2,1)S(1)}, u32[]{:S(2)}, u32[]{:S(2)}) collective-permute-start(bf16[2,64,1792]{2,1,0:T(8,128)(2,1)} %add.62.refs_1_), channel_id=1, source_target_pairs={{0,2},{2,0},{4,6},{6,4},{8,10},{10,8},{12,14},{14,12},{1,3},{3,1},... | collective-permute-start | bytes 1376264 | tf_op jit(solution)/shard_map/ppermute | solution.py:825
  151.7 5.9 %collective-permute-start.22 = (bf16[2,64,1792]{2,1,0:T(8,128)(2,1)}, bf16[2,64,1792]{2,1,0:T(8,128)(2,1)S(1)}, u32[]{:S(2)}, u32[]{:S(2)}) collective-permute-start(bf16[2,64,1792]{2,1,0:T(8,128)(2,1)} %add.62.refs_1_), channel_id=1, source_target_pairs={{0,2},{2,0},{4,8},{6,10},{8,4},{10,6},{12,14},{14,12},{1,3},{3,1},... | collective-permute-start | bytes 1376264 | tf_op jit(solution)/shard_map/ppermute | solution.py:831
  151.7 13.1 %collective-permute-start.21 = (bf16[2,64,1792]{2,1,0:T(8,128)(2,1)}, bf16[2,64,1792]{2,1,0:T(8,128)(2,1)S(1)}, u32[]{:S(2)}, u32[]{:S(2)}) collective-permute-start(bf16[2,64,1792]{2,1,0:T(8,128)(2,1)} %add.62.refs_1_), channel_id=1, source_target_pairs={{0,4},{2,6},{4,0},{6,2},{8,12},{10,14},{12,8},{14,10},{1,5},{3,7},... | collective-permute-start | bytes 1376264 | tf_op jit(solution)/shard_map/ppermute | solution.py:828
  165.4 2.5 %collective-permute-start.23 = (bf16[2,2,64,1792]{3,2,1,0:T(8,128)(2,1)S(1)}, bf16[2,2,64,1792]{3,2,1,0:T(8,128)(2,1)S(1)}, u32[]{:S(2)}, u32[]{:S(2)}) collective-permute-start(bf16[2,2,64,1792]{3,2,1,0:T(8,128)(2,1)S(1)} %late.1), channel_id=1, source_target_pairs={{0,2},{2,0},{4,6},{6,4},{8,10},{10,8},{12,14},{14,12},{1,3},{3,1},... | collective-permute-start | bytes 2752520 | tf_op jit(solution)/shard_map/ppermute | solution.py:825
  (5 other events, 13.4 us)

commit v6 on v4

--- a/solution.py
+++ b/solution.py
@@ -499,9 +499,9 @@
     )(own, other, rows_params, b_qkv, in_hbm(w_qkv), *after)
 
 
-UP_TILE = 768
+UP_TILE = 1536
 DOWN_TILE = 256
-SLOTS = 4
+SLOTS = 3
 
 
 def mlp_kernel(n_after, own_ref, other_ref, mine_ref, theirs_ref, rows_ref, b_up_ref, w_mine, w_theirs,
@@ -795,7 +795,8 @@
         short = short + lax.ppermute(short, "groups", [(0, 1), (1, 0)])
     else:
         short = lax.pmax(short, "groups")
-    short = short[0] > 0
+    flag = short
+    short = flag[0] > 0
 
     parts = tuple(zip(STARTS, CHUNKS))
     sends = [(AT_PAIR + at, size) for at, size in parts] + [(AT_NEXT + at, size) for at, size in parts]
@@ -845,7 +846,7 @@
 
         blocks_0 = deal(0)
         state_0 = start(blocks_0, [])
-        w_sent = line_up([w_near], [blocks_0], "w_near")
+        w_sent = line_up([w_near], [flag], "w_near")
         blocks_1 = deal(1, [w_sent])
         state_1 = start(blocks_1, [])
         w_side = lax.ppermute(w_sent, "groups", [(0, 1), (1, 0)])[0]

time: 180 us -> 182 us (1.011)
  starting transfers between devices: 22.3 us -> 27.6 us
  waiting for transfers between devices: 49.1 us -> 46.5 us
  local copies, waits for them, and re-layouts: 4.52 us -> 1.97 us
    ppermute x4, waiting for transfers between devices: 36.8 us -> 28.9 us  [to_pair(): return lax.ppermute(value, 'dp', pairs)]
    ppermute x7, waiting for transfers between devices: 7.71 us -> 14.2 us  [swap(): return lax.ppermute(value, 'tensor', [(0, 1), (1, 0)])]
    ppermute x4, starting transfers between devices: 6.75 us -> 12 us  [to_pair(): return lax.ppermute(value, 'dp', pairs)]
    another operation x7, local copies, waits for them, and re-layouts: 2.62 us -> 0.12 us  [per_device(): jnp.stack([pre_gain, pre_shift, mlp_gain, mlp_shift, b_out, b_down])]
  transfers between devices with their start and end apart: 24 -> 24, of which waited for: 9 -> 9; matrix products, arithmetic and copies ran while one was open for 2% -> 0% of each run, Pallas kernels for 38% -> 40%
where the time goes in v6:
time: 182 us; the launch traced here: 181 us
  Pallas kernels  89.8 us (49%)
  waiting for transfers between devices  46.5 us (26%)
  starting transfers between devices  27.6 us (15%)
  between operations  14.9 us (8%)
  local copies, waits for them, and re-layouts  1.97 us (1%)
    pallas_call x2, Pallas kernels, mlp(): pl.pallas_call(functools.partial(mlp_kernel, len(after)), out_shape=(jax....  39.3 us
    ppermute x4, waiting for transfers between devices, to_pair(): return lax.ppermute(value, 'dp', pairs)  28.9 us
    pallas_call x2, Pallas kernels, attend(): pl.pallas_call(functools.partial(attend_kernel, len(after)), out_shape=ja...  18.8 us
    ppermute x7, waiting for transfers between devices, swap(): return lax.ppermute(value, 'tensor', [(0, 1), (1, 0)])  14.2 us
    ppermute x4, starting transfers between devices, to_pair(): return lax.ppermute(value, 'dp', pairs)  12 us
    pallas_call x4, Pallas kernels, choose(): pl.pallas_call(functools.partial(choose_kernel, parts, len(sources)), out...  11.4 us
    ppermute x7, starting transfers between devices, swap(): return lax.ppermute(value, 'tensor', [(0, 1), (1, 0)])  9.36 us
    pallas_call x1, Pallas kernels, merge(): pl.pallas_call(functools.partial(merge_kernel, kept_count.shape[0]), out_...  7.03 us
  transfers between devices with their start and end apart: 24, of which 9 were waited for; matrix products, arithmetic and copies ran while one was open for 0% of the time, Pallas kernels for 40%

profile of v6, /device:TPU:0, one launch (start us, length us, event | category | flops | bytes accessed | tf_op | source)
XLA Modules:
  0.0 181.0 jit_solution(9456057850063299039)
XLA Ops:
  6.5 5.5 %pack.1 = (bf16[8,64,1792]{2,1,0:T(8,128)(2,1)}, bf16[8,64,1792]{2,1,0:T(8,128)(2,1)S(1)}) custom-call(s32[1]{0:T(128)} %bitcast.19.device_ref, s32[8]{0:T(128)} %count_ref.5, s32[16]{0:T(128)} %bitcast.44, bf16[64,16,1792]{2,1,0:T(8,128)(2,1)} %bitcast.42), custom_call_target="tpu_custom_call" | custom-call | tf_op jit(solution)/shard_map/pack/pallas_call | solution.py:224
  12.5 1.3 w_piece.1
  13.7 2.6 %collective-permute-start.6 = (bf16[224,1792]{1,0:T(8,128)(2,1)S(1)}, bf16[224,1792]{1,0:T(8,128)(2,1)S(1)}, u32[]{:S(2)}, u32[]{:S(2)}) collective-permute-start(bf16[224,1792]{1,0:T(8,128)(2,1)S(1)} %w_piece.1), channel_id=1, source_target_pairs={{0,1},{1,0},{2,3},{3,2},{4,5},{5,4},{6,7},{7,6},{8,9},{9,8},{10,11... | collective-permute-start | bytes 2408456 | tf_op jit(solution)/shard_map/ppermute | solution.py:660
  16.3 2.0 %plan.1.table_ref = s32[94]{0:T(128)S(1)} custom-call(s32[1]{0:T(128)} %bitcast.19.device_ref, s32[8]{0:T(128)} %count_ref.5), custom_call_target="tpu_custom_call" | custom-call | flops 1000 | bytes 1000 | tf_op jit(solution)/shard_map/plan/pallas_call | solution.py:166
  18.3 3.1 %send.1 = (bf16[3,64,1792]{2,1,0:T(8,128)(2,1)S(1)}, bf16[2,64,1792]{2,1,0:T(8,128)(2,1)S(1)}, bf16[3,64,1792]{2,1,0:T(8,128)(2,1)S(1)}, bf16[2,64,1792]{2,1,0:T(8,128)(2,1)S(1)}) custom-call(s32[94]{0:T(128)S(1)} %plan.1.table_ref, bf16[8,64,1792]{2,1,0:T(8,128)(2,1)S(1)} %copy-done.5, bf16[8,64,1792]{2,1,0:T(8,128)(2,1)} %collective-permute-done.1.refs_1_), custom_call_target="tpu_custom_call" | custom-call | flops 1000 | bytes 1000 | tf_op jit(solution)/shard_map/send/pallas_call | solution.py:352
  24.1 2.9 %collective-permute-start = (f32[1]{0:T(128)}, f32[1]{0:T(128)}, u32[]{:S(2)}, u32[]{:S(2)}) collective-permute-start(f32[1]{0:T(128)} %convert_element_type.8), channel_id=1, source_target_pairs={{0,16},{16,0},{1,17},{17,1},{2,18},{18,2},{3,19},{19,3},{4,20},{20... | collective-permute-start | bytes 20 | tf_op jit(solution)/shard_map/ppermute | solution.py:795
  28.5 6.4 %collective-permute-done.6.refs_0_.near = bf16[224,1792]{1,0:T(8,128)(2,1)S(1)} collective-permute-done((bf16[224,1792]{1,0:T(8,128)(2,1)S(1)}, bf16[224,1792]{1,0:T(8,128)(2,1)S(1)}, u32[]{:S(2)}, u32[]{:S(2)}) %collective-permute-start.6) | collective-permute-done | bytes 802848 | tf_op jit(solution)/shard_map/ppermute | solution.py:660
  34.9 1.0 w_near.1
  35.9 1.8 %collective-permute-start.7 = (bf16[1,224,1792]{2,1,0:T(8,128)(2,1)}, bf16[1,224,1792]{2,1,0:T(8,128)(2,1)S(1)}, u32[]{:S(2)}, u32[]{:S(2)}) collective-permute-start(bf16[1,224,1792]{2,1,0:T(8,128)(2,1)} %w_near.1), channel_id=1, source_target_pairs={{0,16},{16,0},{1,17},{17,1},{2,18},{18,2},{3,19},{19,3},{4,20},{20... | collective-permute-start | bytes 2408456 | tf_op jit(solution)/shard_map/ppermute | solution.py:852
  37.7 1.7 collective-permute-done.2
  39.4 2.6 %conditional.3 = (bf16[3,64,1792]{2,1,0:T(8,128)(2,1)}) conditional(s32[]{:T(128)} %convert_element_type.9, (s32[94]{0:T(128)S(1)}, bf16[8,64,1792]{2,1,0:T(8,128)(2,1)}, bf16[8,64,1792]{2,1,0:T(8,128)(2,1)}, bf16[3,64,1792]{2,1,0:T(8,128)(2,1)}, bf16[3,64,1792]{2,1,0:T(8,128)(2,1)}) %tuple.25, (s32[94]{0:T(128)S(1)}, bf16[8,64,1792]{2,1,0:T(8,128)(2,1)}, ...), branch_computations={%region_0.0_spmd, %region_1.0_spmd} | conditional | flops 689146 | bytes 62391604 | solution.py:829
  39.5 2.6 %deal_0.1 = bf16[3,64,1792]{2,1,0:T(8,128)(2,1)} custom-call(s32[94]{0:T(128)S(1)} %get-tuple-element.58.table_ref, bf16[8,64,1792]{2,1,0:T(8,128)(2,1)} %get-tuple-element.60.refs_0_, bf16[8,64,1792]{2,1,0:T(8,128)(2,1)} %get-tuple-element.62.refs_1_, bf16[3,64,1792]{2,1,0:T(8,128)(2,1)} %get-tuple-element.63.refs_2_.refs_3_, ...), custom_call_target="tpu_custom_call" | custom-call | flops 1000 | bytes 1000 | tf_op jit(solution)/shard_map/cond/branch_0_fun/deal_0/pallas_call | solution.py:352
  42.6 3.0 %collective-permute-start.8 = (bf16[2,64,1792]{2,1,0:T(8,128)(2,1)S(1)}, bf16[2,64,1792]{2,1,0:T(8,128)(2,1)}, u32[]{:S(2)}, u32[]{:S(2)}) collective-permute-start(bf16[2,64,1792]{2,1,0:T(8,128)(2,1)S(1)} %copy-done.3), channel_id=1, source_target_pairs={{0,4},{2,6},{4,0},{6,2},{8,12},{10,14},{12,8},{14,10},{1,5},{3,7},... | collective-permute-start | bytes 1376264 | tf_op jit(solution)/shard_map/ppermute | solution.py:785
  45.9 9.9 %collective-permute-done.8 = bf16[2,64,1792]{2,1,0:T(8,128)(2,1)} collective-permute-done((bf16[2,64,1792]{2,1,0:T(8,128)(2,1)S(1)}, bf16[2,64,1792]{2,1,0:T(8,128)(2,1)}, u32[]{:S(2)}, u32[]{:S(2)}) %collective-permute-start.8) | collective-permute-done | bytes 458784 | tf_op jit(solution)/shard_map/ppermute | solution.py:785
  55.9 1.8 conditional.4
  55.9 1.6 deal_1.1
  57.7 1.6 collective-permute-start.11
  60.0 11.2 %attend.2.mine_ref = bf16[2,3,64,896]{3,2,1,0:T(8,128)(2,1)S(1)} custom-call(bf16[3,64,1792]{2,1,0:T(8,128)(2,1)} %get-tuple-element.133.own_ref, bf16[3,64,1792]{2,1,0:T(8,128)(2,1)S(1)} %collective-permute-done.4.other_ref, f32[6,1792]{1,0:T(8,128)S(1)} %stack.48.rows_ref, f32[3,896]{1,0:T(4,128)S(1)} %copy-done.4, bf16[3,1792,896]{2,1,0:T(8,128)(2,1)} %w_ref.5), custom_call_target="tpu_custom_call" | custom-call | flops 14797504512 | bytes 9633792 | tf_op jit(solution)/shard_map/attend/pallas_call | solution.py:483
  71.8 7.6 %attend.3.refs_0_.mine_ref = bf16[2,2,64,896]{3,2,1,0:T(8,128)(2,1)S(1)} custom-call(bf16[2,64,1792]{2,1,0:T(8,128)(2,1)S(1)} %get-tuple-element.134.refs_2_.own_ref, bf16[2,64,1792]{2,1,0:T(8,128)(2,1)S(1)} %collective-permute-done.11.other_ref, f32[6,1792]{1,0:T(8,128)S(1)} %stack.48.rows_ref, f32[3,896]{1,0:T(4,128)S(1)} %copy-done.4, ...), custom_call_target="tpu_custom_call" | custom-call | flops 9865003008 | bytes 9633792 | tf_op jit(solution)/shard_map/attend/pallas_call | solution.py:483
  79.4 1.6 collective-permute-start.13
  81.9 7.7 %collective-permute-done.5.theirs_ref = bf16[2,3,64,896]{3,2,1,0:T(8,128)(2,1)S(1)} collective-permute-done((bf16[2,3,64,896]{3,2,1,0:T(8,128)(2,1)S(1)}, bf16[2,3,64,896]{3,2,1,0:T(8,128)(2,1)S(1)}, u32[]{:S(2)}, u32[]{:S(2)}) %collective-permute-start.5) | collective-permute-done | bytes 688160 | tf_op jit(solution)/shard_map/ppermute | solution.py:660
  89.6 23.2 %mlp.2 = (f32[3,64,1792]{2,1,0:T(8,128)S(1)}, bf16[3,64,1792]{2,1,0:T(8,128)(2,1)S(1)}) custom-call(bf16[3,64,1792]{2,1,0:T(8,128)(2,1)} %get-tuple-element.133.own_ref, bf16[3,64,1792]{2,1,0:T(8,128)(2,1)S(1)} %collective-permute-done.4.other_ref, bf16[2,3,64,896]{3,2,1,0:T(8,128)(2,1)S(1)} %attend.2.mine_ref, ...), custom_call_target="tpu_custom_call" | custom-call | flops 30299652096 | bytes 39452672 | tf_op jit(solution)/shard_map/mlp/pallas_call | solution.py:609
  113.3 16.1 %mlp.3 = (f32[2,64,1792]{2,1,0:T(8,128)S(1)}, bf16[2,64,1792]{2,1,0:T(8,128)(2,1)S(1)}) custom-call(bf16[2,64,1792]{2,1,0:T(8,128)(2,1)S(1)} %get-tuple-element.134.refs_2_.own_ref, bf16[2,64,1792]{2,1,0:T(8,128)(2,1)S(1)} %collective-permute-done.11.other_ref, bf16[2,2,64,896]{3,2,1,0:T(8,128)(2,1)S(1)} %attend.3.refs_0_.mine_ref, ...), custom_call_target="tpu_custom_call" | custom-call | flops 20199768064 | bytes 39452672 | tf_op jit(solution)/shard_map/mlp/pallas_call | solution.py:609
  129.5 1.0 add.61.refs_0_.refs_3_.refs_5_.refs_9_.refs_11_
  130.5 5.0 %collective-permute-start.15 = (bf16[3,64,1792]{2,1,0:T(8,128)(2,1)}, bf16[3,64,1792]{2,1,0:T(8,128)(2,1)S(1)}, u32[]{:S(2)}, u32[]{:S(2)}) collective-permute-start(bf16[3,64,1792]{2,1,0:T(8,128)(2,1)} %add.61.refs_0_.refs_3_.refs_5_.refs_9_.refs_11_), channel_id=1, source_target_pairs={{0,4},{2,6},{4,0},{6,2},{8,12},{10,14},{12,8},{14,10},{1,5},{3,7},... | collective-permute-start | bytes 2064392 | tf_op jit(solution)/shard_map/ppermute | solution.py:785
  135.5 2.0 %collective-permute-start.14 = (bf16[2,64,1792]{2,1,0:T(8,128)(2,1)S(1)}, bf16[2,64,1792]{2,1,0:T(8,128)(2,1)S(1)}, u32[]{:S(2)}, u32[]{:S(2)}) collective-permute-start(bf16[2,64,1792]{2,1,0:T(8,128)(2,1)S(1)} %get-tuple-element.103), channel_id=1, source_target_pairs={{0,1},{1,0},{2,3},{3,2},{4,5},{5,4},{6,7},{7,6},{8,9},{9,8},{10,11... | collective-permute-start | bytes 1376264 | tf_op jit(solution)/shard_map/ppermute | solution.py:660
  137.7 10.9 %collective-permute-done.15.refs_0_.refs_2_ = bf16[3,64,1792]{2,1,0:T(8,128)(2,1)S(1)} collective-permute-done((bf16[3,64,1792]{2,1,0:T(8,128)(2,1)}, bf16[3,64,1792]{2,1,0:T(8,128)(2,1)S(1)}, u32[]{:S(2)}, u32[]{:S(2)}) %collective-permute-start.15) | collective-permute-done | bytes 688160 | tf_op jit(solution)/shard_map/ppermute | solution.py:785
  150.0 3.4 %collective-permute-start.21 = (bf16[2,64,1792]{2,1,0:T(8,128)(2,1)}, bf16[2,64,1792]{2,1,0:T(8,128)(2,1)S(1)}, u32[]{:S(2)}, u32[]{:S(2)}) collective-permute-start(bf16[2,64,1792]{2,1,0:T(8,128)(2,1)} %add.62.refs_1_), channel_id=1, source_target_pairs={{0,4},{2,6},{4,0},{6,2},{8,12},{10,14},{12,8},{14,10},{1,5},{3,7},... | collective-permute-start | bytes 1376264 | tf_op jit(solution)/shard_map/ppermute | solution.py:785
  153.5 4.1 %gather.11.refs_2_.found_ref = bf16[16,64,1792]{2,1,0:T(8,128)(2,1)S(1)} custom-call(s32[16]{0:T(128)S(1)} %broadcast_select_fusion.2.table_ref.code_ref, bf16[3,64,1792]{2,1,0:T(8,128)(2,1)} %add.61.refs_0_.refs_3_.refs_5_.refs_9_.refs_11_, bf16[2,64,1792]{2,1,0:T(8,128)(2,1)} %add.62.refs_1_, ...), custom_call_target="tpu_custom_call" | custom-call | flops 1000 | bytes 1000 | tf_op jit(solution)/shard_map/gather/pallas_call | solution.py:352
  157.6 6.4 %collective-permute-done.21.refs_0_ = bf16[2,64,1792]{2,1,0:T(8,128)(2,1)S(1)} collective-permute-done((bf16[2,64,1792]{2,1,0:T(8,128)(2,1)}, bf16[2,64,1792]{2,1,0:T(8,128)(2,1)S(1)}, u32[]{:S(2)}, u32[]{:S(2)}) %collective-permute-start.21) | collective-permute-done | bytes 458784 | tf_op jit(solution)/shard_map/ppermute | solution.py:785
  164.7 2.5 %collective-permute-done.23 = bf16[2,2,64,1792]{3,2,1,0:T(8,128)(2,1)S(1)} collective-permute-done((bf16[2,2,64,1792]{3,2,1,0:T(8,128)(2,1)S(1)}, bf16[2,2,64,1792]{3,2,1,0:T(8,128)(2,1)S(1)}, u32[]{:S(2)}, u32[]{:S(2)}) %collective-permute-start.23) | collective-permute-done | bytes 917536 | tf_op jit(solution)/shard_map/ppermute | solution.py:782
  167.1 7.0 %merge.1 = bf16[64,16,1792]{2,1,0:T(8,128)(2,1)} custom-call(s32[1]{0:T(128)} %bitcast.19.device_ref, s32[8]{0:T(128)} %count_ref.5, s32[16]{0:T(128)} %bitcast.45, s32[16]{0:T(128)S(1)} %broadcast_select_fusion.2.table_ref.code_ref, bf16[64,16,1792]{2,1,0:T(8,128)(2,1)} %bitcast.43, bf16[16,64,1792]{2,1,0:T(8,128)(2,1)S(1)} %gather.11.refs_2_.found_ref, ...), custom_call_target="tpu_custom_call" | custom-call | flops 1000 | bytes 1000 | tf_op jit(solution)/shard_map/merge/pallas_call | solution.py:297
  (70 shorter events, 9.2 us)
Async XLA Ops:
  12.0 6.3 %collective-permute-start.1 = (bf16[8,64,1792]{2,1,0:T(8,128)(2,1)S(1)}, bf16[8,64,1792]{2,1,0:T(8,128)(2,1)}, u32[]{:S(2)}, u32[]{:S(2)}) collective-permute-start(bf16[8,64,1792]{2,1,0:T(8,128)(2,1)S(1)} %get-tuple-element.95.refs_0_), channel_id=1, source_target_pairs={{0,2},{2,0},{4,6},{6,4},{8,10},{10,8},{12,14},{14,12},{1,3},{3,1},... | collective-permute-start | bytes 5505032 | tf_op jit(solution)/shard_map/ppermute | solution.py:782
  12.5 5.9 %copy-start.5 = (bf16[8,64,1792]{2,1,0:T(8,128)(2,1)S(1)}, bf16[8,64,1792]{2,1,0:T(8,128)(2,1)}, u32[]{:S(2)}) copy-start(bf16[8,64,1792]{2,1,0:T(8,128)(2,1)} %get-tuple-element.94.refs_0_) | copy-start | bytes 5505028
  13.7 21.1 %collective-permute-start.6 = (bf16[224,1792]{1,0:T(8,128)(2,1)S(1)}, bf16[224,1792]{1,0:T(8,128)(2,1)S(1)}, u32[]{:S(2)}, u32[]{:S(2)}) collective-permute-start(bf16[224,1792]{1,0:T(8,128)(2,1)S(1)} %w_piece.1), channel_id=1, source_target_pairs={{0,1},{1,0},{2,3},{3,2},{4,5},{5,4},{6,7},{7,6},{8,9},{9,8},{10,11... | collective-permute-start | bytes 2408456 | tf_op jit(solution)/shard_map/ppermute | solution.py:660
  22.2 17.2 %collective-permute-start.2 = (bf16[3,64,1792]{2,1,0:T(8,128)(2,1)S(1)}, bf16[3,64,1792]{2,1,0:T(8,128)(2,1)}, u32[]{:S(2)}, u32[]{:S(2)}) collective-permute-start(bf16[3,64,1792]{2,1,0:T(8,128)(2,1)S(1)} %get-tuple-element.96), channel_id=1, source_target_pairs={{0,4},{2,6},{4,0},{6,2},{8,12},{10,14},{12,8},{14,10},{1,5},{3,7},... | collective-permute-start | bytes 2064392 | tf_op jit(solution)/shard_map/ppermute | solution.py:785
  22.8 16.5 %collective-permute-start.3 = (bf16[3,64,1792]{2,1,0:T(8,128)(2,1)S(1)}, bf16[3,64,1792]{2,1,0:T(8,128)(2,1)}, u32[]{:S(2)}, u32[]{:S(2)}) collective-permute-start(bf16[3,64,1792]{2,1,0:T(8,128)(2,1)S(1)} %get-tuple-element.97), channel_id=1, source_target_pairs={{0,2},{2,0},{4,8},{6,10},{8,4},{10,6},{12,14},{14,12},{1,3},{3,1},... | collective-permute-start | bytes 2064392 | tf_op jit(solution)/shard_map/ppermute | solution.py:788
  24.1 3.7 %collective-permute-start = (f32[1]{0:T(128)}, f32[1]{0:T(128)}, u32[]{:S(2)}, u32[]{:S(2)}) collective-permute-start(f32[1]{0:T(128)} %convert_element_type.8), channel_id=1, source_target_pairs={{0,16},{16,0},{1,17},{17,1},{2,18},{18,2},{3,19},{19,3},{4,20},{20... | collective-permute-start | bytes 20 | tf_op jit(solution)/shard_map/ppermute | solution.py:795
  35.9 23.5 %collective-permute-start.7 = (bf16[1,224,1792]{2,1,0:T(8,128)(2,1)}, bf16[1,224,1792]{2,1,0:T(8,128)(2,1)S(1)}, u32[]{:S(2)}, u32[]{:S(2)}) collective-permute-start(bf16[1,224,1792]{2,1,0:T(8,128)(2,1)} %w_near.1), channel_id=1, source_target_pairs={{0,16},{16,0},{1,17},{17,1},{2,18},{18,2},{3,19},{19,3},{4,20},{20... | collective-permute-start | bytes 2408456 | tf_op jit(solution)/shard_map/ppermute | solution.py:852
  39.4 6.2 %copy-start.7 = (f32[1792]{0:T(1024)S(1)}, f32[1792]{0:T(1024)}, u32[]{:S(2)}) copy-start(f32[1792]{0:T(1024)} %param.26) | copy-start | bytes 21508
  39.4 6.2 %copy-start.8 = (f32[1792]{0:T(1024)S(1)}, f32[1792]{0:T(1024)}, u32[]{:S(2)}) copy-start(f32[1792]{0:T(1024)} %param.27) | copy-start | bytes 21508
  39.4 6.2 %copy-start.9 = (f32[1792]{0:T(1024)S(1)}, f32[1792]{0:T(1024)}, u32[]{:S(2)}) copy-start(f32[1792]{0:T(1024)} %param.31) | copy-start | bytes 21508
  39.4 6.3 %copy-start.10 = (f32[1792]{0:T(1024)S(1)}, f32[1792]{0:T(1024)}, u32[]{:S(2)}) copy-start(f32[1792]{0:T(1024)} %param.32) | copy-start | bytes 21508
  39.4 6.3 %copy-start.11 = (f32[1792]{0:T(1024)S(1)}, f32[1792]{0:T(1024)}, u32[]{:S(2)}) copy-start(f32[1792]{0:T(1024)} %param.33) | copy-start | bytes 21508
  39.4 6.3 %copy-start.12 = (f32[1792]{0:T(1024)S(1)}, f32[1792]{0:T(1024)}, u32[]{:S(2)}) copy-start(f32[1792]{0:T(1024)} %param.37) | copy-start | bytes 21508
  39.4 6.3 %copy-start.6 = (f32[4608]{0:T(1024)S(1)}, f32[4608]{0:T(1024)}, u32[]{:S(2)}) copy-start(f32[4608]{0:T(1024)} %param.35) | copy-start | bytes 55300
  42.1 17.5 %collective-permute-start.4 = (bf16[3,64,1792]{2,1,0:T(8,128)(2,1)}, bf16[3,64,1792]{2,1,0:T(8,128)(2,1)S(1)}, u32[]{:S(2)}, u32[]{:S(2)}) collective-permute-start(bf16[3,64,1792]{2,1,0:T(8,128)(2,1)} %get-tuple-element.133.own_ref), channel_id=1, source_target_pairs={{0,1},{1,0},{2,3},{3,2},{4,5},{5,4},{6,7},{7,6},{8,9},{9,8},{10,11... | collective-permute-start | bytes 2064392 | tf_op jit(solution)/shard_map/ppermute | solution.py:660
  42.6 13.3 %collective-permute-start.8 = (bf16[2,64,1792]{2,1,0:T(8,128)(2,1)S(1)}, bf16[2,64,1792]{2,1,0:T(8,128)(2,1)}, u32[]{:S(2)}, u32[]{:S(2)}) collective-permute-start(bf16[2,64,1792]{2,1,0:T(8,128)(2,1)S(1)} %copy-done.3), channel_id=1, source_target_pairs={{0,4},{2,6},{4,0},{6,2},{8,12},{10,14},{12,8},{14,10},{1,5},{3,7},... | collective-permute-start | bytes 1376264 | tf_op jit(solution)/shard_map/ppermute | solution.py:785
  45.6 10.3 %collective-permute-start.9 = (bf16[2,64,1792]{2,1,0:T(8,128)(2,1)S(1)}, bf16[2,64,1792]{2,1,0:T(8,128)(2,1)}, u32[]{:S(2)}, u32[]{:S(2)}) collective-permute-start(bf16[2,64,1792]{2,1,0:T(8,128)(2,1)S(1)} %get-tuple-element.99), channel_id=1, source_target_pairs={{0,2},{2,0},{4,8},{6,10},{8,4},{10,6},{12,14},{14,12},{1,3},{3,1},... | collective-permute-start | bytes 1376264 | tf_op jit(solution)/shard_map/ppermute | solution.py:788
  57.7 14.1 %collective-permute-start.11 = (bf16[2,64,1792]{2,1,0:T(8,128)(2,1)S(1)}, bf16[2,64,1792]{2,1,0:T(8,128)(2,1)S(1)}, u32[]{:S(2)}, u32[]{:S(2)}) collective-permute-start(bf16[2,64,1792]{2,1,0:T(8,128)(2,1)S(1)} %get-tuple-element.134.refs_2_.own_ref), channel_id=1, source_target_pairs={{0,1},{1,0},{2,3},{3,2},{4,5},{5,4},{6,7},{7,6},{8,9},{9,8},{10,11... | collective-permute-start | bytes 1376264 | tf_op jit(solution)/shard_map/ppermute | solution.py:660
  59.5 21.5 %collective-permute-start.10 = (bf16[2,224,1792]{2,1,0:T(8,128)(2,1)S(1)}, bf16[2,224,1792]{2,1,0:T(8,128)(2,1)S(1)}, u32[]{:S(2)}, u32[]{:S(2)}) collective-permute-start(bf16[2,224,1792]{2,1,0:T(8,128)(2,1)S(1)} %w_both.1), channel_id=1, source_target_pairs={{0,2},{2,0},{4,6},{6,4},{8,10},{10,8},{12,14},{14,12},{1,3},{3,1},... | collective-permute-start | bytes 4816904 | tf_op jit(solution)/shard_map/ppermute | solution.py:724
  71.3 18.4 %collective-permute-start.5 = (bf16[2,3,64,896]{3,2,1,0:T(8,128)(2,1)S(1)}, bf16[2,3,64,896]{3,2,1,0:T(8,128)(2,1)S(1)}, u32[]{:S(2)}, u32[]{:S(2)}) collective-permute-start(bf16[2,3,64,896]{3,2,1,0:T(8,128)(2,1)S(1)} %attend.2.mine_ref), channel_id=1, source_target_pairs={{0,1},{1,0},{2,3},{3,2},{4,5},{5,4},{6,7},{7,6},{8,9},{9,8},{10,11... | collective-permute-start | bytes 2064392 | tf_op jit(solution)/shard_map/ppermute | solution.py:660
  79.4 33.9 %collective-permute-start.13 = (bf16[2,2,64,896]{3,2,1,0:T(8,128)(2,1)S(1)}, bf16[2,2,64,896]{3,2,1,0:T(8,128)(2,1)S(1)}, u32[]{:S(2)}, u32[]{:S(2)}) collective-permute-start(bf16[2,2,64,896]{3,2,1,0:T(8,128)(2,1)S(1)} %attend.3.refs_0_.mine_ref), channel_id=1, source_target_pairs={{0,1},{1,0},{2,3},{3,2},{4,5},{5,4},{6,7},{7,6},{8,9},{9,8},{10,11... | collective-permute-start | bytes 1376264 | tf_op jit(solution)/shard_map/ppermute | solution.py:660
  112.8 16.7 %collective-permute-start.12 = (bf16[3,64,1792]{2,1,0:T(8,128)(2,1)S(1)}, bf16[3,64,1792]{2,1,0:T(8,128)(2,1)S(1)}, u32[]{:S(2)}, u32[]{:S(2)}) collective-permute-start(bf16[3,64,1792]{2,1,0:T(8,128)(2,1)S(1)} %get-tuple-element.101), channel_id=1, source_target_pairs={{0,1},{1,0},{2,3},{3,2},{4,5},{5,4},{6,7},{7,6},{8,9},{9,8},{10,11... | collective-permute-start | bytes 2064392 | tf_op jit(solution)/shard_map/ppermute | solution.py:660
  130.5 7.0 %collective-permute-start.16 = (bf16[3,64,1792]{2,1,0:T(8,128)(2,1)}, bf16[3,64,1792]{2,1,0:T(8,128)(2,1)S(1)}, u32[]{:S(2)}, u32[]{:S(2)}) collective-permute-start(bf16[3,64,1792]{2,1,0:T(8,128)(2,1)} %add.61.refs_0_.refs_3_.refs_5_.refs_9_.refs_11_), channel_id=1, source_target_pairs={{0,2},{2,0},{4,8},{6,10},{8,4},{10,6},{12,14},{14,12},{1,3},{3,1},... | collective-permute-start | bytes 2064392 | tf_op jit(solution)/shard_map/ppermute | solution.py:788
  130.5 18.1 %collective-permute-start.15 = (bf16[3,64,1792]{2,1,0:T(8,128)(2,1)}, bf16[3,64,1792]{2,1,0:T(8,128)(2,1)S(1)}, u32[]{:S(2)}, u32[]{:S(2)}) collective-permute-start(bf16[3,64,1792]{2,1,0:T(8,128)(2,1)} %add.61.refs_0_.refs_3_.refs_5_.refs_9_.refs_11_), channel_id=1, source_target_pairs={{0,4},{2,6},{4,0},{6,2},{8,12},{10,14},{12,8},{14,10},{1,5},{3,7},... | collective-permute-start | bytes 2064392 | tf_op jit(solution)/shard_map/ppermute | solution.py:785
  135.5 14.5 %collective-permute-start.17 = (bf16[3,64,1792]{2,1,0:T(8,128)(2,1)}, bf16[3,64,1792]{2,1,0:T(8,128)(2,1)S(1)}, u32[]{:S(2)}, u32[]{:S(2)}) collective-permute-start(bf16[3,64,1792]{2,1,0:T(8,128)(2,1)} %add.61.refs_0_.refs_3_.refs_5_.refs_9_.refs_11_), channel_id=1, source_target_pairs={{0,2},{2,0},{4,6},{6,4},{8,10},{10,8},{12,14},{14,12},{1,3},{3,1},... | collective-permute-start | bytes 2064392 | tf_op jit(solution)/shard_map/ppermute | solution.py:782
  135.5 13.2 %collective-permute-start.14 = (bf16[2,64,1792]{2,1,0:T(8,128)(2,1)S(1)}, bf16[2,64,1792]{2,1,0:T(8,128)(2,1)S(1)}, u32[]{:S(2)}, u32[]{:S(2)}) collective-permute-start(bf16[2,64,1792]{2,1,0:T(8,128)(2,1)S(1)} %get-tuple-element.103), channel_id=1, source_target_pairs={{0,1},{1,0},{2,3},{3,2},{4,5},{5,4},{6,7},{7,6},{8,9},{9,8},{10,11... | collective-permute-start | bytes 1376264 | tf_op jit(solution)/shard_map/ppermute | solution.py:660
  137.5 16.0 %collective-permute-start.20 = (bf16[3,64,1792]{2,1,0:T(8,128)(2,1)S(1)}, bf16[3,64,1792]{2,1,0:T(8,128)(2,1)}, u32[]{:S(2)}, u32[]{:S(2)}) collective-permute-start(bf16[3,64,1792]{2,1,0:T(8,128)(2,1)S(1)} %collective-permute-done.16.refs_1_.refs_4_), channel_id=1, source_target_pairs={{0,2},{2,0},{4,6},{6,4},{8,10},{10,8},{12,14},{14,12},{1,3},{3,1},... | collective-permute-start | bytes 2064392 | tf_op jit(solution)/shard_map/ppermute | solution.py:782
  148.5 4.9 %collective-permute-start.19 = (bf16[3,64,1792]{2,1,0:T(8,128)(2,1)S(1)}, bf16[3,64,1792]{2,1,0:T(8,128)(2,1)}, u32[]{:S(2)}, u32[]{:S(2)}) collective-permute-start(bf16[3,64,1792]{2,1,0:T(8,128)(2,1)S(1)} %collective-permute-done.15.refs_0_.refs_2_), channel_id=1, source_target_pairs={{0,2},{2,0},{4,6},{6,4},{8,10},{10,8},{12,14},{14,12},{1,3},{3,1},... | collective-permute-start | bytes 2064392 | tf_op jit(solution)/shard_map/ppermute | solution.py:782
  149.5 4.0 %collective-permute-start.18 = (bf16[2,64,1792]{2,1,0:T(8,128)(2,1)}, bf16[2,64,1792]{2,1,0:T(8,128)(2,1)S(1)}, u32[]{:S(2)}, u32[]{:S(2)}) collective-permute-start(bf16[2,64,1792]{2,1,0:T(8,128)(2,1)} %add.62.refs_1_), channel_id=1, source_target_pairs={{0,2},{2,0},{4,6},{6,4},{8,10},{10,8},{12,14},{14,12},{1,3},{3,1},... | collective-permute-start | bytes 1376264 | tf_op jit(solution)/shard_map/ppermute | solution.py:782
  149.9 7.7 %collective-permute-start.22 = (bf16[2,64,1792]{2,1,0:T(8,128)(2,1)}, bf16[2,64,1792]{2,1,0:T(8,128)(2,1)S(1)}, u32[]{:S(2)}, u32[]{:S(2)}) collective-permute-start(bf16[2,64,1792]{2,1,0:T(8,128)(2,1)} %add.62.refs_1_), channel_id=1, source_target_pairs={{0,2},{2,0},{4,8},{6,10},{8,4},{10,6},{12,14},{14,12},{1,3},{3,1},... | collective-permute-start | bytes 1376264 | tf_op jit(solution)/shard_map/ppermute | solution.py:788
  150.0 14.0 %collective-permute-start.21 = (bf16[2,64,1792]{2,1,0:T(8,128)(2,1)}, bf16[2,64,1792]{2,1,0:T(8,128)(2,1)S(1)}, u32[]{:S(2)}, u32[]{:S(2)}) collective-permute-start(bf16[2,64,1792]{2,1,0:T(8,128)(2,1)} %add.62.refs_1_), channel_id=1, source_target_pairs={{0,4},{2,6},{4,0},{6,2},{8,12},{10,14},{12,8},{14,10},{1,5},{3,7},... | collective-permute-start | bytes 1376264 | tf_op jit(solution)/shard_map/ppermute | solution.py:785
  164.6 2.5 %collective-permute-start.23 = (bf16[2,2,64,1792]{3,2,1,0:T(8,128)(2,1)S(1)}, bf16[2,2,64,1792]{3,2,1,0:T(8,128)(2,1)S(1)}, u32[]{:S(2)}, u32[]{:S(2)}) collective-permute-start(bf16[2,2,64,1792]{3,2,1,0:T(8,128)(2,1)S(1)} %late.1), channel_id=1, source_target_pairs={{0,2},{2,0},{4,6},{6,4},{8,10},{10,8},{12,14},{14,12},{1,3},{3,1},... | collective-permute-start | bytes 2752520 | tf_op jit(solution)/shard_map/ppermute | solution.py:782
  (3 other events, 4.7 us)

commit v7 on v6

--- a/solution.py
+++ b/solution.py
@@ -499,9 +499,9 @@
     )(own, other, rows_params, b_qkv, in_hbm(w_qkv), *after)
 
 
-UP_TILE = 1536
+UP_TILE = 768
 DOWN_TILE = 256
-SLOTS = 3
+SLOTS = 4
 
 
 def mlp_kernel(n_after, own_ref, other_ref, mine_ref, theirs_ref, rows_ref, b_up_ref, w_mine, w_theirs,

time: 182 us -> 182 us (level)
  waiting for transfers between devices: 46.5 us -> 51.4 us
  starting transfers between devices: 27.6 us -> 22.9 us
    ppermute x4, starting transfers between devices: 12 us -> 8.78 us  [to_pair(): return lax.ppermute(value, 'dp', pairs)]
    ppermute x4, waiting for transfers between devices: 28.9 us -> 31.4 us  [to_pair(): return lax.ppermute(value, 'dp', pairs)]
where the time goes in v7:
time: 182 us
  Pallas kernels  90.7 us (50%)
  waiting for transfers between devices  51.4 us (28%)
  starting transfers between devices  22.9 us (13%)
  between operations  14.9 us (8%)
    pallas_call x2, Pallas kernels, mlp(): pl.pallas_call(functools.partial(mlp_kernel, len(after)), out_shape=(jax....  40.1 us
    ppermute x4, waiting for transfers between devices, to_pair(): return lax.ppermute(value, 'dp', pairs)  31.4 us
    pallas_call x2, Pallas kernels, attend(): pl.pallas_call(functools.partial(attend_kernel, len(after)), out_shape=ja...  18.8 us
    ppermute x7, waiting for transfers between devices, swap(): return lax.ppermute(value, 'tensor', [(0, 1), (1, 0)])  15.8 us
    pallas_call x4, Pallas kernels, choose(): pl.pallas_call(functools.partial(choose_kernel, parts, len(sources)), out...  11.6 us
    ppermute x7, starting transfers between devices, swap(): return lax.ppermute(value, 'tensor', [(0, 1), (1, 0)])  8.98 us
    ppermute x4, starting transfers between devices, to_pair(): return lax.ppermute(value, 'dp', pairs)  8.78 us
    pallas_call x1, Pallas kernels, merge(): pl.pallas_call(functools.partial(merge_kernel, kept_count.shape[0]), out_...  7.03 us
  transfers between devices with their start and end apart: 24, of which 9 were waited for; matrix products, arithmetic and copies ran while one was open for 0% of the time, Pallas kernels for 40%

profile of v7, /device:TPU:0, one launch (start us, length us, event | category | flops | bytes accessed | tf_op | source)
XLA Modules:
  0.0 181.9 jit_solution(7015825626556694260)
XLA Ops:
  6.5 5.5 %pack.1 = (bf16[8,64,1792]{2,1,0:T(8,128)(2,1)}, bf16[8,64,1792]{2,1,0:T(8,128)(2,1)S(1)}) custom-call(s32[1]{0:T(128)} %bitcast.19.device_ref, s32[8]{0:T(128)} %count_ref.5, s32[16]{0:T(128)} %bitcast.44, bf16[64,16,1792]{2,1,0:T(8,128)(2,1)} %bitcast.42), custom_call_target="tpu_custom_call" | custom-call | tf_op jit(solution)/shard_map/pack/pallas_call | solution.py:224
  13.7 2.6 %collective-permute-start.6 = (bf16[224,1792]{1,0:T(8,128)(2,1)S(1)}, bf16[224,1792]{1,0:T(8,128)(2,1)S(1)}, u32[]{:S(2)}, u32[]{:S(2)}) collective-permute-start(bf16[224,1792]{1,0:T(8,128)(2,1)S(1)} %w_piece.1), channel_id=1, source_target_pairs={{0,1},{1,0},{2,3},{3,2},{4,5},{5,4},{6,7},{7,6},{8,9},{9,8},{10,11... | collective-permute-start | bytes 2408456 | tf_op jit(solution)/shard_map/ppermute | solution.py:660
  16.3 2.0 %plan.1.table_ref = s32[94]{0:T(128)S(1)} custom-call(s32[1]{0:T(128)} %bitcast.19.device_ref, s32[8]{0:T(128)} %count_ref.5), custom_call_target="tpu_custom_call" | custom-call | flops 1000 | bytes 1000 | tf_op jit(solution)/shard_map/plan/pallas_call | solution.py:166
  18.3 3.1 %send.1 = (bf16[3,64,1792]{2,1,0:T(8,128)(2,1)S(1)}, bf16[2,64,1792]{2,1,0:T(8,128)(2,1)S(1)}, bf16[3,64,1792]{2,1,0:T(8,128)(2,1)S(1)}, bf16[2,64,1792]{2,1,0:T(8,128)(2,1)S(1)}) custom-call(s32[94]{0:T(128)S(1)} %plan.1.table_ref, bf16[8,64,1792]{2,1,0:T(8,128)(2,1)S(1)} %copy-done.5, bf16[8,64,1792]{2,1,0:T(8,128)(2,1)} %collective-permute-done.1.refs_1_), custom_call_target="tpu_custom_call" | custom-call | flops 1000 | bytes 1000 | tf_op jit(solution)/shard_map/send/pallas_call | solution.py:352
  22.3 1.6 collective-permute-start.2
  25.1 2.0 %collective-permute-start = (f32[1]{0:T(128)}, f32[1]{0:T(128)}, u32[]{:S(2)}, u32[]{:S(2)}) collective-permute-start(f32[1]{0:T(128)} %convert_element_type.8), channel_id=1, source_target_pairs={{0,16},{16,0},{1,17},{17,1},{2,18},{18,2},{3,19},{19,3},{4,20},{20... | collective-permute-start | bytes 20 | tf_op jit(solution)/shard_map/ppermute | solution.py:795
  27.0 1.7 collective-permute-done
  29.4 5.5 %collective-permute-done.6.refs_0_.near = bf16[224,1792]{1,0:T(8,128)(2,1)S(1)} collective-permute-done((bf16[224,1792]{1,0:T(8,128)(2,1)S(1)}, bf16[224,1792]{1,0:T(8,128)(2,1)S(1)}, u32[]{:S(2)}, u32[]{:S(2)}) %collective-permute-start.6) | collective-permute-done | bytes 802848 | tf_op jit(solution)/shard_map/ppermute | solution.py:660
  35.9 1.8 %collective-permute-start.7 = (bf16[1,224,1792]{2,1,0:T(8,128)(2,1)}, bf16[1,224,1792]{2,1,0:T(8,128)(2,1)S(1)}, u32[]{:S(2)}, u32[]{:S(2)}) collective-permute-start(bf16[1,224,1792]{2,1,0:T(8,128)(2,1)} %w_near.1), channel_id=1, source_target_pairs={{0,16},{16,0},{1,17},{17,1},{2,18},{18,2},{3,19},{19,3},{4,20},{20... | collective-permute-start | bytes 2408456 | tf_op jit(solution)/shard_map/ppermute | solution.py:852
  37.7 2.5 %collective-permute-done.2 = bf16[3,64,1792]{2,1,0:T(8,128)(2,1)} collective-permute-done((bf16[3,64,1792]{2,1,0:T(8,128)(2,1)S(1)}, bf16[3,64,1792]{2,1,0:T(8,128)(2,1)}, u32[]{:S(2)}, u32[]{:S(2)}) %collective-permute-start.2) | collective-permute-done | bytes 688160 | tf_op jit(solution)/shard_map/ppermute | solution.py:785
  40.2 2.6 %conditional.3 = (bf16[3,64,1792]{2,1,0:T(8,128)(2,1)}) conditional(s32[]{:T(128)} %convert_element_type.9, (s32[94]{0:T(128)S(1)}, bf16[8,64,1792]{2,1,0:T(8,128)(2,1)}, bf16[8,64,1792]{2,1,0:T(8,128)(2,1)}, bf16[3,64,1792]{2,1,0:T(8,128)(2,1)}, bf16[3,64,1792]{2,1,0:T(8,128)(2,1)}) %tuple.25, (s32[94]{0:T(128)S(1)}, bf16[8,64,1792]{2,1,0:T(8,128)(2,1)}, ...), branch_computations={%region_0.0_spmd, %region_1.0_spmd} | conditional | flops 689146 | bytes 62391604 | solution.py:829
  40.2 2.6 %deal_0.1 = bf16[3,64,1792]{2,1,0:T(8,128)(2,1)} custom-call(s32[94]{0:T(128)S(1)} %get-tuple-element.58.table_ref, bf16[8,64,1792]{2,1,0:T(8,128)(2,1)} %get-tuple-element.60.refs_0_, bf16[8,64,1792]{2,1,0:T(8,128)(2,1)} %get-tuple-element.62.refs_1_, bf16[3,64,1792]{2,1,0:T(8,128)(2,1)} %get-tuple-element.63.refs_2_.refs_3_, ...), custom_call_target="tpu_custom_call" | custom-call | flops 1000 | bytes 1000 | tf_op jit(solution)/shard_map/cond/branch_0_fun/deal_0/pallas_call | solution.py:352
  43.4 1.8 collective-permute-start.8
  45.4 9.8 %collective-permute-done.8 = bf16[2,64,1792]{2,1,0:T(8,128)(2,1)} collective-permute-done((bf16[2,64,1792]{2,1,0:T(8,128)(2,1)S(1)}, bf16[2,64,1792]{2,1,0:T(8,128)(2,1)}, u32[]{:S(2)}, u32[]{:S(2)}) %collective-permute-start.8) | collective-permute-done | bytes 458784 | tf_op jit(solution)/shard_map/ppermute | solution.py:785
  55.2 1.8 conditional.4
  55.2 1.6 deal_1.1
  57.0 1.7 collective-permute-start.11
  59.0 2.5 %collective-permute-done.4.other_ref = bf16[3,64,1792]{2,1,0:T(8,128)(2,1)S(1)} collective-permute-done((bf16[3,64,1792]{2,1,0:T(8,128)(2,1)}, bf16[3,64,1792]{2,1,0:T(8,128)(2,1)S(1)}, u32[]{:S(2)}, u32[]{:S(2)}) %collective-permute-start.4) | collective-permute-done | bytes 688160 | tf_op jit(solution)/shard_map/ppermute | solution.py:660
  61.5 11.2 %attend.2.mine_ref = bf16[2,3,64,896]{3,2,1,0:T(8,128)(2,1)S(1)} custom-call(bf16[3,64,1792]{2,1,0:T(8,128)(2,1)} %get-tuple-element.133.own_ref, bf16[3,64,1792]{2,1,0:T(8,128)(2,1)S(1)} %collective-permute-done.4.other_ref, f32[6,1792]{1,0:T(8,128)S(1)} %stack.48.rows_ref, f32[3,896]{1,0:T(4,128)S(1)} %copy-done.4, bf16[3,1792,896]{2,1,0:T(8,128)(2,1)} %w_ref.5), custom_call_target="tpu_custom_call" | custom-call | flops 14797504512 | bytes 9633792 | tf_op jit(solution)/shard_map/attend/pallas_call | solution.py:483
  72.8 7.6 %attend.3.refs_0_.mine_ref = bf16[2,2,64,896]{3,2,1,0:T(8,128)(2,1)S(1)} custom-call(bf16[2,64,1792]{2,1,0:T(8,128)(2,1)S(1)} %get-tuple-element.134.refs_2_.own_ref, bf16[2,64,1792]{2,1,0:T(8,128)(2,1)S(1)} %collective-permute-done.11.other_ref, f32[6,1792]{1,0:T(8,128)S(1)} %stack.48.rows_ref, f32[3,896]{1,0:T(4,128)S(1)} %copy-done.4, ...), custom_call_target="tpu_custom_call" | custom-call | flops 9865003008 | bytes 9633792 | tf_op jit(solution)/shard_map/attend/pallas_call | solution.py:483
  80.4 2.1 %collective-permute-start.13 = (bf16[2,2,64,896]{3,2,1,0:T(8,128)(2,1)S(1)}, bf16[2,2,64,896]{3,2,1,0:T(8,128)(2,1)S(1)}, u32[]{:S(2)}, u32[]{:S(2)}) collective-permute-start(bf16[2,2,64,896]{3,2,1,0:T(8,128)(2,1)S(1)} %attend.3.refs_0_.mine_ref), channel_id=1, source_target_pairs={{0,1},{1,0},{2,3},{3,2},{4,5},{5,4},{6,7},{7,6},{8,9},{9,8},{10,11... | collective-permute-start | bytes 1376264 | tf_op jit(solution)/shard_map/ppermute | solution.py:660
  83.4 7.8 %collective-permute-done.5.theirs_ref = bf16[2,3,64,896]{3,2,1,0:T(8,128)(2,1)S(1)} collective-permute-done((bf16[2,3,64,896]{3,2,1,0:T(8,128)(2,1)S(1)}, bf16[2,3,64,896]{3,2,1,0:T(8,128)(2,1)S(1)}, u32[]{:S(2)}, u32[]{:S(2)}) %collective-permute-start.5) | collective-permute-done | bytes 688160 | tf_op jit(solution)/shard_map/ppermute | solution.py:660
  91.2 23.5 %mlp.2 = (f32[3,64,1792]{2,1,0:T(8,128)S(1)}, bf16[3,64,1792]{2,1,0:T(8,128)(2,1)S(1)}) custom-call(bf16[3,64,1792]{2,1,0:T(8,128)(2,1)} %get-tuple-element.133.own_ref, bf16[3,64,1792]{2,1,0:T(8,128)(2,1)S(1)} %collective-permute-done.4.other_ref, bf16[2,3,64,896]{3,2,1,0:T(8,128)(2,1)S(1)} %attend.2.mine_ref, ...), custom_call_target="tpu_custom_call" | custom-call | flops 30299652096 | bytes 39452672 | tf_op jit(solution)/shard_map/mlp/pallas_call | solution.py:609
  114.8 16.5 %mlp.3 = (f32[2,64,1792]{2,1,0:T(8,128)S(1)}, bf16[2,64,1792]{2,1,0:T(8,128)(2,1)S(1)}) custom-call(bf16[2,64,1792]{2,1,0:T(8,128)(2,1)S(1)} %get-tuple-element.134.refs_2_.own_ref, bf16[2,64,1792]{2,1,0:T(8,128)(2,1)S(1)} %collective-permute-done.11.other_ref, bf16[2,2,64,896]{3,2,1,0:T(8,128)(2,1)S(1)} %attend.3.refs_0_.mine_ref, ...), custom_call_target="tpu_custom_call" | custom-call | flops 20199768064 | bytes 39452672 | tf_op jit(solution)/shard_map/mlp/pallas_call | solution.py:609
  132.4 3.4 %collective-permute-start.15 = (bf16[3,64,1792]{2,1,0:T(8,128)(2,1)}, bf16[3,64,1792]{2,1,0:T(8,128)(2,1)S(1)}, u32[]{:S(2)}, u32[]{:S(2)}) collective-permute-start(bf16[3,64,1792]{2,1,0:T(8,128)(2,1)} %add.61.refs_0_.refs_3_.refs_5_.refs_9_.refs_11_), channel_id=1, source_target_pairs={{0,4},{2,6},{4,0},{6,2},{8,12},{10,14},{12,8},{14,10},{1,5},{3,7},... | collective-permute-start | bytes 2064392 | tf_op jit(solution)/shard_map/ppermute | solution.py:785
  135.8 2.0 %collective-permute-start.14 = (bf16[2,64,1792]{2,1,0:T(8,128)(2,1)S(1)}, bf16[2,64,1792]{2,1,0:T(8,128)(2,1)S(1)}, u32[]{:S(2)}, u32[]{:S(2)}) collective-permute-start(bf16[2,64,1792]{2,1,0:T(8,128)(2,1)S(1)} %get-tuple-element.103), channel_id=1, source_target_pairs={{0,1},{1,0},{2,3},{3,2},{4,5},{5,4},{6,7},{7,6},{8,9},{9,8},{10,11... | collective-permute-start | bytes 1376264 | tf_op jit(solution)/shard_map/ppermute | solution.py:660
  138.0 12.4 %collective-permute-done.15.refs_0_.refs_2_ = bf16[3,64,1792]{2,1,0:T(8,128)(2,1)S(1)} collective-permute-done((bf16[3,64,1792]{2,1,0:T(8,128)(2,1)}, bf16[3,64,1792]{2,1,0:T(8,128)(2,1)S(1)}, u32[]{:S(2)}, u32[]{:S(2)}) %collective-permute-start.15) | collective-permute-done | bytes 688160 | tf_op jit(solution)/shard_map/ppermute | solution.py:785
  151.8 2.0 %collective-permute-start.21 = (bf16[2,64,1792]{2,1,0:T(8,128)(2,1)}, bf16[2,64,1792]{2,1,0:T(8,128)(2,1)S(1)}, u32[]{:S(2)}, u32[]{:S(2)}) collective-permute-start(bf16[2,64,1792]{2,1,0:T(8,128)(2,1)} %add.62.refs_1_), channel_id=1, source_target_pairs={{0,4},{2,6},{4,0},{6,2},{8,12},{10,14},{12,8},{14,10},{1,5},{3,7},... | collective-permute-start | bytes 1376264 | tf_op jit(solution)/shard_map/ppermute | solution.py:785
  153.8 4.2 %gather.11.refs_2_.found_ref = bf16[16,64,1792]{2,1,0:T(8,128)(2,1)S(1)} custom-call(s32[16]{0:T(128)S(1)} %broadcast_select_fusion.2.table_ref.code_ref, bf16[3,64,1792]{2,1,0:T(8,128)(2,1)} %add.61.refs_0_.refs_3_.refs_5_.refs_9_.refs_11_, bf16[2,64,1792]{2,1,0:T(8,128)(2,1)} %add.62.refs_1_, ...), custom_call_target="tpu_custom_call" | custom-call | flops 1000 | bytes 1000 | tf_op jit(solution)/shard_map/gather/pallas_call | solution.py:352
  158.1 6.8 %collective-permute-done.21.refs_0_ = bf16[2,64,1792]{2,1,0:T(8,128)(2,1)S(1)} collective-permute-done((bf16[2,64,1792]{2,1,0:T(8,128)(2,1)}, bf16[2,64,1792]{2,1,0:T(8,128)(2,1)S(1)}, u32[]{:S(2)}, u32[]{:S(2)}) %collective-permute-start.21) | collective-permute-done | bytes 458784 | tf_op jit(solution)/shard_map/ppermute | solution.py:785
  165.6 2.5 %collective-permute-done.23 = bf16[2,2,64,1792]{3,2,1,0:T(8,128)(2,1)S(1)} collective-permute-done((bf16[2,2,64,1792]{3,2,1,0:T(8,128)(2,1)S(1)}, bf16[2,2,64,1792]{3,2,1,0:T(8,128)(2,1)S(1)}, u32[]{:S(2)}, u32[]{:S(2)}) %collective-permute-start.23) | collective-permute-done | bytes 917536 | tf_op jit(solution)/shard_map/ppermute | solution.py:782
  168.0 7.0 %merge.1 = bf16[64,16,1792]{2,1,0:T(8,128)(2,1)} custom-call(s32[1]{0:T(128)} %bitcast.19.device_ref, s32[8]{0:T(128)} %count_ref.5, s32[16]{0:T(128)} %bitcast.45, s32[16]{0:T(128)S(1)} %broadcast_select_fusion.2.table_ref.code_ref, bf16[64,16,1792]{2,1,0:T(8,128)(2,1)} %bitcast.43, bf16[16,64,1792]{2,1,0:T(8,128)(2,1)S(1)} %gather.11.refs_2_.found_ref, ...), custom_call_target="tpu_custom_call" | custom-call | flops 1000 | bytes 1000 | tf_op jit(solution)/shard_map/merge/pallas_call | solution.py:297
  (70 shorter events, 9.4 us)
Async XLA Ops:
  12.0 6.3 %collective-permute-start.1 = (bf16[8,64,1792]{2,1,0:T(8,128)(2,1)S(1)}, bf16[8,64,1792]{2,1,0:T(8,128)(2,1)}, u32[]{:S(2)}, u32[]{:S(2)}) collective-permute-start(bf16[8,64,1792]{2,1,0:T(8,128)(2,1)S(1)} %get-tuple-element.95.refs_0_), channel_id=1, source_target_pairs={{0,2},{2,0},{4,6},{6,4},{8,10},{10,8},{12,14},{14,12},{1,3},{3,1},... | collective-permute-start | bytes 5505032 | tf_op jit(solution)/shard_map/ppermute | solution.py:782
  12.5 5.9 %copy-start.5 = (bf16[8,64,1792]{2,1,0:T(8,128)(2,1)S(1)}, bf16[8,64,1792]{2,1,0:T(8,128)(2,1)}, u32[]{:S(2)}) copy-start(bf16[8,64,1792]{2,1,0:T(8,128)(2,1)} %get-tuple-element.94.refs_0_) | copy-start | bytes 5505028
  13.7 21.1 %collective-permute-start.6 = (bf16[224,1792]{1,0:T(8,128)(2,1)S(1)}, bf16[224,1792]{1,0:T(8,128)(2,1)S(1)}, u32[]{:S(2)}, u32[]{:S(2)}) collective-permute-start(bf16[224,1792]{1,0:T(8,128)(2,1)S(1)} %w_piece.1), channel_id=1, source_target_pairs={{0,1},{1,0},{2,3},{3,2},{4,5},{5,4},{6,7},{7,6},{8,9},{9,8},{10,11... | collective-permute-start | bytes 2408456 | tf_op jit(solution)/shard_map/ppermute | solution.py:660
  22.3 17.9 %collective-permute-start.2 = (bf16[3,64,1792]{2,1,0:T(8,128)(2,1)S(1)}, bf16[3,64,1792]{2,1,0:T(8,128)(2,1)}, u32[]{:S(2)}, u32[]{:S(2)}) collective-permute-start(bf16[3,64,1792]{2,1,0:T(8,128)(2,1)S(1)} %get-tuple-element.96), channel_id=1, source_target_pairs={{0,4},{2,6},{4,0},{6,2},{8,12},{10,14},{12,8},{14,10},{1,5},{3,7},... | collective-permute-start | bytes 2064392 | tf_op jit(solution)/shard_map/ppermute | solution.py:785
  23.9 16.2 %collective-permute-start.3 = (bf16[3,64,1792]{2,1,0:T(8,128)(2,1)S(1)}, bf16[3,64,1792]{2,1,0:T(8,128)(2,1)}, u32[]{:S(2)}, u32[]{:S(2)}) collective-permute-start(bf16[3,64,1792]{2,1,0:T(8,128)(2,1)S(1)} %get-tuple-element.97), channel_id=1, source_target_pairs={{0,2},{2,0},{4,8},{6,10},{8,4},{10,6},{12,14},{14,12},{1,3},{3,1},... | collective-permute-start | bytes 2064392 | tf_op jit(solution)/shard_map/ppermute | solution.py:788
  25.1 3.7 %collective-permute-start = (f32[1]{0:T(128)}, f32[1]{0:T(128)}, u32[]{:S(2)}, u32[]{:S(2)}) collective-permute-start(f32[1]{0:T(128)} %convert_element_type.8), channel_id=1, source_target_pairs={{0,16},{16,0},{1,17},{17,1},{2,18},{18,2},{3,19},{19,3},{4,20},{20... | collective-permute-start | bytes 20 | tf_op jit(solution)/shard_map/ppermute | solution.py:795
  35.9 22.9 %collective-permute-start.7 = (bf16[1,224,1792]{2,1,0:T(8,128)(2,1)}, bf16[1,224,1792]{2,1,0:T(8,128)(2,1)S(1)}, u32[]{:S(2)}, u32[]{:S(2)}) collective-permute-start(bf16[1,224,1792]{2,1,0:T(8,128)(2,1)} %w_near.1), channel_id=1, source_target_pairs={{0,16},{16,0},{1,17},{17,1},{2,18},{18,2},{3,19},{19,3},{4,20},{20... | collective-permute-start | bytes 2408456 | tf_op jit(solution)/shard_map/ppermute | solution.py:852
  40.2 5.0 %copy-start.7 = (f32[1792]{0:T(1024)S(1)}, f32[1792]{0:T(1024)}, u32[]{:S(2)}) copy-start(f32[1792]{0:T(1024)} %param.26) | copy-start | bytes 21508
  40.2 5.0 %copy-start.8 = (f32[1792]{0:T(1024)S(1)}, f32[1792]{0:T(1024)}, u32[]{:S(2)}) copy-start(f32[1792]{0:T(1024)} %param.27) | copy-start | bytes 21508
  40.2 5.0 %copy-start.9 = (f32[1792]{0:T(1024)S(1)}, f32[1792]{0:T(1024)}, u32[]{:S(2)}) copy-start(f32[1792]{0:T(1024)} %param.31) | copy-start | bytes 21508
  40.2 5.0 %copy-start.10 = (f32[1792]{0:T(1024)S(1)}, f32[1792]{0:T(1024)}, u32[]{:S(2)}) copy-start(f32[1792]{0:T(1024)} %param.32) | copy-start | bytes 21508
  40.2 5.0 %copy-start.11 = (f32[1792]{0:T(1024)S(1)}, f32[1792]{0:T(1024)}, u32[]{:S(2)}) copy-start(f32[1792]{0:T(1024)} %param.33) | copy-start | bytes 21508
  40.2 5.0 %copy-start.12 = (f32[1792]{0:T(1024)S(1)}, f32[1792]{0:T(1024)}, u32[]{:S(2)}) copy-start(f32[1792]{0:T(1024)} %param.37) | copy-start | bytes 21508
  40.2 5.0 %copy-start.6 = (f32[4608]{0:T(1024)S(1)}, f32[4608]{0:T(1024)}, u32[]{:S(2)}) copy-start(f32[4608]{0:T(1024)} %param.35) | copy-start | bytes 55300
  42.9 18.6 %collective-permute-start.4 = (bf16[3,64,1792]{2,1,0:T(8,128)(2,1)}, bf16[3,64,1792]{2,1,0:T(8,128)(2,1)S(1)}, u32[]{:S(2)}, u32[]{:S(2)}) collective-permute-start(bf16[3,64,1792]{2,1,0:T(8,128)(2,1)} %get-tuple-element.133.own_ref), channel_id=1, source_target_pairs={{0,1},{1,0},{2,3},{3,2},{4,5},{5,4},{6,7},{7,6},{8,9},{9,8},{10,11... | collective-permute-start | bytes 2064392 | tf_op jit(solution)/shard_map/ppermute | solution.py:660
  43.4 11.8 %collective-permute-start.8 = (bf16[2,64,1792]{2,1,0:T(8,128)(2,1)S(1)}, bf16[2,64,1792]{2,1,0:T(8,128)(2,1)}, u32[]{:S(2)}, u32[]{:S(2)}) collective-permute-start(bf16[2,64,1792]{2,1,0:T(8,128)(2,1)S(1)} %copy-done.3), channel_id=1, source_target_pairs={{0,4},{2,6},{4,0},{6,2},{8,12},{10,14},{12,8},{14,10},{1,5},{3,7},... | collective-permute-start | bytes 1376264 | tf_op jit(solution)/shard_map/ppermute | solution.py:785
  45.1 10.1 %collective-permute-start.9 = (bf16[2,64,1792]{2,1,0:T(8,128)(2,1)S(1)}, bf16[2,64,1792]{2,1,0:T(8,128)(2,1)}, u32[]{:S(2)}, u32[]{:S(2)}) collective-permute-start(bf16[2,64,1792]{2,1,0:T(8,128)(2,1)S(1)} %get-tuple-element.99), channel_id=1, source_target_pairs={{0,2},{2,0},{4,8},{6,10},{8,4},{10,6},{12,14},{14,12},{1,3},{3,1},... | collective-permute-start | bytes 1376264 | tf_op jit(solution)/shard_map/ppermute | solution.py:788
  57.0 15.8 %collective-permute-start.11 = (bf16[2,64,1792]{2,1,0:T(8,128)(2,1)S(1)}, bf16[2,64,1792]{2,1,0:T(8,128)(2,1)S(1)}, u32[]{:S(2)}, u32[]{:S(2)}) collective-permute-start(bf16[2,64,1792]{2,1,0:T(8,128)(2,1)S(1)} %get-tuple-element.134.refs_2_.own_ref), channel_id=1, source_target_pairs={{0,1},{1,0},{2,3},{3,2},{4,5},{5,4},{6,7},{7,6},{8,9},{9,8},{10,11... | collective-permute-start | bytes 1376264 | tf_op jit(solution)/shard_map/ppermute | solution.py:660
  58.9 23.6 %collective-permute-start.10 = (bf16[2,224,1792]{2,1,0:T(8,128)(2,1)S(1)}, bf16[2,224,1792]{2,1,0:T(8,128)(2,1)S(1)}, u32[]{:S(2)}, u32[]{:S(2)}) collective-permute-start(bf16[2,224,1792]{2,1,0:T(8,128)(2,1)S(1)} %w_both.1), channel_id=1, source_target_pairs={{0,2},{2,0},{4,6},{6,4},{8,10},{10,8},{12,14},{14,12},{1,3},{3,1},... | collective-permute-start | bytes 4816904 | tf_op jit(solution)/shard_map/ppermute | solution.py:724
  72.7 18.4 %collective-permute-start.5 = (bf16[2,3,64,896]{3,2,1,0:T(8,128)(2,1)S(1)}, bf16[2,3,64,896]{3,2,1,0:T(8,128)(2,1)S(1)}, u32[]{:S(2)}, u32[]{:S(2)}) collective-permute-start(bf16[2,3,64,896]{3,2,1,0:T(8,128)(2,1)S(1)} %attend.2.mine_ref), channel_id=1, source_target_pairs={{0,1},{1,0},{2,3},{3,2},{4,5},{5,4},{6,7},{7,6},{8,9},{9,8},{10,11... | collective-permute-start | bytes 2064392 | tf_op jit(solution)/shard_map/ppermute | solution.py:660
  80.4 34.4 %collective-permute-start.13 = (bf16[2,2,64,896]{3,2,1,0:T(8,128)(2,1)S(1)}, bf16[2,2,64,896]{3,2,1,0:T(8,128)(2,1)S(1)}, u32[]{:S(2)}, u32[]{:S(2)}) collective-permute-start(bf16[2,2,64,896]{3,2,1,0:T(8,128)(2,1)S(1)} %attend.3.refs_0_.mine_ref), channel_id=1, source_target_pairs={{0,1},{1,0},{2,3},{3,2},{4,5},{5,4},{6,7},{7,6},{8,9},{9,8},{10,11... | collective-permute-start | bytes 1376264 | tf_op jit(solution)/shard_map/ppermute | solution.py:660
  114.7 16.6 %collective-permute-start.12 = (bf16[3,64,1792]{2,1,0:T(8,128)(2,1)S(1)}, bf16[3,64,1792]{2,1,0:T(8,128)(2,1)S(1)}, u32[]{:S(2)}, u32[]{:S(2)}) collective-permute-start(bf16[3,64,1792]{2,1,0:T(8,128)(2,1)S(1)} %get-tuple-element.101), channel_id=1, source_target_pairs={{0,1},{1,0},{2,3},{3,2},{4,5},{5,4},{6,7},{7,6},{8,9},{9,8},{10,11... | collective-permute-start | bytes 2064392 | tf_op jit(solution)/shard_map/ppermute | solution.py:660
  132.4 5.4 %collective-permute-start.16 = (bf16[3,64,1792]{2,1,0:T(8,128)(2,1)}, bf16[3,64,1792]{2,1,0:T(8,128)(2,1)S(1)}, u32[]{:S(2)}, u32[]{:S(2)}) collective-permute-start(bf16[3,64,1792]{2,1,0:T(8,128)(2,1)} %add.61.refs_0_.refs_3_.refs_5_.refs_9_.refs_11_), channel_id=1, source_target_pairs={{0,2},{2,0},{4,8},{6,10},{8,4},{10,6},{12,14},{14,12},{1,3},{3,1},... | collective-permute-start | bytes 2064392 | tf_op jit(solution)/shard_map/ppermute | solution.py:788
  132.4 18.1 %collective-permute-start.15 = (bf16[3,64,1792]{2,1,0:T(8,128)(2,1)}, bf16[3,64,1792]{2,1,0:T(8,128)(2,1)S(1)}, u32[]{:S(2)}, u32[]{:S(2)}) collective-permute-start(bf16[3,64,1792]{2,1,0:T(8,128)(2,1)} %add.61.refs_0_.refs_3_.refs_5_.refs_9_.refs_11_), channel_id=1, source_target_pairs={{0,4},{2,6},{4,0},{6,2},{8,12},{10,14},{12,8},{14,10},{1,5},{3,7},... | collective-permute-start | bytes 2064392 | tf_op jit(solution)/shard_map/ppermute | solution.py:785
  135.8 16.0 %collective-permute-start.17 = (bf16[3,64,1792]{2,1,0:T(8,128)(2,1)}, bf16[3,64,1792]{2,1,0:T(8,128)(2,1)S(1)}, u32[]{:S(2)}, u32[]{:S(2)}) collective-permute-start(bf16[3,64,1792]{2,1,0:T(8,128)(2,1)} %add.61.refs_0_.refs_3_.refs_5_.refs_9_.refs_11_), channel_id=1, source_target_pairs={{0,2},{2,0},{4,6},{6,4},{8,10},{10,8},{12,14},{14,12},{1,3},{3,1},... | collective-permute-start | bytes 2064392 | tf_op jit(solution)/shard_map/ppermute | solution.py:782
  135.8 14.6 %collective-permute-start.14 = (bf16[2,64,1792]{2,1,0:T(8,128)(2,1)S(1)}, bf16[2,64,1792]{2,1,0:T(8,128)(2,1)S(1)}, u32[]{:S(2)}, u32[]{:S(2)}) collective-permute-start(bf16[2,64,1792]{2,1,0:T(8,128)(2,1)S(1)} %get-tuple-element.103), channel_id=1, source_target_pairs={{0,1},{1,0},{2,3},{3,2},{4,5},{5,4},{6,7},{7,6},{8,9},{9,8},{10,11... | collective-permute-start | bytes 1376264 | tf_op jit(solution)/shard_map/ppermute | solution.py:660
  137.8 16.0 %collective-permute-start.20 = (bf16[3,64,1792]{2,1,0:T(8,128)(2,1)S(1)}, bf16[3,64,1792]{2,1,0:T(8,128)(2,1)}, u32[]{:S(2)}, u32[]{:S(2)}) collective-permute-start(bf16[3,64,1792]{2,1,0:T(8,128)(2,1)S(1)} %collective-permute-done.16.refs_1_.refs_4_), channel_id=1, source_target_pairs={{0,2},{2,0},{4,6},{6,4},{8,10},{10,8},{12,14},{14,12},{1,3},{3,1},... | collective-permute-start | bytes 2064392 | tf_op jit(solution)/shard_map/ppermute | solution.py:782
  150.4 3.4 %collective-permute-start.19 = (bf16[3,64,1792]{2,1,0:T(8,128)(2,1)S(1)}, bf16[3,64,1792]{2,1,0:T(8,128)(2,1)}, u32[]{:S(2)}, u32[]{:S(2)}) collective-permute-start(bf16[3,64,1792]{2,1,0:T(8,128)(2,1)S(1)} %collective-permute-done.15.refs_0_.refs_2_), channel_id=1, source_target_pairs={{0,2},{2,0},{4,6},{6,4},{8,10},{10,8},{12,14},{14,12},{1,3},{3,1},... | collective-permute-start | bytes 2064392 | tf_op jit(solution)/shard_map/ppermute | solution.py:782
  151.3 2.5 %collective-permute-start.18 = (bf16[2,64,1792]{2,1,0:T(8,128)(2,1)}, bf16[2,64,1792]{2,1,0:T(8,128)(2,1)S(1)}, u32[]{:S(2)}, u32[]{:S(2)}) collective-permute-start(bf16[2,64,1792]{2,1,0:T(8,128)(2,1)} %add.62.refs_1_), channel_id=1, source_target_pairs={{0,2},{2,0},{4,6},{6,4},{8,10},{10,8},{12,14},{14,12},{1,3},{3,1},... | collective-permute-start | bytes 1376264 | tf_op jit(solution)/shard_map/ppermute | solution.py:782
  151.8 6.3 %collective-permute-start.22 = (bf16[2,64,1792]{2,1,0:T(8,128)(2,1)}, bf16[2,64,1792]{2,1,0:T(8,128)(2,1)S(1)}, u32[]{:S(2)}, u32[]{:S(2)}) collective-permute-start(bf16[2,64,1792]{2,1,0:T(8,128)(2,1)} %add.62.refs_1_), channel_id=1, source_target_pairs={{0,2},{2,0},{4,8},{6,10},{8,4},{10,6},{12,14},{14,12},{1,3},{3,1},... | collective-permute-start | bytes 1376264 | tf_op jit(solution)/shard_map/ppermute | solution.py:788
  151.8 13.1 %collective-permute-start.21 = (bf16[2,64,1792]{2,1,0:T(8,128)(2,1)}, bf16[2,64,1792]{2,1,0:T(8,128)(2,1)S(1)}, u32[]{:S(2)}, u32[]{:S(2)}) collective-permute-start(bf16[2,64,1792]{2,1,0:T(8,128)(2,1)} %add.62.refs_1_), channel_id=1, source_target_pairs={{0,4},{2,6},{4,0},{6,2},{8,12},{10,14},{12,8},{14,10},{1,5},{3,7},... | collective-permute-start | bytes 1376264 | tf_op jit(solution)/shard_map/ppermute | solution.py:785
  165.5 2.5 %collective-permute-start.23 = (bf16[2,2,64,1792]{3,2,1,0:T(8,128)(2,1)S(1)}, bf16[2,2,64,1792]{3,2,1,0:T(8,128)(2,1)S(1)}, u32[]{:S(2)}, u32[]{:S(2)}) collective-permute-start(bf16[2,2,64,1792]{3,2,1,0:T(8,128)(2,1)S(1)} %late.1), channel_id=1, source_target_pairs={{0,2},{2,0},{4,6},{6,4},{8,10},{10,8},{12,14},{14,12},{1,3},{3,1},... | collective-permute-start | bytes 2752520 | tf_op jit(solution)/shard_map/ppermute | solution.py:782
  (3 other events, 6.7 us)
